TPU v7x, 512 devices: a whole 4x8x8 slice. The times are simulated.
512 devices in a mesh: chips: 32 (over z, y_lo, core), samples: 16 (over y_hi, x).
Axes of the slice: x: 4, y: 8 (y_hi: 4, y_lo: 2; y = y_hi * 2 + y_lo), z: 8, core: 2. Of those that a mesh axis runs over, the one named last changes fastest.
Arguments:
- telemetry: bfloat16 [73728, 16384], P('chips', 'samples'), may hold values from 0 to 100, as said below
- chip_factors: float32 [64, 73728], P(None, ('chips', 'samples')), may hold values from 0.03 to 0.3
- sample_factors: float32 [64, 16384], P(None, ('samples', 'chips')), may hold values from 0.03 to 0.3
Outputs:
- chip_updated: float32 [64, 73728], P(None, ('chips', 'samples'))
- sample_updated: float32 [64, 16384], P(None, ('samples', 'chips'))
- relative_error: float32 [], replicated
Inputs may be any that keep to these rules, and one draw needn't show every extreme that they name: `telemetry`: nonnegative readings.
All inputs are finite; a program needn't handle non-finite values.
Results may differ from a plain program's by a relative error of at most 0.00035.
Values may be sent and summed in bfloat16 or wider, within the bound.
No kernel may reach another device: no remote copies, remote signals or barrier semaphores. Data moves between devices by JAX's collectives and lax.ppermute only.
A program may use at most 64 MiB of HBM per device.

v0:
```python
import jax
import jax.numpy as jnp
from jax import lax
from jax.sharding import PartitionSpec as P

ITERS = 2


epsilon = 1e-09


def body(telemetry, chip_factors, sample_factors):
    highest = lax.Precision.HIGHEST
    chips_now = chip_factors
    samples_now = sample_factors
    for sweep in range(ITERS):
        gram_chip = lax.psum(
            jnp.dot(chips_now, chips_now.T, precision=highest), ("chips", "samples")
        )
        partial_h = jnp.dot(
            lax.all_gather(chips_now.astype(jnp.bfloat16), "samples", axis=1, tiled=True),
            telemetry,
            preferred_element_type=jnp.float32,
        )
        numer_h = lax.psum_scatter(partial_h, "chips", scatter_dimension=1, tiled=True)
        samples_now = (
            samples_now * numer_h / (jnp.dot(gram_chip, samples_now, precision=highest) + epsilon)
        )
        gram_sample = lax.psum(
            jnp.dot(samples_now, samples_now.T, precision=highest), ("chips", "samples")
        )
        partial_w = lax.dot_general(
            lax.all_gather(samples_now.astype(jnp.bfloat16), "chips", axis=1, tiled=True),
            telemetry,
            (((1,), (1,)), ((), ())),
            preferred_element_type=jnp.float32,
        )
        numer_w = lax.psum_scatter(partial_w, "samples", scatter_dimension=1, tiled=True)
        chips_now = (
            chips_now * numer_w / (jnp.dot(gram_sample, chips_now, precision=highest) + epsilon)
        )
    sample_whole = lax.all_gather(samples_now.astype(jnp.bfloat16), "chips", axis=1, tiled=True)
    rebuilt = lax.dot_general(
        lax.all_gather(chips_now.astype(jnp.bfloat16), "samples", axis=1, tiled=True),
        sample_whole,
        (((0,), (0,)), ((), ())),
        preferred_element_type=jnp.float32,
    )
    difference = telemetry.astype(jnp.float32) - rebuilt
    per_row = jnp.sum(difference * difference, axis=1)
    own_error = jnp.sum(per_row)
    readings = telemetry.astype(jnp.float32)
    own_energy = jnp.sum(readings * readings)
    fit_error, energy = lax.psum((own_error, own_energy), ("chips", "samples"))
    relative_error = jnp.sqrt(fit_error / energy)
    return (chips_now, samples_now, relative_error)


def solution(mesh):
    return jax.shard_map(
        body,
        mesh=mesh,
        in_specs=(
            P("chips", "samples"),
            P(None, ("chips", "samples")),
            P(None, ("samples", "chips")),
        ),
        out_specs=(P(None, ("chips", "samples")), P(None, ("samples", "chips")), P()),
        check_vma=False,
    )
```

profile of v0, /device:TPU:1, one launch (start us, length us, event | category | flops | bytes accessed | tf_op | source)
XLA Modules:
  0.0 776.3 jit_solution(1189298416496678070)
XLA Ops:
  7.2 0.0 copy-start
  7.2 0.0 copy-start.3
  7.2 0.0 reduce-scatter.9.cloned.1.call-start
  7.2 0.9 convert_bitcast_fusion.2
  8.1 41.3 %all-gather = bf16[16,144,64]{1,2,0:T(8,128)(2,1)S(1)} all-gather(bf16[1,144,64]{1,2,0:T(8,128)(2,1)S(1)} %convert_bitcast_fusion.2), channel_id=1, replica_groups=mesh['chips'=32,'samples'=16] {'samples'}, dimensions={0}, use_global_device_ids=true | all-gather | bytes 313344 | tf_op jit(solution)/shard_map/all_gather | solution.py:21
  49.4 0.3 copy.9
  49.6 0.6 reshape.7
  50.3 5.1 fusion.9
  55.3 0.0 reduce-scatter.9.cloned.1.call-update
  55.4 0.0 reduce-scatter.13.cloned.1.call-start
  55.4 0.2 fusion.10
  55.6 108.9 %psum.42 = f32[64,64]{1,0:T(8,128)S(1)} all-reduce(f32[64,64]{1,0:T(8,128)S(1)} %fusion.10), channel_id=1, replica_groups=mesh['chips'=32,'samples'=16] {'chips','samples'}, use_global_device_ids=true, to_apply=%region_1.0 | all-reduce | flops 4096 | bytes 32768 | tf_op jit(solution)/shard_map/psum | solution.py:17
  164.6 12.5 %reduce-scatter.9.cloned.1.call-done = f32[64,32]{0,1:T(8,128)} async-done(((f32[64,1024]{0,1:T(8,128)}), f32[64,32]{0,1:T(8,128)}) %reduce-scatter.9.cloned.1.call-update) | async-done | bytes 8208 | tf_op jit(solution)/shard_map/reduce_scatter | solution.py:25
  177.0 0.0 copy-done.3
  177.0 0.9 fusion.7
  177.9 35.7 %all_gather.17 = bf16[64,1024]{0,1:T(8,128)(2,1)S(1)} all-gather(bf16[64,32]{0,1:T(8,128)(2,1)S(1)} %get-tuple-element.5), channel_id=1, replica_groups=mesh['chips'=32,'samples'=16] {'chips'}, dimensions={1}, use_global_device_ids=true | all-gather | bytes 135168 | tf_op jit(solution)/shard_map/all_gather | solution.py:33
  213.6 4.7 convolution_bitcast_fusion.1
  218.3 0.0 reduce-scatter.13.cloned.1.call-update
  218.4 0.0 reduce-scatter.11.cloned.1.call-start
  218.4 0.2 fusion.11
  218.7 98.1 %psum.43 = f32[64,64]{1,0:T(8,128)S(1)} all-reduce(f32[64,64]{1,0:T(8,128)S(1)} %fusion.11), channel_id=1, replica_groups=mesh['chips'=32,'samples'=16] {'chips','samples'}, use_global_device_ids=true, to_apply=%region_3.0 | all-reduce | flops 4096 | bytes 32768 | tf_op jit(solution)/shard_map/psum | solution.py:29
  316.8 1.0 copy.13
  317.7 0.2 fusion.4
  318.0 36.8 %all-gather.1 = bf16[16,144,64]{1,2,0:T(8,128)(2,1)S(1)} all-gather(bf16[1,144,64]{1,2,0:T(8,128)(2,1)S(1)} %convert_bitcast_fusion.1), channel_id=1, replica_groups=mesh['chips'=32,'samples'=16] {'samples'}, dimensions={0}, use_global_device_ids=true | all-gather | bytes 313344 | tf_op jit(solution)/shard_map/all_gather | solution.py:21
  354.8 0.3 copy.10
  355.1 0.6 reshape.9
  355.7 5.1 fusion.12
  360.7 0.0 reduce-scatter.11.cloned.1.call-update
  360.8 0.0 reduce-scatter.15.cloned.1.call-start
  360.8 0.2 fusion.13
  361.0 100.7 %psum.44 = f32[64,64]{1,0:T(8,128)S(1)} all-reduce(f32[64,64]{1,0:T(8,128)S(1)} %fusion.13), channel_id=1, replica_groups=mesh['chips'=32,'samples'=16] {'chips','samples'}, use_global_device_ids=true, to_apply=%region_5.0 | all-reduce | flops 4096 | bytes 32768 | tf_op jit(solution)/shard_map/psum | solution.py:17
  461.7 15.3 %reduce-scatter.11.cloned.1.call-done = f32[64,32]{0,1:T(8,128)} async-done(((f32[64,1024]{0,1:T(8,128)}), f32[64,32]{0,1:T(8,128)}) %reduce-scatter.11.cloned.1.call-update) | async-done | bytes 8208 | tf_op jit(solution)/shard_map/reduce_scatter | solution.py:25
  477.0 0.9 fusion.8
  477.9 0.0 copy-start.1
  477.9 35.9 %all_gather.19 = bf16[64,1024]{0,1:T(8,128)(2,1)S(1)} all-gather(bf16[64,32]{0,1:T(8,128)(2,1)S(1)} %get-tuple-element.7), channel_id=1, replica_groups=mesh['chips'=32,'samples'=16] {'chips'}, dimensions={1}, use_global_device_ids=true | all-gather | bytes 135168 | tf_op jit(solution)/shard_map/all_gather | solution.py:33
  513.8 4.7 convolution_bitcast_fusion
  518.5 0.0 reduce-scatter.15.cloned.1.call-update
  518.5 5.4 fusion.2
  524.0 0.2 fusion.14
  524.2 98.0 %psum.45 = f32[64,64]{1,0:T(8,128)S(1)} all-reduce(f32[64,64]{1,0:T(8,128)S(1)} %fusion.14), channel_id=1, replica_groups=mesh['chips'=32,'samples'=16] {'chips','samples'}, use_global_device_ids=true, to_apply=%region_7.0 | all-reduce | flops 4096 | bytes 32768 | tf_op jit(solution)/shard_map/psum | solution.py:29
  622.2 1.0 copy.15
  623.2 0.2 fusion.3
  623.4 0.0 copy-start.2
  623.4 36.6 %all-gather.2 = bf16[16,144,64]{1,2,0:T(8,128)(2,1)S(1)} all-gather(bf16[1,144,64]{1,2,0:T(8,128)(2,1)S(1)} %convert_bitcast_fusion), channel_id=1, replica_groups=mesh['chips'=32,'samples'=16] {'samples'}, dimensions={0}, use_global_device_ids=true | all-gather | bytes 313344 | tf_op jit(solution)/shard_map/all_gather | solution.py:44
  660.0 0.3 copy.11
  660.3 0.6 reshape.11
  660.9 5.6 fusion.1
  666.5 100.7 %all-reduce = (f32[]{:T(128)}, f32[]{:T(128)}) all-reduce(f32[]{:T(128)} %fusion.1, f32[]{:T(128)} %fusion.2), channel_id=1, replica_groups=mesh['chips'=32,'samples'=16] {'chips','samples'}, use_global_device_ids=true, to_apply=%region_9.0 | all-reduce | flops 2 | bytes 16 | tf_op jit(solution)/shard_map/psum | solution.py:54
  (7 shorter events, 0.0 us)
Async XLA Ops:
  7.2 48.2 %copy-start = (f32[64,144]{1,0:T(8,128)S(1)}, f32[64,144]{1,0:T(8,128)}, u32[]{:S(2)}) copy-start(f32[64,144]{1,0:T(8,128)} %param.4) | copy-start | bytes 110596
  7.2 169.9 %copy-start.3 = (f32[64,32]{0,1:T(8,128)S(1)}, f32[64,32]{0,1:T(8,128)}, u32[]{:S(2)}) copy-start(f32[64,32]{0,1:T(8,128)} %param.5) | copy-start | bytes 24580
  7.2 169.9 %reduce-scatter.9.cloned.1.call-start = ((), (), s32[]{:S(2)}) async-start(), calls=%async_computation.4 | async-start | bytes 540672 | tf_op jit(solution)/shard_map/reduce_scatter | solution.py:25
  55.4 261.4 %reduce-scatter.13.cloned.1.call-start = ((), (), s32[]{:S(2)}) async-start(), calls=%async_computation.6 | async-start | bytes 1253376
  218.4 258.6 %reduce-scatter.11.cloned.1.call-start = ((), (), s32[]{:S(2)}) async-start(), calls=%async_computation.5 | async-start | bytes 540672 | tf_op jit(solution)/shard_map/reduce_scatter | solution.py:25
  360.8 261.4 %reduce-scatter.15.cloned.1.call-start = ((), (), s32[]{:S(2)}) async-start(), calls=%async_computation.7 | async-start | bytes 1253376
  477.9 46.1 %copy-start.1 = (f32[64,32]{0,1:T(8,128)}, f32[64,32]{0,1:T(8,128)S(1)}, u32[]{:S(2)}) copy-start(f32[64,32]{0,1:T(8,128)S(1)} %get-tuple-element.8) | copy-start | bytes 24580
  623.4 43.1 %copy-start.2 = (f32[64,144]{1,0:T(8,128)}, f32[64,144]{1,0:T(8,128)S(1)}, u32[]{:S(2)}) copy-start(f32[64,144]{1,0:T(8,128)S(1)} %fusion.3) | copy-start | bytes 110596
Sparse Core Ops, SparseCore 0:
  55.5 121.5 reduce-scatter.8
  218.5 87.4 reduce-scatter.12
  360.9 116.0 reduce-scatter.10
  518.7 86.9 reduce-scatter.14
where the time goes:
time: 777 us; the launch traced here: 776 us
  blocking collectives  693 us (89%)
  matrix products  28.3 us (4%)
  waiting for transfers between devices  27.8 us (4%)
  between operations  16.5 us (2%)
    psum x2, blocking collectives, body(): lax.psum(jnp.dot(chips_now, chips_now.T, precision=highest), ('chips', 's...  210 us
    psum x2, blocking collectives, body(): lax.psum(jnp.dot(samples_now, samples_now.T, precision=highest), ('chips'...  196 us
    all_gather x3, blocking collectives, body(): lax.all_gather(chips_now.astype(jnp.bfloat16), 'samples', axis=1, tiled=T...  115 us
    psum x1, blocking collectives, body(): fit_error, energy = lax.psum((own_error, own_energy), ('chips', 'samples'))  101 us
    all_gather x2, blocking collectives, body(): lax.all_gather(samples_now.astype(jnp.bfloat16), 'chips', axis=1, tiled=T...  71.5 us
    reduce_scatter x2, waiting for transfers between devices, body(): lax.psum_scatter(partial_h, 'chips', scatter_dimension=1, tiled=True)  27.8 us
  transfers between devices with their start and end apart: 4, of which 2 were waited for; matrix products, arithmetic and copies ran while one was open for 1% of the time, Pallas kernels for 0%

commit v1 on v0

v1 whole, which is shorter than its diff:
```python
import jax
import jax.numpy as jnp
from jax import lax
from jax.experimental import pallas as pl
from jax.experimental.pallas import tpu as pltpu
from jax.sharding import PartitionSpec as P

ITERS = 2

epsilon = 1e-09

F32 = jnp.float32
BF16 = jnp.bfloat16
HIGHEST = lax.Precision.HIGHEST

K = 64
CHIPS = 32
SAMPLES = 16
ROWS = 2304
COLS = 1024
W_OWN = ROWS // SAMPLES
H_OWN = COLS // CHIPS
GRAM = 32
W_HALF = 80
W_MSG = W_HALF + GRAM
H_RED = H_OWN + GRAM
W_RED = W_OWN + GRAM


def split(x):
    high = x.astype(BF16).astype(F32)
    return jnp.concatenate([high, x - high], axis=1).astype(BF16)


def join(x):
    return x[:, :K] + x[:, K:]


def squares():
    row = lax.broadcasted_iota(jnp.int32, (32, 32), 0)
    col = lax.broadcasted_iota(jnp.int32, (32, 32), 1)
    return row, col


def pack_parts(upper, block, lower_diag, row, col):
    high = upper.astype(BF16).astype(F32)
    low = upper - high
    block_high = block.astype(BF16).astype(F32)
    own = row == col
    return jnp.concatenate(
        [jnp.where(own, upper, high), block_high, jnp.where(own, lower_diag, low), block - block_high],
        axis=1,
    ).astype(BF16)


def pack_gram(gram):
    row, col = squares()
    first, block, last = gram[:32, :32], gram[:32, 32:], gram[32:, 32:]
    return pack_parts(jnp.where(row <= col, first, last), block, last, row, col)


def repack_gram(total):
    row, col = squares()
    own = row == col
    first, third = total[:, :32], total[:, 64:96]
    upper = jnp.where(own, first, first + third)
    return pack_parts(upper, total[:, 32:64] + total[:, 96:], third, row, col)


def unpack_gram(total):
    row, col = squares()
    first, third = total[:, :32], total[:, 64:96]
    mixed = first + third
    block = total[:, 32:64] + total[:, 96:]
    eye = (row == col).astype(F32)
    turned = lax.dot_general(
        eye,
        jnp.concatenate([mixed, block], axis=0),
        (((1,), (1,)), ((), ())),
        precision=HIGHEST,
        preferred_element_type=F32,
    )
    mixed_t, block_t = turned[:, :32], turned[:, 32:]
    one = jnp.where(row < col, mixed, jnp.where(row > col, mixed_t, first))
    two = jnp.where(row > col, mixed, jnp.where(row < col, mixed_t, third))
    return jnp.concatenate(
        [jnp.concatenate([one, block], axis=1), jnp.concatenate([block_t, two], axis=1)], axis=0
    )


def gram_of(halves):
    four = lax.dot_general(
        halves, halves, (((0,), (0,)), ((), ())), preferred_element_type=F32
    )
    two = four[:K] + four[K:]
    return two[:, :K] + two[:, K:]


def fill_w(w, out):
    tail = jnp.concatenate([w[W_HALF:], jnp.zeros((2 * W_HALF - W_OWN, K), F32)], axis=0)
    rows = jnp.concatenate([w[:W_HALF], tail], axis=1).astype(BF16)
    gram = pack_gram(gram_of(split(w)))
    for i in range(SAMPLES):
        out[i, :W_HALF, :] = rows
        out[i, W_HALF:, :] = gram


def own_rows(ref, i):
    both = ref[i, :W_HALF, :].astype(F32)
    return jnp.concatenate([both[:, :K], both[: W_OWN - W_HALF, K:]], axis=0)


def start_kernel(w, out):
    fill_w(w[...], out)


def h_numer_kernel(got, tel, out, w_all, w_turned):
    total = jnp.zeros((GRAM, 128), F32)
    for i in range(SAMPLES):
        w_all[i * W_OWN : (i + 1) * W_OWN, :] = own_rows(got, i)
        total += got[i, W_HALF:, :].astype(F32)
    gram = repack_gram(total)
    for j in range(ROWS // 128):
        w_turned[:, j * 128 : (j + 1) * 128] = w_all[j * 128 : (j + 1) * 128, :].T.astype(BF16)
    width = 256
    per = width // H_OWN

    def step(n, carry):
        cols = pl.ds(pl.multiple_of(n * width, width), width)
        part = jnp.dot(w_turned[...], tel[:, cols], preferred_element_type=F32).T
        for q in range(per):
            out[n * per + q, :H_OWN, :] = split(part[q * H_OWN : (q + 1) * H_OWN])
            out[n * per + q, H_OWN:, :] = gram
        return carry

    lax.fori_loop(0, COLS // width, step, 0)


def h_update_kernel(got, h, h_out, out):
    total = jnp.zeros((H_RED, 128), F32)
    for i in range(CHIPS):
        total += got[i].astype(F32)
    gram = unpack_gram(total[H_OWN:])
    old = h[...]
    below = jnp.dot(old, gram, precision=HIGHEST, preferred_element_type=F32) + epsilon
    new = old * join(total[:H_OWN]) / below
    h_out[...] = new
    halves = split(new)
    for i in range(CHIPS):
        out[i] = halves


def w_numer_kernel(got, tel, out):
    halves = got[...].reshape(COLS, 128)
    gram = pack_gram(gram_of(halves))
    high = halves[:, :K]
    per = 4
    block = per * W_OWN

    def step(b, carry):
        rows = pl.ds(pl.multiple_of(b * block, block), block)
        part = jnp.dot(tel[rows, :], high, preferred_element_type=F32)
        for q in range(per):
            out[b * per + q, :W_OWN, :] = split(part[q * W_OWN : (q + 1) * W_OWN])
            out[b * per + q, W_OWN:, :] = gram
        return carry

    lax.fori_loop(0, ROWS // block, step, 0)


def w_update_kernel(got, w, w_out, out):
    total = jnp.zeros((W_RED, 128), F32)
    for i in range(SAMPLES):
        total += got[i].astype(F32)
    gram = unpack_gram(total[W_OWN:])
    old = w[...]
    below = jnp.dot(old, gram, precision=HIGHEST, preferred_element_type=F32) + epsilon
    new = old * join(total[:W_OWN]) / below
    w_out[...] = new
    fill_w(new, out)


def error_kernel(got_w, got_h, tel, out):
    high = got_h[...].reshape(COLS, 128)[:, :K]

    def step(i, carry):
        error, energy = carry
        rows = pl.ds(pl.multiple_of(i * W_OWN, W_OWN), W_OWN)
        rebuilt = lax.dot_general(
            own_rows(got_w, i).astype(BF16),
            high,
            (((1,), (1,)), ((), ())),
            preferred_element_type=F32,
        )
        values = tel[rows, :].astype(F32)
        difference = values - rebuilt
        error += jnp.sum((difference * difference).reshape(W_OWN // 8, 8, COLS), axis=0)
        energy += jnp.sum((values * values).reshape(W_OWN // 8, 8, COLS), axis=0)
        return error, energy

    zero = jnp.zeros((8, COLS), F32)
    error, energy = lax.fori_loop(0, SAMPLES, step, (zero, zero))
    lane = lax.broadcasted_iota(jnp.int32, (8, 128), 1)
    pair = jnp.where(lane < K, jnp.sum(error), jnp.sum(energy))
    for i in range(SAMPLES):
        out[i] = pair


VMEM = pl.BlockSpec(memory_space=pltpu.VMEM)


def call(kernel, inputs, outs, scratch=(), cost=(0, 0)):
    return pl.pallas_call(
        kernel,
        out_shape=[jax.ShapeDtypeStruct(shape, dtype) for shape, dtype in outs],
        in_specs=[VMEM] * len(inputs),
        out_specs=[VMEM] * len(outs),
        scratch_shapes=list(scratch),
        compiler_params=pltpu.CompilerParams(vmem_limit_bytes=32 * 1024 * 1024),
        cost_estimate=pl.CostEstimate(flops=cost[0], bytes_accessed=cost[1], transcendentals=0),
    )(*inputs)


def exchange(x, axis):
    return lax.all_to_all(x, axis, 0, 0, tiled=True)


def body(telemetry, chip_factors, sample_factors):
    w, h = chip_factors.T, sample_factors.T
    product = (2 * K * ROWS * COLS, ROWS * COLS * 2)
    (sent,) = call(start_kernel, (w,), [((SAMPLES, W_MSG, 128), BF16)])
    got_w = exchange(sent, "samples")
    for sweep in range(ITERS):
        (sent,) = call(
            h_numer_kernel,
            (got_w, telemetry),
            [((CHIPS, H_RED, 128), BF16)],
            (pltpu.VMEM((ROWS, K), F32), pltpu.VMEM((K, ROWS), BF16)),
            product,
        )
        got = exchange(sent, "chips")
        h, sent = call(
            h_update_kernel, (got, h), [((H_OWN, K), F32), ((CHIPS, H_OWN, 128), BF16)]
        )
        got_h = exchange(sent, "chips")
        (sent,) = call(
            w_numer_kernel, (got_h, telemetry), [((SAMPLES, W_RED, 128), BF16)], (), product
        )
        got = exchange(sent, "samples")
        w, sent = call(
            w_update_kernel, (got, w), [((W_OWN, K), F32), ((SAMPLES, W_MSG, 128), BF16)]
        )
        got_w = exchange(sent, "samples")
    (pair,) = call(
        error_kernel, (got_w, got_h, telemetry), [((SAMPLES, 8, 128), F32)], (), product
    )
    pair = jnp.sum(exchange(pair, "samples"), axis=0)
    pair = exchange(jnp.broadcast_to(pair[None], (CHIPS, 8, 128)), "chips")
    pair = jnp.sum(pair, axis=0)
    return w.T, h.T, jnp.sqrt(pair[0, 0] / pair[0, K])


def solution(mesh):
    return jax.shard_map(
        body,
        mesh=mesh,
        in_specs=(
            P("chips", "samples"),
            P(None, ("chips", "samples")),
            P(None, ("samples", "chips")),
        ),
        out_specs=(P(None, ("chips", "samples")), P(None, ("samples", "chips")), P()),
        check_vma=False,
    )
```

time: 777 us -> 253 us (0.33)
  blocking collectives: 693 us -> 201 us
  matrix products: 28.3 us -> 0 us
  waiting for transfers between devices: 27.8 us -> 7.88 us
  Pallas kernels: 0 us -> 19.5 us
  starting transfers between devices: 0.16 us -> 15.7 us
  between operations: 16.5 us -> 3.15 us
    psum x5 -> x0, blocking collectives: 506 us -> none  [the longest x2 210 us: body(): lax.psum(jnp.dot(chips_now, chips_now.T, precision=highest), ('chips', 's...]
    all_to_all x0 -> x10, blocking collectives: none -> 201 us  [exchange(): return lax.all_to_all(x, axis, 0, 0, tiled=True)]
    all_gather x5 -> x0, blocking collectives: 186 us -> none  [the longest x3 115 us: body(): lax.all_gather(chips_now.astype(jnp.bfloat16), 'samples', axis=1, tiled=T...]
    reduce_scatter x2 -> x0, waiting for transfers between devices: 27.8 us -> none  [body(): lax.psum_scatter(partial_h, 'chips', scatter_dimension=1, tiled=True)]
    pallas_call x0 -> x10, Pallas kernels: none -> 19.5 us  [call(): pl.pallas_call(kernel, out_shape=[jax.ShapeDtypeStruct(shape, dtype) for...]
    dot_general x11 -> x0, matrix products: 18.8 us -> none  [the longest x2 10.1 us: body(): jnp.dot(lax.all_gather(chips_now.astype(jnp.bfloat16), 'samples', axis=1,...]
    all_to_all x0 -> x1, starting transfers between devices: none -> 15.7 us  [exchange(): return lax.all_to_all(x, axis, 0, 0, tiled=True)]
    unnamed x2 -> x0, matrix products: 9.47 us -> none
  transfers between devices with their start and end apart: 4 -> 1, of which waited for: 2 -> 1; matrix products, arithmetic and copies ran while one was open for 1% -> 0% of each run, Pallas kernels for 0% -> 0%
where the time goes in v1:
time: 253 us
  blocking collectives  201 us (79%)
  Pallas kernels  19.5 us (8%)
  starting transfers between devices  15.7 us (6%)
  waiting for transfers between devices  7.88 us (3%)
  local copies, waits for them, and re-layouts  5.31 us (2%)
  between operations  3.15 us (1%)
    all_to_all x10, blocking collectives, exchange(): return lax.all_to_all(x, axis, 0, 0, tiled=True)  201 us
    pallas_call x10, Pallas kernels, call(): pl.pallas_call(kernel, out_shape=[jax.ShapeDtypeStruct(shape, dtype) for...  19.5 us
    all_to_all x1, starting transfers between devices, exchange(): return lax.all_to_all(x, axis, 0, 0, tiled=True)  15.7 us
    all_to_all x1, waiting for transfers between devices, exchange(): return lax.all_to_all(x, axis, 0, 0, tiled=True)  7.88 us
  transfers between devices with their start and end apart: 1, of which 1 were waited for; matrix products, arithmetic and copies ran while one was open for 0% of the time, Pallas kernels for 0%

profile of v1, /device:TPU:1, one launch (start us, length us, event | category | flops | bytes accessed | tf_op | source)
XLA Modules:
  0.0 252.7 jit_solution(11165158847229350239)
XLA Ops:
  0.6 0.0 slice-start
  0.6 0.0 copy-start.1
  0.7 1.0 copy.8
  1.7 0.5 shard_map.58
  2.2 25.3 %all_to_all.55.got = bf16[16,112,128]{2,1,0:T(8,128)(2,1)S(1)} all-to-all(bf16[16,112,128]{2,1,0:T(8,128)(2,1)S(1)} %shard_map.58), channel_id=1, replica_groups=mesh['chips'=32,'samples'=16] {'samples'}, dimensions={0} | all-to-all | bytes 917504 | tf_op jit(solution)/shard_map/all_to_all | solution.py:225
  27.5 0.0 copy-start
  27.5 2.3 copy-done
  29.8 0.0 slice-start.1
  29.8 2.5 shard_map.59
  32.3 29.3 %all_to_all.56.got = bf16[32,64,128]{2,1,0:T(8,128)(2,1)S(1)} all-to-all(bf16[32,64,128]{2,1,0:T(8,128)(2,1)S(1)} %shard_map.59), channel_id=1, replica_groups=mesh['chips'=32,'samples'=16] {'chips'}, dimensions={0} | all-to-all | bytes 1048576 | tf_op jit(solution)/shard_map/all_to_all | solution.py:225
  61.6 0.0 copy-done.1
  61.6 0.7 shard_map.60
  62.3 15.4 %all_to_all.57.got = bf16[32,32,128]{2,1,0:T(8,128)(2,1)S(1)} all-to-all(bf16[32,32,128]{2,1,0:T(8,128)(2,1)S(1)} %get-tuple-element.11), channel_id=1, replica_groups=mesh['chips'=32,'samples'=16] {'chips'}, dimensions={0} | all-to-all | bytes 524288 | tf_op jit(solution)/shard_map/all_to_all | solution.py:225
  77.8 0.0 slice-done
  77.8 0.0 slice-done.1
  77.8 2.7 %shard_map.61 = bf16[16,176,128]{2,1,0:T(8,128)(2,1)S(1)} custom-call(bf16[32,32,128]{2,1,0:T(8,128)(2,1)S(1)} %all_to_all.57.got, bf16[2304,1024]{1,0:T(8,128)(2,1)S(1)} %bitcast.6), custom_call_target="tpu_custom_call" | custom-call | flops 301989888 | bytes 4718592 | tf_op jit(solution)/shard_map/pallas_call | solution.py:213
  80.5 20.9 %all_to_all.58.got = bf16[16,176,128]{2,1,0:T(8,128)(2,1)S(1)} all-to-all(bf16[16,176,128]{2,1,0:T(8,128)(2,1)S(1)} %shard_map.61), channel_id=1, replica_groups=mesh['chips'=32,'samples'=16] {'samples'}, dimensions={0} | all-to-all | bytes 1441792 | tf_op jit(solution)/shard_map/all_to_all | solution.py:225
  101.3 1.2 shard_map.62
  102.5 15.7 %all_to_all.59.got = bf16[16,112,128]{2,1,0:T(8,128)(2,1)S(1)} all-to-all(bf16[16,112,128]{2,1,0:T(8,128)(2,1)S(1)} %get-tuple-element.12), channel_id=1, replica_groups=mesh['chips'=32,'samples'=16] {'samples'}, dimensions={0} | all-to-all | bytes 917504 | tf_op jit(solution)/shard_map/all_to_all | solution.py:225
  118.2 2.5 shard_map.63
  120.7 30.0 %all_to_all.60.got = bf16[32,64,128]{2,1,0:T(8,128)(2,1)S(1)} all-to-all(bf16[32,64,128]{2,1,0:T(8,128)(2,1)S(1)} %shard_map.63), channel_id=1, replica_groups=mesh['chips'=32,'samples'=16] {'chips'}, dimensions={0} | all-to-all | bytes 1048576 | tf_op jit(solution)/shard_map/all_to_all | solution.py:225
  150.7 1.2 shard_map.64
  151.9 15.4 %all_to_all.61.got.got_h = bf16[32,32,128]{2,1,0:T(8,128)(2,1)S(1)} all-to-all(bf16[32,32,128]{2,1,0:T(8,128)(2,1)S(1)} %get-tuple-element.14), channel_id=1, replica_groups=mesh['chips'=32,'samples'=16] {'chips'}, dimensions={0} | all-to-all | bytes 524288 | tf_op jit(solution)/shard_map/all_to_all | solution.py:225
  167.4 2.7 %shard_map.65 = bf16[16,176,128]{2,1,0:T(8,128)(2,1)S(1)} custom-call(bf16[32,32,128]{2,1,0:T(8,128)(2,1)S(1)} %all_to_all.61.got.got_h, bf16[2304,1024]{1,0:T(8,128)(2,1)S(1)} %bitcast.6), custom_call_target="tpu_custom_call" | custom-call | flops 301989888 | bytes 4718592 | tf_op jit(solution)/shard_map/pallas_call | solution.py:213
  170.0 20.9 %all_to_all.62.got = bf16[16,176,128]{2,1,0:T(8,128)(2,1)S(1)} all-to-all(bf16[16,176,128]{2,1,0:T(8,128)(2,1)S(1)} %shard_map.65), channel_id=1, replica_groups=mesh['chips'=32,'samples'=16] {'samples'}, dimensions={0} | all-to-all | bytes 1441792 | tf_op jit(solution)/shard_map/all_to_all | solution.py:225
  190.9 1.2 shard_map.66
  192.1 15.7 %all_to_all.63.got_w = bf16[16,112,128]{2,1,0:T(8,128)(2,1)S(1)} all-to-all(bf16[16,112,128]{2,1,0:T(8,128)(2,1)S(1)} %get-tuple-element.18), channel_id=1, replica_groups=mesh['chips'=32,'samples'=16] {'samples'}, dimensions={0} | all-to-all | bytes 917504 | tf_op jit(solution)/shard_map/all_to_all | solution.py:225
  207.8 4.4 %shard_map.67 = f32[16,8,128]{2,1,0:T(8,128)S(1)} custom-call(bf16[16,112,128]{2,1,0:T(8,128)(2,1)S(1)} %all_to_all.63.got_w, bf16[32,32,128]{2,1,0:T(8,128)(2,1)S(1)} %all_to_all.61.got.got_h, bf16[2304,1024]{1,0:T(8,128)(2,1)S(1)} %bitcast.6), custom_call_target="tpu_custom_call" | custom-call | flops 301989888 | bytes 4718592 | tf_op jit(solution)/shard_map/pallas_call | solution.py:213
  212.2 12.5 %all_to_all.64 = f32[16,8,128]{2,1,0:T(8,128)S(1)} all-to-all(f32[16,8,128]{2,1,0:T(8,128)S(1)} %shard_map.67), channel_id=1, replica_groups=mesh['chips'=32,'samples'=16] {'samples'}, dimensions={0} | all-to-all | bytes 131072 | tf_op jit(solution)/shard_map/all_to_all | solution.py:225
  224.7 0.7 broadcast_in_dim.2
  225.4 15.7 %all-to-all-start.10 = ((f32[32,8,128]{2,1,0:T(8,128)}), f32[32,8,128]{2,1,0:T(8,128)S(1)}, u32[]{:S(2)}, u32[]{:S(2)}) async-start(f32[32,8,128]{2,1,0:T(8,128)} %broadcast_in_dim.2), calls=%async_computation.10 | async-start | bytes 262144 | tf_op jit(solution)/shard_map/all_to_all | solution.py:225
  241.1 0.7 copy.9
  241.8 7.9 %all-to-all-done.10 = f32[32,8,128]{2,1,0:T(8,128)S(1)} async-done(((f32[32,8,128]{2,1,0:T(8,128)}), f32[32,8,128]{2,1,0:T(8,128)S(1)}, u32[]{:S(2)}, u32[]{:S(2)}) %all-to-all-start.10) | async-done | bytes 131104 | tf_op jit(solution)/shard_map/all_to_all | solution.py:225
  249.7 0.6 fusion
  (3 shorter events, 0.1 us)
Async XLA Ops:
  0.6 77.2 %slice-start = ((s8[4718592]{0:T(1024)(128)(4,1)}), s8[524288]{0:T(1024)(128)(4,1)S(1)}, s32[]{:S(2)}) async-start(s8[4718592]{0:T(1024)(128)(4,1)} %bitcast.5), calls=%async_computation.11 | async-start | bytes 1048576
  0.6 61.0 %copy-start.1 = (f32[64,32]{0,1:T(8,128)S(1)}, f32[64,32]{0,1:T(8,128)}, u32[]{:S(2)}) copy-start(f32[64,32]{0,1:T(8,128)} %param.5) | copy-start | bytes 24580
  27.5 2.3 copy-start
  29.8 47.9 %slice-start.1 = ((s8[4718592]{0:T(1024)(128)(4,1)}), s8[4194304]{0:T(1024)(128)(4,1)S(1)}, s32[]{:S(2)}) async-start(s8[4718592]{0:T(1024)(128)(4,1)} %bitcast.5), calls=%async_computation.12 | async-start | bytes 8388608
  225.4 24.3 %all-to-all-start.10 = ((f32[32,8,128]{2,1,0:T(8,128)}), f32[32,8,128]{2,1,0:T(8,128)S(1)}, u32[]{:S(2)}, u32[]{:S(2)}) async-start(f32[32,8,128]{2,1,0:T(8,128)} %broadcast_in_dim.2), calls=%async_computation.10 | async-start | bytes 262144 | tf_op jit(solution)/shard_map/all_to_all | solution.py:225

commit v2 on v1

--- a/solution.py
+++ b/solution.py
@@ -3,6 +3,7 @@
 from jax import lax
 from jax.experimental import pallas as pl
 from jax.experimental.pallas import tpu as pltpu
+from jax.sharding import Mesh
 from jax.sharding import PartitionSpec as P
 
 ITERS = 2
@@ -15,11 +16,13 @@
 
 K = 64
 CHIPS = 32
+PAIRS = CHIPS // 2
 SAMPLES = 16
 ROWS = 2304
 COLS = 1024
 W_OWN = ROWS // SAMPLES
 H_OWN = COLS // CHIPS
+H_WIDTH = 256
 GRAM = 32
 W_HALF = 80
 W_MSG = W_HALF + GRAM
@@ -99,10 +102,12 @@
 def fill_w(w, out):
     tail = jnp.concatenate([w[W_HALF:], jnp.zeros((2 * W_HALF - W_OWN, K), F32)], axis=0)
     rows = jnp.concatenate([w[:W_HALF], tail], axis=1).astype(BF16)
-    gram = pack_gram(gram_of(split(w)))
     for i in range(SAMPLES):
         out[i, :W_HALF, :] = rows
-        out[i, W_HALF:, :] = gram
+    if out.shape[1] > W_HALF:
+        gram = pack_gram(gram_of(split(w)))
+        for i in range(SAMPLES):
+            out[i, W_HALF:, :] = gram
 
 
 def own_rows(ref, i):
@@ -114,31 +119,41 @@
     fill_w(w[...], out)
 
 
-def h_numer_kernel(got, tel, out, w_all, w_turned):
-    total = jnp.zeros((GRAM, 128), F32)
-    for i in range(SAMPLES):
-        w_all[i * W_OWN : (i + 1) * W_OWN, :] = own_rows(got, i)
-        total += got[i, W_HALF:, :].astype(F32)
-    gram = repack_gram(total)
-    for j in range(ROWS // 128):
-        w_turned[:, j * 128 : (j + 1) * 128] = w_all[j * 128 : (j + 1) * 128, :].T.astype(BF16)
-    width = 256
-    per = width // H_OWN
-
-    def step(n, carry):
-        cols = pl.ds(pl.multiple_of(n * width, width), width)
-        part = jnp.dot(w_turned[...], tel[:, cols], preferred_element_type=F32).T
-        for q in range(per):
-            out[n * per + q, :H_OWN, :] = split(part[q * H_OWN : (q + 1) * H_OWN])
-            out[n * per + q, H_OWN:, :] = gram
-        return carry
-
-    lax.fori_loop(0, COLS // width, step, 0)
+def h_numer_kernel(core, got, tel, keep, give, w_turned, w_all, gram):
+    step = pl.program_id(0)
+
+    @pl.when(step == 0)
+    def _():
+        total = jnp.zeros((GRAM, 128), F32)
+        for i in range(SAMPLES):
+            w_all[i * W_OWN : (i + 1) * W_OWN, :] = own_rows(got, i)
+            total += got[i, W_HALF:, :].astype(F32)
+        gram[...] = repack_gram(total)
+        for j in range(ROWS // 128):
+            w_turned[:, j * 128 : (j + 1) * 128] = w_all[j * 128 : (j + 1) * 128, :].T.astype(BF16)
+
+    part = jnp.dot(w_turned[...], tel[...], preferred_element_type=F32).T
+    first = core[0] == 0
+    for q in range(H_WIDTH // (2 * H_OWN)):
+        even = part[2 * q * H_OWN : (2 * q + 1) * H_OWN]
+        odd = part[(2 * q + 1) * H_OWN : (2 * q + 2) * H_OWN]
+        keep[q, :H_OWN, :] = split(jnp.where(first, even, odd))
+        give[q, :H_OWN, :] = split(jnp.where(first, odd, even))
+        keep[q, H_OWN:, :] = gram[...]
+        give[q, H_OWN:, :] = gram[...]
+
+
+def pair_kernel(keep, got, out):
+    gram = repack_gram(keep[0, H_OWN:, :].astype(F32) + got[0, H_OWN:, :].astype(F32))
+    for i in range(PAIRS):
+        total = keep[i, :H_OWN, :].astype(F32) + got[i, :H_OWN, :].astype(F32)
+        out[i, :H_OWN, :] = split(join(total))
+        out[i, H_OWN:, :] = gram
 
 
 def h_update_kernel(got, h, h_out, out):
     total = jnp.zeros((H_RED, 128), F32)
-    for i in range(CHIPS):
+    for i in range(PAIRS):
         total += got[i].astype(F32)
     gram = unpack_gram(total[H_OWN:])
     old = h[...]
@@ -207,18 +222,45 @@
 
 
 VMEM = pl.BlockSpec(memory_space=pltpu.VMEM)
-
-
-def call(kernel, inputs, outs, scratch=(), cost=(0, 0)):
+LIMIT = pltpu.CompilerParams(vmem_limit_bytes=32 * 1024 * 1024)
+PRODUCT = pl.CostEstimate(
+    flops=2 * K * ROWS * COLS, bytes_accessed=2 * ROWS * COLS, transcendentals=0
+)
+
+
+def call(kernel, inputs, outs, cost=None):
     return pl.pallas_call(
         kernel,
         out_shape=[jax.ShapeDtypeStruct(shape, dtype) for shape, dtype in outs],
         in_specs=[VMEM] * len(inputs),
         out_specs=[VMEM] * len(outs),
-        scratch_shapes=list(scratch),
-        compiler_params=pltpu.CompilerParams(vmem_limit_bytes=32 * 1024 * 1024),
-        cost_estimate=pl.CostEstimate(flops=cost[0], bytes_accessed=cost[1], transcendentals=0),
+        compiler_params=LIMIT,
+        cost_estimate=cost,
     )(*inputs)
+
+
+def h_numer(core, got_w, telemetry):
+    per = H_WIDTH // (2 * H_OWN)
+    piece = pl.BlockSpec((per, H_RED, 128), lambda n: (n, 0, 0))
+    message = jax.ShapeDtypeStruct((PAIRS, H_RED, 128), BF16)
+    return pl.pallas_call(
+        h_numer_kernel,
+        grid=(COLS // H_WIDTH,),
+        out_shape=[message, message],
+        in_specs=[
+            pl.BlockSpec(memory_space=pltpu.SMEM),
+            pl.BlockSpec(got_w.shape, lambda n: (0, 0, 0)),
+            pl.BlockSpec((ROWS, H_WIDTH), lambda n: (0, n)),
+        ],
+        out_specs=[piece, piece],
+        scratch_shapes=[
+            pltpu.VMEM((K, ROWS), BF16),
+            pltpu.VMEM((ROWS, K), F32),
+            pltpu.VMEM((GRAM, 128), BF16),
+        ],
+        compiler_params=LIMIT,
+        cost_estimate=PRODUCT,
+    )(core, got_w, telemetry)
 
 
 def exchange(x, axis):
@@ -226,49 +268,48 @@
 
 
 def body(telemetry, chip_factors, sample_factors):
+    core = lax.axis_index("core").reshape(1)
     w, h = chip_factors.T, sample_factors.T
-    product = (2 * K * ROWS * COLS, ROWS * COLS * 2)
     (sent,) = call(start_kernel, (w,), [((SAMPLES, W_MSG, 128), BF16)])
     got_w = exchange(sent, "samples")
     for sweep in range(ITERS):
-        (sent,) = call(
-            h_numer_kernel,
-            (got_w, telemetry),
-            [((CHIPS, H_RED, 128), BF16)],
-            (pltpu.VMEM((ROWS, K), F32), pltpu.VMEM((K, ROWS), BF16)),
-            product,
-        )
-        got = exchange(sent, "chips")
+        keep, give = h_numer(core, got_w, telemetry)
+        taken = lax.ppermute(give, "core", [(0, 1), (1, 0)])
+        (sent,) = call(pair_kernel, (keep, taken), [((PAIRS, H_RED, 128), BF16)])
+        got = exchange(sent, "pairs")
         h, sent = call(
             h_update_kernel, (got, h), [((H_OWN, K), F32), ((CHIPS, H_OWN, 128), BF16)]
         )
-        got_h = exchange(sent, "chips")
+        got_h = exchange(sent, ("pairs", "core"))
         (sent,) = call(
-            w_numer_kernel, (got_h, telemetry), [((SAMPLES, W_RED, 128), BF16)], (), product
+            w_numer_kernel, (got_h, telemetry), [((SAMPLES, W_RED, 128), BF16)], PRODUCT
         )
         got = exchange(sent, "samples")
+        rows = W_MSG if sweep < ITERS - 1 else W_HALF
         w, sent = call(
-            w_update_kernel, (got, w), [((W_OWN, K), F32), ((SAMPLES, W_MSG, 128), BF16)]
+            w_update_kernel, (got, w), [((W_OWN, K), F32), ((SAMPLES, rows, 128), BF16)]
         )
         got_w = exchange(sent, "samples")
     (pair,) = call(
-        error_kernel, (got_w, got_h, telemetry), [((SAMPLES, 8, 128), F32)], (), product
+        error_kernel, (got_w, got_h, telemetry), [((SAMPLES, 8, 128), F32)], PRODUCT
     )
     pair = jnp.sum(exchange(pair, "samples"), axis=0)
-    pair = exchange(jnp.broadcast_to(pair[None], (CHIPS, 8, 128)), "chips")
+    pair = exchange(jnp.broadcast_to(pair[None], (CHIPS, 8, 128)), ("pairs", "core"))
     pair = jnp.sum(pair, axis=0)
     return w.T, h.T, jnp.sqrt(pair[0, 0] / pair[0, K])
 
 
 def solution(mesh):
+    split_mesh = Mesh(mesh.devices.reshape(PAIRS, 2, SAMPLES), ("pairs", "core", "samples"))
+    chips = ("pairs", "core")
     return jax.shard_map(
         body,
-        mesh=mesh,
+        mesh=split_mesh,
         in_specs=(
-            P("chips", "samples"),
-            P(None, ("chips", "samples")),
-            P(None, ("samples", "chips")),
+            P(chips, "samples"),
+            P(None, (*chips, "samples")),
+            P(None, ("samples", *chips)),
         ),
-        out_specs=(P(None, ("chips", "samples")), P(None, ("samples", "chips")), P()),
+        out_specs=(P(None, (*chips, "samples")), P(None, ("samples", *chips)), P()),
         check_vma=False,
     )

time: 253 us -> 248 us (0.980)
  blocking collectives: 201 us -> 155 us
  starting transfers between devices: 15.7 us -> 36.6 us
  waiting for transfers between devices: 7.88 us -> 25.5 us
    all_to_all x10 -> x9, blocking collectives: 201 us -> 155 us  [exchange(): return lax.all_to_all(x, axis, 0, 0, tiled=True)]
    all_to_all x1 -> x2, waiting for transfers between devices: 7.88 us -> 23.2 us  [exchange(): return lax.all_to_all(x, axis, 0, 0, tiled=True)]
    ppermute x0 -> x2, starting transfers between devices: none -> 12.1 us  [body(): taken = lax.ppermute(give, 'core', [(0, 1), (1, 0)])]
    all_to_all x1 -> x2, starting transfers between devices: 15.7 us -> 24.5 us  [exchange(): return lax.all_to_all(x, axis, 0, 0, tiled=True)]
    pallas_call x0 -> x2, Pallas kernels: none -> 6.23 us  [h_numer(): pl.pallas_call(h_numer_kernel, grid=(COLS // H_WIDTH,), out_shape=[messag...]
    pallas_call x10, Pallas kernels: 19.5 us -> 15.4 us  [call(): pl.pallas_call(kernel, out_shape=[jax.ShapeDtypeStruct(shape, dtype) for...]
  transfers between devices with their start and end apart: 1 -> 4, of which waited for: 1 -> 4; matrix products, arithmetic and copies ran while one was open for 0% -> 0% of each run, Pallas kernels for 0% -> 0%
where the time goes in v2:
time: 248 us; the launch traced here: 247 us
  blocking collectives  155 us (62%)
  starting transfers between devices  36.6 us (15%)
  waiting for transfers between devices  25.5 us (10%)
  Pallas kernels  21.7 us (9%)
  local copies, waits for them, and re-layouts  5.24 us (2%)
  between operations  3.25 us (1%)
    all_to_all x9, blocking collectives, exchange(): return lax.all_to_all(x, axis, 0, 0, tiled=True)  155 us
    all_to_all x2, starting transfers between devices, exchange(): return lax.all_to_all(x, axis, 0, 0, tiled=True)  24.5 us
    all_to_all x2, waiting for transfers between devices, exchange(): return lax.all_to_all(x, axis, 0, 0, tiled=True)  23.2 us
    pallas_call x10, Pallas kernels, call(): pl.pallas_call(kernel, out_shape=[jax.ShapeDtypeStruct(shape, dtype) for...  15.4 us
    ppermute x2, starting transfers between devices, body(): taken = lax.ppermute(give, 'core', [(0, 1), (1, 0)])  12.1 us
    pallas_call x2, Pallas kernels, h_numer(): pl.pallas_call(h_numer_kernel, grid=(COLS // H_WIDTH,), out_shape=[messag...  6.23 us
  transfers between devices with their start and end apart: 4, of which 4 were waited for; matrix products, arithmetic and copies ran while one was open for 0% of the time, Pallas kernels for 0%

profile of v2, /device:TPU:1, one launch (start us, length us, event | category | flops | bytes accessed | tf_op | source)
XLA Modules:
  0.0 247.1 jit_solution(4313082888967867472)
XLA Ops:
  0.6 0.0 copy-start.2
  0.6 0.9 copy.8
  1.6 1.3 shard_map.58
  2.9 10.2 %all-to-all-start = ((bf16[16,112,128]{2,1,0:T(8,128)(2,1)}), bf16[16,112,128]{2,1,0:T(8,128)(2,1)S(1)}, u32[]{:S(2)}, u32[]{:S(2)}) async-start(bf16[16,112,128]{2,1,0:T(8,128)(2,1)} %shard_map.58), calls=%async_computation | async-start | bytes 917504 | tf_op jit(solution)/shard_map/all_to_all | solution.py:267
  13.1 15.3 %all-to-all-done.got = bf16[16,112,128]{2,1,0:T(8,128)(2,1)S(1)} async-done(((bf16[16,112,128]{2,1,0:T(8,128)(2,1)}), bf16[16,112,128]{2,1,0:T(8,128)(2,1)S(1)}, u32[]{:S(2)}, u32[]{:S(2)}) %all-to-all-start) | async-done | bytes 458784 | tf_op jit(solution)/shard_map/all_to_all | solution.py:267
  28.4 0.0 copy-start
  28.4 2.3 copy-done
  30.7 0.0 copy-start.1
  30.7 3.1 %shard_map.59 = (bf16[16,64,128]{2,1,0:T(8,128)(2,1)S(1)}, bf16[16,64,128]{2,1,0:T(8,128)(2,1)S(1)}) custom-call(s32[1]{0:T(128)} %bitcast.core, bf16[16,112,128]{2,1,0:T(8,128)(2,1)S(1)} %all-to-all-done.got, bf16[2304,1024]{1,0:T(8,128)(2,1)S(1)} %copy-done), custom_call_target="tpu_custom_call" | custom-call | flops 301989888 | bytes 4718592 | tf_op jit(solution)/shard_map/pallas_call | solution.py:246
  33.9 4.2 %collective-permute-start = (bf16[16,64,128]{2,1,0:T(8,128)(2,1)S(1)}, bf16[16,64,128]{2,1,0:T(8,128)(2,1)S(1)}, u32[]{:S(2)}, u32[]{:S(2)}) collective-permute-start(bf16[16,64,128]{2,1,0:T(8,128)(2,1)S(1)} %get-tuple-element.16), channel_id=1, source_target_pairs={{0,16},{16,0},{1,17},{17,1},{2,18},{18,2},{3,19},{19,3},{4,20},{20... | collective-permute-start | bytes 786440 | tf_op jit(solution)/shard_map/ppermute | solution.py:277
  38.1 1.1 collective-permute-done.got
  39.3 0.3 shard_map.60
  39.5 18.9 %all_to_all.55.got = bf16[16,64,128]{2,1,0:T(8,128)(2,1)S(1)} all-to-all(bf16[16,64,128]{2,1,0:T(8,128)(2,1)S(1)} %shard_map.60), channel_id=1, replica_groups=mesh['pairs'=16,'core'=2,'samples'=16] {'pairs'}, dimensions={0} | all-to-all | bytes 524288 | tf_op jit(solution)/shard_map/all_to_all | solution.py:267
  58.4 0.0 copy-done.2
  58.4 0.7 shard_map.61
  59.1 17.6 %all_to_all.56.got = bf16[32,32,128]{2,1,0:T(8,128)(2,1)S(1)} all-to-all(bf16[32,32,128]{2,1,0:T(8,128)(2,1)S(1)} %get-tuple-element.17), channel_id=1, replica_groups=mesh['pairs'=16,'core'=2,'samples'=16] {'pairs','core'}, dimensions={0} | all-to-all | bytes 524288 | tf_op jit(solution)/shard_map/all_to_all | solution.py:267
  76.8 0.0 copy-done.1
  76.8 2.7 %shard_map.62 = bf16[16,176,128]{2,1,0:T(8,128)(2,1)S(1)} custom-call(bf16[32,32,128]{2,1,0:T(8,128)(2,1)S(1)} %all_to_all.56.got, bf16[2304,1024]{1,0:T(8,128)(2,1)S(1)} %copy-done.1), custom_call_target="tpu_custom_call" | custom-call | flops 301989888 | bytes 4718592 | tf_op jit(solution)/shard_map/pallas_call | solution.py:232
  79.5 20.9 %all_to_all.57.got = bf16[16,176,128]{2,1,0:T(8,128)(2,1)S(1)} all-to-all(bf16[16,176,128]{2,1,0:T(8,128)(2,1)S(1)} %shard_map.62), channel_id=1, replica_groups=mesh['pairs'=16,'core'=2,'samples'=16] {'samples'}, dimensions={0} | all-to-all | bytes 1441792 | tf_op jit(solution)/shard_map/all_to_all | solution.py:267
  100.4 1.2 shard_map.63
  101.6 15.8 %all_to_all.58.got = bf16[16,112,128]{2,1,0:T(8,128)(2,1)S(1)} all-to-all(bf16[16,112,128]{2,1,0:T(8,128)(2,1)S(1)} %get-tuple-element.18), channel_id=1, replica_groups=mesh['pairs'=16,'core'=2,'samples'=16] {'samples'}, dimensions={0} | all-to-all | bytes 917504 | tf_op jit(solution)/shard_map/all_to_all | solution.py:267
  117.4 3.1 %shard_map.64 = (bf16[16,64,128]{2,1,0:T(8,128)(2,1)S(1)}, bf16[16,64,128]{2,1,0:T(8,128)(2,1)S(1)}) custom-call(s32[1]{0:T(128)} %bitcast.core, bf16[16,112,128]{2,1,0:T(8,128)(2,1)S(1)} %all_to_all.58.got, bf16[2304,1024]{1,0:T(8,128)(2,1)S(1)} %copy-done.1), custom_call_target="tpu_custom_call" | custom-call | flops 301989888 | bytes 4718592 | tf_op jit(solution)/shard_map/pallas_call | solution.py:246
  120.5 7.9 %collective-permute-start.1 = (bf16[16,64,128]{2,1,0:T(8,128)(2,1)S(1)}, bf16[16,64,128]{2,1,0:T(8,128)(2,1)S(1)}, u32[]{:S(2)}, u32[]{:S(2)}) collective-permute-start(bf16[16,64,128]{2,1,0:T(8,128)(2,1)S(1)} %get-tuple-element.20), channel_id=1, source_target_pairs={{0,16},{16,0},{1,17},{17,1},{2,18},{18,2},{3,19},{19,3},{4,20},{20... | collective-permute-start | bytes 786440 | tf_op jit(solution)/shard_map/ppermute | solution.py:277
  128.4 1.1 collective-permute-done.1.got
  129.5 0.3 shard_map.65
  129.8 15.7 %all_to_all.59.got = bf16[16,64,128]{2,1,0:T(8,128)(2,1)S(1)} all-to-all(bf16[16,64,128]{2,1,0:T(8,128)(2,1)S(1)} %shard_map.65), channel_id=1, replica_groups=mesh['pairs'=16,'core'=2,'samples'=16] {'pairs'}, dimensions={0} | all-to-all | bytes 524288 | tf_op jit(solution)/shard_map/all_to_all | solution.py:267
  145.6 1.2 shard_map.66
  146.8 17.6 %all_to_all.60.got.got_h = bf16[32,32,128]{2,1,0:T(8,128)(2,1)S(1)} all-to-all(bf16[32,32,128]{2,1,0:T(8,128)(2,1)S(1)} %get-tuple-element.22), channel_id=1, replica_groups=mesh['pairs'=16,'core'=2,'samples'=16] {'pairs','core'}, dimensions={0} | all-to-all | bytes 524288 | tf_op jit(solution)/shard_map/all_to_all | solution.py:267
  164.4 2.7 %shard_map.67 = bf16[16,176,128]{2,1,0:T(8,128)(2,1)S(1)} custom-call(bf16[32,32,128]{2,1,0:T(8,128)(2,1)S(1)} %all_to_all.60.got.got_h, bf16[2304,1024]{1,0:T(8,128)(2,1)S(1)} %copy-done.1), custom_call_target="tpu_custom_call" | custom-call | flops 301989888 | bytes 4718592 | tf_op jit(solution)/shard_map/pallas_call | solution.py:232
  167.1 21.1 %all_to_all.61.got = bf16[16,176,128]{2,1,0:T(8,128)(2,1)S(1)} all-to-all(bf16[16,176,128]{2,1,0:T(8,128)(2,1)S(1)} %shard_map.67), channel_id=1, replica_groups=mesh['pairs'=16,'core'=2,'samples'=16] {'samples'}, dimensions={0} | all-to-all | bytes 1441792 | tf_op jit(solution)/shard_map/all_to_all | solution.py:267
  188.2 0.8 shard_map.68
  188.9 15.0 %all_to_all.62.got_w = bf16[16,80,128]{2,1,0:T(8,128)(2,1)S(1)} all-to-all(bf16[16,80,128]{2,1,0:T(8,128)(2,1)S(1)} %get-tuple-element.26), channel_id=1, replica_groups=mesh['pairs'=16,'core'=2,'samples'=16] {'samples'}, dimensions={0} | all-to-all | bytes 655360 | tf_op jit(solution)/shard_map/all_to_all | solution.py:267
  204.0 4.4 %shard_map.69 = f32[16,8,128]{2,1,0:T(8,128)S(1)} custom-call(bf16[16,80,128]{2,1,0:T(8,128)(2,1)S(1)} %all_to_all.62.got_w, bf16[32,32,128]{2,1,0:T(8,128)(2,1)S(1)} %all_to_all.60.got.got_h, bf16[2304,1024]{1,0:T(8,128)(2,1)S(1)} %copy-done.1), custom_call_target="tpu_custom_call" | custom-call | flops 301989888 | bytes 4718592 | tf_op jit(solution)/shard_map/pallas_call | solution.py:232
  208.4 12.1 %all_to_all.63 = f32[16,8,128]{2,1,0:T(8,128)S(1)} all-to-all(f32[16,8,128]{2,1,0:T(8,128)S(1)} %shard_map.69), channel_id=1, replica_groups=mesh['pairs'=16,'core'=2,'samples'=16] {'samples'}, dimensions={0} | all-to-all | bytes 131072 | tf_op jit(solution)/shard_map/all_to_all | solution.py:267
  220.5 0.7 broadcast_in_dim.2
  221.1 14.3 %all-to-all-start.10 = ((f32[32,8,128]{2,1,0:T(8,128)}), f32[32,8,128]{2,1,0:T(8,128)S(1)}, u32[]{:S(2)}, u32[]{:S(2)}) async-start(f32[32,8,128]{2,1,0:T(8,128)} %broadcast_in_dim.2), calls=%async_computation.10 | async-start | bytes 262144 | tf_op jit(solution)/shard_map/all_to_all | solution.py:267
  235.4 0.7 copy.9
  236.2 7.9 %all-to-all-done.10 = f32[32,8,128]{2,1,0:T(8,128)S(1)} async-done(((f32[32,8,128]{2,1,0:T(8,128)}), f32[32,8,128]{2,1,0:T(8,128)S(1)}, u32[]{:S(2)}, u32[]{:S(2)}) %all-to-all-start.10) | async-done | bytes 131104 | tf_op jit(solution)/shard_map/all_to_all | solution.py:267
  244.1 0.6 fusion
  (2 shorter events, 0.1 us)
Async XLA Ops:
  0.6 57.8 %copy-start.2 = (f32[64,32]{0,1:T(8,128)S(1)}, f32[64,32]{0,1:T(8,128)}, u32[]{:S(2)}) copy-start(f32[64,32]{0,1:T(8,128)} %param.5) | copy-start | bytes 24580
  2.9 25.6 %all-to-all-start = ((bf16[16,112,128]{2,1,0:T(8,128)(2,1)}), bf16[16,112,128]{2,1,0:T(8,128)(2,1)S(1)}, u32[]{:S(2)}, u32[]{:S(2)}) async-start(bf16[16,112,128]{2,1,0:T(8,128)(2,1)} %shard_map.58), calls=%async_computation | async-start | bytes 917504 | tf_op jit(solution)/shard_map/all_to_all | solution.py:267
  28.4 2.3 copy-start
  30.7 46.0 %copy-start.1 = (bf16[2304,1024]{1,0:T(8,128)(2,1)S(1)}, bf16[2304,1024]{1,0:T(8,128)(2,1)}, u32[]{:S(2)}) copy-start(bf16[2304,1024]{1,0:T(8,128)(2,1)} %tel.9) | copy-start | bytes 14155780
  33.9 5.4 %collective-permute-start = (bf16[16,64,128]{2,1,0:T(8,128)(2,1)S(1)}, bf16[16,64,128]{2,1,0:T(8,128)(2,1)S(1)}, u32[]{:S(2)}, u32[]{:S(2)}) collective-permute-start(bf16[16,64,128]{2,1,0:T(8,128)(2,1)S(1)} %get-tuple-element.16), channel_id=1, source_target_pairs={{0,16},{16,0},{1,17},{17,1},{2,18},{18,2},{3,19},{19,3},{4,20},{20... | collective-permute-start | bytes 786440 | tf_op jit(solution)/shard_map/ppermute | solution.py:277
  120.5 9.1 %collective-permute-start.1 = (bf16[16,64,128]{2,1,0:T(8,128)(2,1)S(1)}, bf16[16,64,128]{2,1,0:T(8,128)(2,1)S(1)}, u32[]{:S(2)}, u32[]{:S(2)}) collective-permute-start(bf16[16,64,128]{2,1,0:T(8,128)(2,1)S(1)} %get-tuple-element.20), channel_id=1, source_target_pairs={{0,16},{16,0},{1,17},{17,1},{2,18},{18,2},{3,19},{19,3},{4,20},{20... | collective-permute-start | bytes 786440 | tf_op jit(solution)/shard_map/ppermute | solution.py:277
  221.1 22.9 %all-to-all-start.10 = ((f32[32,8,128]{2,1,0:T(8,128)}), f32[32,8,128]{2,1,0:T(8,128)S(1)}, u32[]{:S(2)}, u32[]{:S(2)}) async-start(f32[32,8,128]{2,1,0:T(8,128)} %broadcast_in_dim.2), calls=%async_computation.10 | async-start | bytes 262144 | tf_op jit(solution)/shard_map/all_to_all | solution.py:267

commit v3 on v2

--- a/solution.py
+++ b/solution.py
@@ -91,23 +91,26 @@
     )
 
 
-def gram_of(halves):
-    four = lax.dot_general(
-        halves, halves, (((0,), (0,)), ((), ())), preferred_element_type=F32
-    )
+def products(halves):
+    return lax.dot_general(halves, halves, (((0,), (0,)), ((), ())), preferred_element_type=F32)
+
+
+def quarters(four):
     two = four[:K] + four[K:]
     return two[:, :K] + two[:, K:]
 
 
+def two_halves(w):
+    tail = jnp.concatenate([w[W_HALF:], jnp.zeros((2 * W_HALF - W_OWN, K), F32)], axis=0)
+    return jnp.concatenate([w[:W_HALF], tail], axis=1).astype(BF16)
+
+
 def fill_w(w, out):
-    tail = jnp.concatenate([w[W_HALF:], jnp.zeros((2 * W_HALF - W_OWN, K), F32)], axis=0)
-    rows = jnp.concatenate([w[:W_HALF], tail], axis=1).astype(BF16)
+    rows = two_halves(w)
+    gram = pack_gram(quarters(products(split(w))))
     for i in range(SAMPLES):
         out[i, :W_HALF, :] = rows
-    if out.shape[1] > W_HALF:
-        gram = pack_gram(gram_of(split(w)))
-        for i in range(SAMPLES):
-            out[i, W_HALF:, :] = gram
+        out[i, W_HALF:, :] = gram
 
 
 def own_rows(ref, i):
@@ -167,7 +170,10 @@
 
 def w_numer_kernel(got, tel, out):
     halves = got[...].reshape(COLS, 128)
-    gram = pack_gram(gram_of(halves))
+    four = products(halves)
+    gram = pack_gram(quarters(four))
+    if out.shape[1] > W_RED:
+        gram = jnp.concatenate([gram, pack_gram(four[:K, :K])], axis=0)
     high = halves[:, :K]
     per = 4
     block = per * W_OWN
@@ -183,23 +189,60 @@
     lax.fori_loop(0, ROWS // block, step, 0)
 
 
-def w_update_kernel(got, w, w_out, out):
-    total = jnp.zeros((W_RED, 128), F32)
+def w_new(got, w):
+    total = jnp.zeros(got.shape[1:], F32)
     for i in range(SAMPLES):
         total += got[i].astype(F32)
-    gram = unpack_gram(total[W_OWN:])
+    numer = join(total[:W_OWN])
+    gram = unpack_gram(total[W_OWN:W_RED])
     old = w[...]
     below = jnp.dot(old, gram, precision=HIGHEST, preferred_element_type=F32) + epsilon
-    new = old * join(total[:W_OWN]) / below
+    return old * numer / below, numer, total[W_RED:]
+
+
+def w_update_kernel(got, w, w_out, out):
+    new, _, _ = w_new(got, w)
     w_out[...] = new
     fill_w(new, out)
 
 
+def tile_pair(left, right):
+    lane = lax.broadcasted_iota(jnp.int32, (8, 128), 1)
+    return jnp.where(lane < K, left, right)
+
+
+def w_last_kernel(got, w, energy, w_out, out):
+    new, numer, rest = w_new(got, w)
+    w_out[...] = new
+    rounded = new.astype(BF16).astype(F32)
+    gram = unpack_gram(rest)
+    fitted = jnp.dot(rounded, gram, precision=HIGHEST, preferred_element_type=F32)
+    share = jnp.sum(rounded * (fitted - 2.0 * numer))
+    pair = tile_pair(share, energy[...])
+    for i in range(SAMPLES):
+        out[i] = pair
+
+
+def energy_kernel(tel, out):
+    def step(i, energy):
+        rows = pl.ds(pl.multiple_of(i * W_OWN, W_OWN), W_OWN)
+        values = tel[rows, :].astype(F32)
+        return energy + jnp.sum((values * values).reshape(W_OWN // 8, 8, COLS), axis=0)
+
+    energy = lax.fori_loop(0, SAMPLES, step, jnp.zeros((8, COLS), F32))
+    out[...] = jnp.full((8, 128), jnp.sum(energy), F32)
+
+
+def last_rows_kernel(w, out):
+    rows = two_halves(w[...])
+    for i in range(SAMPLES):
+        out[i] = rows
+
+
 def error_kernel(got_w, got_h, tel, out):
     high = got_h[...].reshape(COLS, 128)[:, :K]
 
-    def step(i, carry):
-        error, energy = carry
+    def step(i, error):
         rows = pl.ds(pl.multiple_of(i * W_OWN, W_OWN), W_OWN)
         rebuilt = lax.dot_general(
             own_rows(got_w, i).astype(BF16),
@@ -207,18 +250,13 @@
             (((1,), (1,)), ((), ())),
             preferred_element_type=F32,
         )
-        values = tel[rows, :].astype(F32)
-        difference = values - rebuilt
-        error += jnp.sum((difference * difference).reshape(W_OWN // 8, 8, COLS), axis=0)
-        energy += jnp.sum((values * values).reshape(W_OWN // 8, 8, COLS), axis=0)
-        return error, energy
-
-    zero = jnp.zeros((8, COLS), F32)
-    error, energy = lax.fori_loop(0, SAMPLES, step, (zero, zero))
-    lane = lax.broadcasted_iota(jnp.int32, (8, 128), 1)
-    pair = jnp.where(lane < K, jnp.sum(error), jnp.sum(energy))
-    for i in range(SAMPLES):
-        out[i] = pair
+        difference = tel[rows, :].astype(F32) - rebuilt
+        return error + jnp.sum((difference * difference).reshape(W_OWN // 8, 8, COLS), axis=0)
+
+    error = lax.fori_loop(0, SAMPLES, step, jnp.zeros((8, COLS), F32))
+    share = jnp.full((8, 128), jnp.sum(error), F32)
+    for i in range(SAMPLES):
+        out[i] = share
 
 
 VMEM = pl.BlockSpec(memory_space=pltpu.VMEM)
@@ -267,12 +305,27 @@
     return lax.all_to_all(x, axis, 0, 0, tiled=True)
 
 
+def sum_everywhere(shares):
+    part = jnp.sum(exchange(shares, "samples"), axis=0)
+    part = exchange(jnp.broadcast_to(part[None], (CHIPS, 8, 128)), ("pairs", "core"))
+    return jnp.sum(part, axis=0)
+
+
 def body(telemetry, chip_factors, sample_factors):
     core = lax.axis_index("core").reshape(1)
     w, h = chip_factors.T, sample_factors.T
     (sent,) = call(start_kernel, (w,), [((SAMPLES, W_MSG, 128), BF16)])
     got_w = exchange(sent, "samples")
+    (energy,) = call(
+        energy_kernel,
+        (telemetry,),
+        [((8, 128), F32)],
+        pl.CostEstimate(
+            flops=2 * ROWS * COLS, bytes_accessed=2 * ROWS * COLS, transcendentals=0
+        ),
+    )
     for sweep in range(ITERS):
+        last = sweep == ITERS - 1
         keep, give = h_numer(core, got_w, telemetry)
         taken = lax.ppermute(give, "core", [(0, 1), (1, 0)])
         (sent,) = call(pair_kernel, (keep, taken), [((PAIRS, H_RED, 128), BF16)])
@@ -281,22 +334,40 @@
             h_update_kernel, (got, h), [((H_OWN, K), F32), ((CHIPS, H_OWN, 128), BF16)]
         )
         got_h = exchange(sent, ("pairs", "core"))
-        (sent,) = call(
-            w_numer_kernel, (got_h, telemetry), [((SAMPLES, W_RED, 128), BF16)], PRODUCT
+        rows = W_RED + GRAM if last else W_RED
+        (sent,) = call(w_numer_kernel, (got_h, telemetry), [((SAMPLES, rows, 128), BF16)], PRODUCT)
+        got = exchange(sent, "samples")
+        if not last:
+            w, sent = call(
+                w_update_kernel, (got, w), [((W_OWN, K), F32), ((SAMPLES, W_MSG, 128), BF16)]
+            )
+            got_w = exchange(sent, "samples")
+    w, shares = call(
+        w_last_kernel, (got, w, energy), [((W_OWN, K), F32), ((SAMPLES, 8, 128), F32)]
+    )
+    sums = sum_everywhere(shares)
+    total = sums[0, K]
+    expanded = sums[0, 0] + total
+
+    def direct(w, got_h, telemetry):
+        (sent,) = call(last_rows_kernel, (w,), [((SAMPLES, W_HALF, 128), BF16)])
+        (shares,) = call(
+            error_kernel,
+            (exchange(sent, "samples"), got_h, telemetry),
+            [((SAMPLES, 8, 128), F32)],
+            PRODUCT,
         )
-        got = exchange(sent, "samples")
-        rows = W_MSG if sweep < ITERS - 1 else W_HALF
-        w, sent = call(
-            w_update_kernel, (got, w), [((W_OWN, K), F32), ((SAMPLES, rows, 128), BF16)]
-        )
-        got_w = exchange(sent, "samples")
-    (pair,) = call(
-        error_kernel, (got_w, got_h, telemetry), [((SAMPLES, 8, 128), F32)], PRODUCT
-    )
-    pair = jnp.sum(exchange(pair, "samples"), axis=0)
-    pair = exchange(jnp.broadcast_to(pair[None], (CHIPS, 8, 128)), ("pairs", "core"))
-    pair = jnp.sum(pair, axis=0)
-    return w.T, h.T, jnp.sqrt(pair[0, 0] / pair[0, K])
+        return sum_everywhere(shares)[0, 0]
+
+    fit_error = lax.cond(
+        expanded < 0.02 * total,
+        direct,
+        lambda *operands: expanded,
+        w,
+        got_h,
+        telemetry,
+    )
+    return w.T, h.T, jnp.sqrt(fit_error / total)
 
 
 def solution(mesh):

time: 248 us -> 232 us (0.935)
  blocking collectives: 155 us -> 123 us
  waiting for transfers between devices: 25.5 us -> 40.3 us
    all_to_all x9 -> x7, blocking collectives: 155 us -> 123 us  [exchange(): return lax.all_to_all(x, axis, 0, 0, tiled=True)]
    all_to_all x2 -> x3, waiting for transfers between devices: 23.2 us -> 38 us  [exchange(): return lax.all_to_all(x, axis, 0, 0, tiled=True)]
    all_to_all x2 -> x3, starting transfers between devices: 24.5 us -> 25 us  [exchange(): return lax.all_to_all(x, axis, 0, 0, tiled=True)]
  transfers between devices with their start and end apart: 4 -> 5, of which waited for: 4 -> 5; matrix products, arithmetic and copies ran while one was open for 0% -> 0% of each run, Pallas kernels for 0% -> 1%
where the time goes in v3:
time: 232 us; the launch traced here: 231 us
  blocking collectives  123 us (53%)
  waiting for transfers between devices  40.3 us (17%)
  starting transfers between devices  37.2 us (16%)
  Pallas kernels  22.9 us (10%)
  between operations  4.6 us (2%)
  local copies, waits for them, and re-layouts  2.91 us (1%)
    all_to_all x7, blocking collectives, exchange(): return lax.all_to_all(x, axis, 0, 0, tiled=True)  123 us
    all_to_all x3, waiting for transfers between devices, exchange(): return lax.all_to_all(x, axis, 0, 0, tiled=True)  38 us
    all_to_all x3, starting transfers between devices, exchange(): return lax.all_to_all(x, axis, 0, 0, tiled=True)  25 us
    pallas_call x10, Pallas kernels, call(): pl.pallas_call(kernel, out_shape=[jax.ShapeDtypeStruct(shape, dtype) for...  15 us
    ppermute x2, starting transfers between devices, body(): taken = lax.ppermute(give, 'core', [(0, 1), (1, 0)])  12.2 us
    pallas_call x2, Pallas kernels, h_numer(): pl.pallas_call(h_numer_kernel, grid=(COLS // H_WIDTH,), out_shape=[messag...  7.85 us
  transfers between devices with their start and end apart: 5, of which 5 were waited for; matrix products, arithmetic and copies ran while one was open for 0% of the time, Pallas kernels for 1%

profile of v3, /device:TPU:1, one launch (start us, length us, event | category | flops | bytes accessed | tf_op | source)
XLA Modules:
  0.0 230.8 jit_solution(10334562729408310433)
XLA Ops:
  0.6 0.0 copy-start
  0.6 0.9 copy.8
  1.6 1.3 shard_map.58
  2.8 10.2 %all-to-all-start.3 = ((bf16[16,112,128]{2,1,0:T(8,128)(2,1)}), bf16[16,112,128]{2,1,0:T(8,128)(2,1)S(1)}, u32[]{:S(2)}, u32[]{:S(2)}) async-start(bf16[16,112,128]{2,1,0:T(8,128)(2,1)} %shard_map.58), calls=%async_computation.3 | async-start | bytes 917504 | tf_op jit(solution)/shard_map/all_to_all | solution.py:305
  13.1 15.3 %all-to-all-done.3.got = bf16[16,112,128]{2,1,0:T(8,128)(2,1)S(1)} async-done(((bf16[16,112,128]{2,1,0:T(8,128)(2,1)}), bf16[16,112,128]{2,1,0:T(8,128)(2,1)S(1)}, u32[]{:S(2)}, u32[]{:S(2)}) %all-to-all-start.3) | async-done | bytes 458784 | tf_op jit(solution)/shard_map/all_to_all | solution.py:305
  28.4 0.0 copy-start.1
  28.4 4.7 %shard_map.59 = (bf16[16,64,128]{2,1,0:T(8,128)(2,1)S(1)}, bf16[16,64,128]{2,1,0:T(8,128)(2,1)S(1)}) custom-call(s32[1]{0:T(128)} %bitcast.1.core, bf16[16,112,128]{2,1,0:T(8,128)(2,1)S(1)} %all-to-all-done.3.got, bf16[2304,1024]{1,0:T(8,128)(2,1)} %tel.9), custom_call_target="tpu_custom_call" | custom-call | flops 301989888 | bytes 4718592 | tf_op jit(solution)/shard_map/pallas_call | solution.py:284
  33.2 4.2 %collective-permute-start = (bf16[16,64,128]{2,1,0:T(8,128)(2,1)S(1)}, bf16[16,64,128]{2,1,0:T(8,128)(2,1)S(1)}, u32[]{:S(2)}, u32[]{:S(2)}) collective-permute-start(bf16[16,64,128]{2,1,0:T(8,128)(2,1)S(1)} %get-tuple-element.29), channel_id=1, source_target_pairs={{0,16},{16,0},{1,17},{17,1},{2,18},{18,2},{3,19},{19,3},{4,20},{20... | collective-permute-start | bytes 786440 | tf_op jit(solution)/shard_map/ppermute | solution.py:330
  37.4 1.1 collective-permute-done.got
  38.5 0.3 shard_map.60
  38.8 18.9 %all_to_all.65.got = bf16[16,64,128]{2,1,0:T(8,128)(2,1)S(1)} all-to-all(bf16[16,64,128]{2,1,0:T(8,128)(2,1)S(1)} %shard_map.60), channel_id=1, replica_groups=mesh['pairs'=16,'core'=2,'samples'=16] {'pairs'}, dimensions={0} | all-to-all | bytes 524288 | tf_op jit(solution)/shard_map/all_to_all | solution.py:305
  57.7 0.0 copy-done
  57.7 0.7 shard_map.61
  58.4 17.6 %all_to_all.66.got = bf16[32,32,128]{2,1,0:T(8,128)(2,1)S(1)} all-to-all(bf16[32,32,128]{2,1,0:T(8,128)(2,1)S(1)} %get-tuple-element.30), channel_id=1, replica_groups=mesh['pairs'=16,'core'=2,'samples'=16] {'pairs','core'}, dimensions={0} | all-to-all | bytes 524288 | tf_op jit(solution)/shard_map/all_to_all | solution.py:305
  76.1 0.0 copy-done.1
  76.1 2.7 %shard_map.62 = bf16[16,176,128]{2,1,0:T(8,128)(2,1)S(1)} custom-call(bf16[32,32,128]{2,1,0:T(8,128)(2,1)S(1)} %all_to_all.66.got, bf16[2304,1024]{1,0:T(8,128)(2,1)S(1)} %copy-done.1), custom_call_target="tpu_custom_call" | custom-call | flops 301989888 | bytes 4718592 | tf_op jit(solution)/shard_map/pallas_call | solution.py:270
  78.7 20.9 %all_to_all.67.got = bf16[16,176,128]{2,1,0:T(8,128)(2,1)S(1)} all-to-all(bf16[16,176,128]{2,1,0:T(8,128)(2,1)S(1)} %shard_map.62), channel_id=1, replica_groups=mesh['pairs'=16,'core'=2,'samples'=16] {'samples'}, dimensions={0} | all-to-all | bytes 1441792 | tf_op jit(solution)/shard_map/all_to_all | solution.py:305
  99.6 1.2 shard_map.63
  100.8 15.8 %all_to_all.68.got = bf16[16,112,128]{2,1,0:T(8,128)(2,1)S(1)} all-to-all(bf16[16,112,128]{2,1,0:T(8,128)(2,1)S(1)} %get-tuple-element.31), channel_id=1, replica_groups=mesh['pairs'=16,'core'=2,'samples'=16] {'samples'}, dimensions={0} | all-to-all | bytes 917504 | tf_op jit(solution)/shard_map/all_to_all | solution.py:305
  116.6 3.1 %shard_map.64 = (bf16[16,64,128]{2,1,0:T(8,128)(2,1)S(1)}, bf16[16,64,128]{2,1,0:T(8,128)(2,1)S(1)}) custom-call(s32[1]{0:T(128)} %bitcast.1.core, bf16[16,112,128]{2,1,0:T(8,128)(2,1)S(1)} %all_to_all.68.got, bf16[2304,1024]{1,0:T(8,128)(2,1)S(1)} %copy-done.1), custom_call_target="tpu_custom_call" | custom-call | flops 301989888 | bytes 4718592 | tf_op jit(solution)/shard_map/pallas_call | solution.py:284
  119.7 7.9 %collective-permute-start.1 = (bf16[16,64,128]{2,1,0:T(8,128)(2,1)S(1)}, bf16[16,64,128]{2,1,0:T(8,128)(2,1)S(1)}, u32[]{:S(2)}, u32[]{:S(2)}) collective-permute-start(bf16[16,64,128]{2,1,0:T(8,128)(2,1)S(1)} %get-tuple-element.33), channel_id=1, source_target_pairs={{0,16},{16,0},{1,17},{17,1},{2,18},{18,2},{3,19},{19,3},{4,20},{20... | collective-permute-start | bytes 786440 | tf_op jit(solution)/shard_map/ppermute | solution.py:330
  127.7 1.1 collective-permute-done.1.got
  128.8 0.3 shard_map.65
  129.1 15.8 %all_to_all.69.got = bf16[16,64,128]{2,1,0:T(8,128)(2,1)S(1)} all-to-all(bf16[16,64,128]{2,1,0:T(8,128)(2,1)S(1)} %shard_map.65), channel_id=1, replica_groups=mesh['pairs'=16,'core'=2,'samples'=16] {'pairs'}, dimensions={0} | all-to-all | bytes 524288 | tf_op jit(solution)/shard_map/all_to_all | solution.py:305
  144.9 1.2 shard_map.66
  146.1 17.6 %all_to_all.70.got = bf16[32,32,128]{2,1,0:T(8,128)(2,1)S(1)} all-to-all(bf16[32,32,128]{2,1,0:T(8,128)(2,1)S(1)} %get-tuple-element.35), channel_id=1, replica_groups=mesh['pairs'=16,'core'=2,'samples'=16] {'pairs','core'}, dimensions={0} | all-to-all | bytes 524288 | tf_op jit(solution)/shard_map/all_to_all | solution.py:305
  163.7 3.6 %shard_map.67 = bf16[16,208,128]{2,1,0:T(8,128)(2,1)} custom-call(bf16[32,32,128]{2,1,0:T(8,128)(2,1)S(1)} %all_to_all.70.got, bf16[2304,1024]{1,0:T(8,128)(2,1)S(1)} %copy-done.1), custom_call_target="tpu_custom_call" | custom-call | flops 301989888 | bytes 4718592 | tf_op jit(solution)/shard_map/pallas_call | solution.py:270
  167.3 4.1 %all-to-all-start.10 = ((bf16[16,208,128]{2,1,0:T(8,128)(2,1)}), bf16[16,208,128]{2,1,0:T(8,128)(2,1)S(1)}, u32[]{:S(2)}, u32[]{:S(2)}) async-start(bf16[16,208,128]{2,1,0:T(8,128)(2,1)} %shard_map.67), calls=%async_computation.10 | async-start | bytes 1703936 | tf_op jit(solution)/shard_map/all_to_all | solution.py:305
  171.4 2.8 %shard_map.68.energy = f32[8,128]{1,0:T(8,128)S(1)} custom-call(bf16[2304,1024]{1,0:T(8,128)(2,1)} %tel.9), custom_call_target="tpu_custom_call" | custom-call | flops 4718592 | bytes 4718592 | tf_op jit(solution)/shard_map/pallas_call | solution.py:270
  174.2 14.9 %all-to-all-done.10.got = bf16[16,208,128]{2,1,0:T(8,128)(2,1)S(1)} async-done(((bf16[16,208,128]{2,1,0:T(8,128)(2,1)}), bf16[16,208,128]{2,1,0:T(8,128)(2,1)S(1)}, u32[]{:S(2)}, u32[]{:S(2)}) %all-to-all-start.10) | async-done | bytes 852000 | tf_op jit(solution)/shard_map/all_to_all | solution.py:305
  189.1 1.1 shard_map.69
  190.2 16.3 %all_to_all.71 = f32[16,8,128]{2,1,0:T(8,128)S(1)} all-to-all(f32[16,8,128]{2,1,0:T(8,128)S(1)} %get-tuple-element.39), channel_id=1, replica_groups=mesh['pairs'=16,'core'=2,'samples'=16] {'samples'}, dimensions={0} | all-to-all | bytes 131072 | tf_op jit(solution)/shard_map/all_to_all | solution.py:305
  206.5 0.7 broadcast_in_dim.4
  207.2 10.7 %all-to-all-start.12 = ((f32[32,8,128]{2,1,0:T(8,128)}), f32[32,8,128]{2,1,0:T(8,128)S(1)}, u32[]{:S(2)}, u32[]{:S(2)}) async-start(f32[32,8,128]{2,1,0:T(8,128)} %broadcast_in_dim.4), calls=%async_computation.12 | async-start | bytes 262144 | tf_op jit(solution)/shard_map/all_to_all | solution.py:305
  217.9 0.7 copy.9
  218.6 7.8 %all-to-all-done.12 = f32[32,8,128]{2,1,0:T(8,128)S(1)} async-done(((f32[32,8,128]{2,1,0:T(8,128)}), f32[32,8,128]{2,1,0:T(8,128)S(1)}, u32[]{:S(2)}, u32[]{:S(2)}) %all-to-all-start.12) | async-done | bytes 131104 | tf_op jit(solution)/shard_map/all_to_all | solution.py:305
  226.4 0.6 fusion
  (3 shorter events, 0.1 us)
Async XLA Ops:
  0.6 57.1 %copy-start = (f32[64,32]{0,1:T(8,128)S(1)}, f32[64,32]{0,1:T(8,128)}, u32[]{:S(2)}) copy-start(f32[64,32]{0,1:T(8,128)} %param.7) | copy-start | bytes 24580
  2.8 25.6 %all-to-all-start.3 = ((bf16[16,112,128]{2,1,0:T(8,128)(2,1)}), bf16[16,112,128]{2,1,0:T(8,128)(2,1)S(1)}, u32[]{:S(2)}, u32[]{:S(2)}) async-start(bf16[16,112,128]{2,1,0:T(8,128)(2,1)} %shard_map.58), calls=%async_computation.3 | async-start | bytes 917504 | tf_op jit(solution)/shard_map/all_to_all | solution.py:305
  28.4 47.7 %copy-start.1 = (bf16[2304,1024]{1,0:T(8,128)(2,1)S(1)}, bf16[2304,1024]{1,0:T(8,128)(2,1)}, u32[]{:S(2)}) copy-start(bf16[2304,1024]{1,0:T(8,128)(2,1)} %tel.9) | copy-start | bytes 14155780
  33.2 5.4 %collective-permute-start = (bf16[16,64,128]{2,1,0:T(8,128)(2,1)S(1)}, bf16[16,64,128]{2,1,0:T(8,128)(2,1)S(1)}, u32[]{:S(2)}, u32[]{:S(2)}) collective-permute-start(bf16[16,64,128]{2,1,0:T(8,128)(2,1)S(1)} %get-tuple-element.29), channel_id=1, source_target_pairs={{0,16},{16,0},{1,17},{17,1},{2,18},{18,2},{3,19},{19,3},{4,20},{20... | collective-permute-start | bytes 786440 | tf_op jit(solution)/shard_map/ppermute | solution.py:330
  119.7 9.1 %collective-permute-start.1 = (bf16[16,64,128]{2,1,0:T(8,128)(2,1)S(1)}, bf16[16,64,128]{2,1,0:T(8,128)(2,1)S(1)}, u32[]{:S(2)}, u32[]{:S(2)}) collective-permute-start(bf16[16,64,128]{2,1,0:T(8,128)(2,1)S(1)} %get-tuple-element.33), channel_id=1, source_target_pairs={{0,16},{16,0},{1,17},{17,1},{2,18},{18,2},{3,19},{19,3},{4,20},{20... | collective-permute-start | bytes 786440 | tf_op jit(solution)/shard_map/ppermute | solution.py:330
  167.3 21.8 %all-to-all-start.10 = ((bf16[16,208,128]{2,1,0:T(8,128)(2,1)}), bf16[16,208,128]{2,1,0:T(8,128)(2,1)S(1)}, u32[]{:S(2)}, u32[]{:S(2)}) async-start(bf16[16,208,128]{2,1,0:T(8,128)(2,1)} %shard_map.67), calls=%async_computation.10 | async-start | bytes 1703936 | tf_op jit(solution)/shard_map/all_to_all | solution.py:305
  207.2 19.2 %all-to-all-start.12 = ((f32[32,8,128]{2,1,0:T(8,128)}), f32[32,8,128]{2,1,0:T(8,128)S(1)}, u32[]{:S(2)}, u32[]{:S(2)}) async-start(f32[32,8,128]{2,1,0:T(8,128)} %broadcast_in_dim.4), calls=%async_computation.12 | async-start | bytes 262144 | tf_op jit(solution)/shard_map/all_to_all | solution.py:305

commit v4 on v3

--- a/solution.py
+++ b/solution.py
@@ -27,7 +27,6 @@
 W_HALF = 80
 W_MSG = W_HALF + GRAM
 H_RED = H_OWN + GRAM
-W_RED = W_OWN + GRAM
 
 
 def split(x):
@@ -102,11 +101,32 @@
 
 def two_halves(w):
     tail = jnp.concatenate([w[W_HALF:], jnp.zeros((2 * W_HALF - W_OWN, K), F32)], axis=0)
-    return jnp.concatenate([w[:W_HALF], tail], axis=1).astype(BF16)
+    return jnp.concatenate([w[:W_HALF], tail], axis=1)
+
+
+def one_column(both):
+    return jnp.concatenate([both[:, :K], both[: W_OWN - W_HALF, K:]], axis=0)
+
+
+TOP = 14.0
+
+
+def sender_factor(i):
+    return 1.0 + i / 32.0
+
+
+def eighth_power(x):
+    x = x * x
+    x = x * x
+    return x * x
+
+
+def eighth_root(x):
+    return jnp.sqrt(jnp.sqrt(jnp.sqrt(x)))
 
 
 def fill_w(w, out):
-    rows = two_halves(w)
+    rows = two_halves(w).astype(BF16)
     gram = pack_gram(quarters(products(split(w))))
     for i in range(SAMPLES):
         out[i, :W_HALF, :] = rows
@@ -114,8 +134,7 @@
 
 
 def own_rows(ref, i):
-    both = ref[i, :W_HALF, :].astype(F32)
-    return jnp.concatenate([both[:, :K], both[: W_OWN - W_HALF, K:]], axis=0)
+    return one_column(ref[i, :W_HALF, :].astype(F32))
 
 
 def start_kernel(w, out):
@@ -168,47 +187,59 @@
         out[i] = halves
 
 
-def w_numer_kernel(got, tel, out):
+def w_numer_kernel(sender, got, tel, out, sums):
     halves = got[...].reshape(COLS, 128)
     four = products(halves)
     gram = pack_gram(quarters(four))
-    if out.shape[1] > W_RED:
+    if out.shape[1] > W_MSG:
         gram = jnp.concatenate([gram, pack_gram(four[:K, :K])], axis=0)
     high = halves[:, :K]
-    per = 4
-    block = per * W_OWN
-
-    def step(b, carry):
+    block = 4 * W_OWN
+
+    def multiply(b, largest):
         rows = pl.ds(pl.multiple_of(b * block, block), block)
         part = jnp.dot(tel[rows, :], high, preferred_element_type=F32)
-        for q in range(per):
-            out[b * per + q, :W_OWN, :] = split(part[q * W_OWN : (q + 1) * W_OWN])
-            out[b * per + q, W_OWN:, :] = gram
+        sums[rows, :] = part
+        return jnp.maximum(largest, jnp.max(part.reshape(block // 8, 8, K), axis=0))
+
+    largest = lax.fori_loop(0, ROWS // block, multiply, jnp.zeros((8, K), F32))
+    largest = jnp.max(jnp.max(largest, axis=0, keepdims=True), axis=1, keepdims=True)
+    power = jnp.floor(jnp.log2(jnp.maximum(largest, 1e-30)))
+    scale = jnp.exp2(TOP - 1.0 - power) * sender_factor(sender[0].astype(F32))
+    row = lax.broadcasted_iota(jnp.int32, (W_HALF, 128), 0)
+    lane = lax.broadcasted_iota(jnp.int32, (W_HALF, 128), 1)
+    free = (row >= W_OWN - W_HALF) & (lane >= K)
+
+    def code(i, carry):
+        rows = pl.ds(pl.multiple_of(i * W_OWN, W_OWN), W_OWN)
+        coded = eighth_power(two_halves(sums[rows, :]) * scale)
+        out[i, :W_HALF, :] = jnp.where(free, power, coded).astype(BF16)
+        out[i, W_HALF:, :] = gram
         return carry
 
-    lax.fori_loop(0, ROWS // block, step, 0)
+    lax.fori_loop(0, SAMPLES, code, 0)
 
 
 def w_new(got, w):
-    total = jnp.zeros(got.shape[1:], F32)
+    numer = jnp.zeros((W_HALF, 128), F32)
+    rest = jnp.zeros((got.shape[1] - W_HALF, 128), F32)
     for i in range(SAMPLES):
-        total += got[i].astype(F32)
-    numer = join(total[:W_OWN])
-    gram = unpack_gram(total[W_OWN:W_RED])
+        coded = got[i, :W_HALF, :].astype(F32)
+        power = coded[W_HALF - 1 :, 127:]
+        scale = jnp.exp2(power - (TOP - 1.0)) * (1.0 / sender_factor(i))
+        numer += eighth_root(jnp.abs(coded)) * scale
+        rest += got[i, W_HALF:, :].astype(F32)
+    numer = one_column(numer)
+    gram = unpack_gram(rest[:GRAM])
     old = w[...]
     below = jnp.dot(old, gram, precision=HIGHEST, preferred_element_type=F32) + epsilon
-    return old * numer / below, numer, total[W_RED:]
+    return old * numer / below, numer, rest[GRAM:]
 
 
 def w_update_kernel(got, w, w_out, out):
     new, _, _ = w_new(got, w)
     w_out[...] = new
     fill_w(new, out)
-
-
-def tile_pair(left, right):
-    lane = lax.broadcasted_iota(jnp.int32, (8, 128), 1)
-    return jnp.where(lane < K, left, right)
 
 
 def w_last_kernel(got, w, energy, w_out, out):
@@ -218,7 +249,8 @@
     gram = unpack_gram(rest)
     fitted = jnp.dot(rounded, gram, precision=HIGHEST, preferred_element_type=F32)
     share = jnp.sum(rounded * (fitted - 2.0 * numer))
-    pair = tile_pair(share, energy[...])
+    lane = lax.broadcasted_iota(jnp.int32, (1, 128), 1)
+    pair = jnp.where(lane < K, share, energy[...])
     for i in range(SAMPLES):
         out[i] = pair
 
@@ -230,11 +262,11 @@
         return energy + jnp.sum((values * values).reshape(W_OWN // 8, 8, COLS), axis=0)
 
     energy = lax.fori_loop(0, SAMPLES, step, jnp.zeros((8, COLS), F32))
-    out[...] = jnp.full((8, 128), jnp.sum(energy), F32)
+    out[...] = jnp.full((1, 128), jnp.sum(energy), F32)
 
 
 def last_rows_kernel(w, out):
-    rows = two_halves(w[...])
+    rows = two_halves(w[...]).astype(BF16)
     for i in range(SAMPLES):
         out[i] = rows
 
@@ -254,7 +286,7 @@
         return error + jnp.sum((difference * difference).reshape(W_OWN // 8, 8, COLS), axis=0)
 
     error = lax.fori_loop(0, SAMPLES, step, jnp.zeros((8, COLS), F32))
-    share = jnp.full((8, 128), jnp.sum(error), F32)
+    share = jnp.full((1, 128), jnp.sum(error), F32)
     for i in range(SAMPLES):
         out[i] = share
 
@@ -301,25 +333,38 @@
     )(core, got_w, telemetry)
 
 
+def w_numer(sender, got_h, telemetry, rows):
+    return pl.pallas_call(
+        w_numer_kernel,
+        out_shape=jax.ShapeDtypeStruct((SAMPLES, rows, 128), BF16),
+        in_specs=[pl.BlockSpec(memory_space=pltpu.SMEM), VMEM, VMEM],
+        out_specs=VMEM,
+        scratch_shapes=[pltpu.VMEM((ROWS, K), F32)],
+        compiler_params=LIMIT,
+        cost_estimate=PRODUCT,
+    )(sender, got_h, telemetry)
+
+
 def exchange(x, axis):
     return lax.all_to_all(x, axis, 0, 0, tiled=True)
 
 
 def sum_everywhere(shares):
     part = jnp.sum(exchange(shares, "samples"), axis=0)
-    part = exchange(jnp.broadcast_to(part[None], (CHIPS, 8, 128)), ("pairs", "core"))
+    part = exchange(jnp.broadcast_to(part[None], (CHIPS, 1, 128)), ("pairs", "core"))
     return jnp.sum(part, axis=0)
 
 
 def body(telemetry, chip_factors, sample_factors):
     core = lax.axis_index("core").reshape(1)
+    sender = lax.axis_index("samples").reshape(1)
     w, h = chip_factors.T, sample_factors.T
     (sent,) = call(start_kernel, (w,), [((SAMPLES, W_MSG, 128), BF16)])
     got_w = exchange(sent, "samples")
     (energy,) = call(
         energy_kernel,
         (telemetry,),
-        [((8, 128), F32)],
+        [((1, 128), F32)],
         pl.CostEstimate(
             flops=2 * ROWS * COLS, bytes_accessed=2 * ROWS * COLS, transcendentals=0
         ),
@@ -334,8 +379,7 @@
             h_update_kernel, (got, h), [((H_OWN, K), F32), ((CHIPS, H_OWN, 128), BF16)]
         )
         got_h = exchange(sent, ("pairs", "core"))
-        rows = W_RED + GRAM if last else W_RED
-        (sent,) = call(w_numer_kernel, (got_h, telemetry), [((SAMPLES, rows, 128), BF16)], PRODUCT)
+        sent = w_numer(sender, got_h, telemetry, W_MSG + GRAM if last else W_MSG)
         got = exchange(sent, "samples")
         if not last:
             w, sent = call(
@@ -343,7 +387,7 @@
             )
             got_w = exchange(sent, "samples")
     w, shares = call(
-        w_last_kernel, (got, w, energy), [((W_OWN, K), F32), ((SAMPLES, 8, 128), F32)]
+        w_last_kernel, (got, w, energy), [((W_OWN, K), F32), ((SAMPLES, 1, 128), F32)]
     )
     sums = sum_everywhere(shares)
     total = sums[0, K]
@@ -354,7 +398,7 @@
         (shares,) = call(
             error_kernel,
             (exchange(sent, "samples"), got_h, telemetry),
-            [((SAMPLES, 8, 128), F32)],
+            [((SAMPLES, 1, 128), F32)],
             PRODUCT,
         )
         return sum_everywhere(shares)[0, 0]

time: 232 us -> 227 us (0.978)
  blocking collectives: 123 us -> 97.4 us
  Pallas kernels: 22.9 us -> 30.3 us
  starting transfers between devices: 37.2 us -> 44.6 us
  waiting for transfers between devices: 40.3 us -> 46.2 us
    all_to_all x7 -> x6, blocking collectives: 123 us -> 97.4 us  [exchange(): return lax.all_to_all(x, axis, 0, 0, tiled=True)]
    pallas_call x0 -> x2, Pallas kernels: none -> 10.9 us  [w_numer(): pl.pallas_call(w_numer_kernel, out_shape=jax.ShapeDtypeStruct((SAMPLES, r...]
    all_to_all x3 -> x4, starting transfers between devices: 25 us -> 31.5 us  [exchange(): return lax.all_to_all(x, axis, 0, 0, tiled=True)]
    all_to_all x3 -> x4, waiting for transfers between devices: 38 us -> 43.9 us  [exchange(): return lax.all_to_all(x, axis, 0, 0, tiled=True)]
    pallas_call x10 -> x8, Pallas kernels: 15 us -> 10.2 us  [call(): pl.pallas_call(kernel, out_shape=[jax.ShapeDtypeStruct(shape, dtype) for...]
  transfers between devices with their start and end apart: 5 -> 6, of which waited for: 5 -> 6; matrix products, arithmetic and copies ran while one was open for 0% -> 0% of each run, Pallas kernels for 1% -> 1%
where the time goes in v4:
time: 227 us; the launch traced here: 226 us
  blocking collectives  97.4 us (43%)
  waiting for transfers between devices  46.2 us (20%)
  starting transfers between devices  44.6 us (20%)
  Pallas kernels  30.3 us (13%)
  between operations  4.5 us (2%)
  local copies, waits for them, and re-layouts  2.86 us (1%)
    all_to_all x6, blocking collectives, exchange(): return lax.all_to_all(x, axis, 0, 0, tiled=True)  97.4 us
    all_to_all x4, waiting for transfers between devices, exchange(): return lax.all_to_all(x, axis, 0, 0, tiled=True)  43.9 us
    all_to_all x4, starting transfers between devices, exchange(): return lax.all_to_all(x, axis, 0, 0, tiled=True)  31.5 us
    ppermute x2, starting transfers between devices, body(): taken = lax.ppermute(give, 'core', [(0, 1), (1, 0)])  13.2 us
    pallas_call x2, Pallas kernels, w_numer(): pl.pallas_call(w_numer_kernel, out_shape=jax.ShapeDtypeStruct((SAMPLES, r...  10.9 us
    pallas_call x8, Pallas kernels, call(): pl.pallas_call(kernel, out_shape=[jax.ShapeDtypeStruct(shape, dtype) for...  10.2 us
    pallas_call x2, Pallas kernels, h_numer(): pl.pallas_call(h_numer_kernel, grid=(COLS // H_WIDTH,), out_shape=[messag...  9.18 us
  transfers between devices with their start and end apart: 6, of which 6 were waited for; matrix products, arithmetic and copies ran while one was open for 0% of the time, Pallas kernels for 1%

profile of v4, /device:TPU:1, one launch (start us, length us, event | category | flops | bytes accessed | tf_op | source)
XLA Modules:
  0.0 226.0 jit_solution(17085947133732021961)
XLA Ops:
  0.6 0.0 copy-start
  0.6 0.9 copy.11
  1.6 1.3 shard_map.58
  2.9 10.2 %all-to-all-start.3 = ((bf16[16,112,128]{2,1,0:T(8,128)(2,1)}), bf16[16,112,128]{2,1,0:T(8,128)(2,1)S(1)}, u32[]{:S(2)}, u32[]{:S(2)}) async-start(bf16[16,112,128]{2,1,0:T(8,128)(2,1)} %shard_map.58), calls=%async_computation.3 | async-start | bytes 917504 | tf_op jit(solution)/shard_map/all_to_all | solution.py:349
  13.1 15.3 %all-to-all-done.3.got = bf16[16,112,128]{2,1,0:T(8,128)(2,1)S(1)} async-done(((bf16[16,112,128]{2,1,0:T(8,128)(2,1)}), bf16[16,112,128]{2,1,0:T(8,128)(2,1)S(1)}, u32[]{:S(2)}, u32[]{:S(2)}) %all-to-all-start.3) | async-done | bytes 458784 | tf_op jit(solution)/shard_map/all_to_all | solution.py:349
  28.4 4.6 %shard_map.59 = (bf16[16,64,128]{2,1,0:T(8,128)(2,1)S(1)}, bf16[16,64,128]{2,1,0:T(8,128)(2,1)S(1)}) custom-call(s32[1]{0:T(128)} %bitcast.4.core, bf16[16,112,128]{2,1,0:T(8,128)(2,1)S(1)} %all-to-all-done.3.got, bf16[2304,1024]{1,0:T(8,128)(2,1)} %tel.9), custom_call_target="tpu_custom_call" | custom-call | flops 301989888 | bytes 4718592 | tf_op jit(solution)/shard_map/pallas_call | solution.py:316
  33.0 4.2 %collective-permute-start = (bf16[16,64,128]{2,1,0:T(8,128)(2,1)S(1)}, bf16[16,64,128]{2,1,0:T(8,128)(2,1)S(1)}, u32[]{:S(2)}, u32[]{:S(2)}) collective-permute-start(bf16[16,64,128]{2,1,0:T(8,128)(2,1)S(1)} %get-tuple-element.29), channel_id=1, source_target_pairs={{0,16},{16,0},{1,17},{17,1},{2,18},{18,2},{3,19},{19,3},{4,20},{20... | collective-permute-start | bytes 786440 | tf_op jit(solution)/shard_map/ppermute | solution.py:375
  37.3 1.1 collective-permute-done.got
  38.4 0.3 shard_map.60
  38.7 18.9 %all_to_all.65.got = bf16[16,64,128]{2,1,0:T(8,128)(2,1)S(1)} all-to-all(bf16[16,64,128]{2,1,0:T(8,128)(2,1)S(1)} %shard_map.60), channel_id=1, replica_groups=mesh['pairs'=16,'core'=2,'samples'=16] {'pairs'}, dimensions={0} | all-to-all | bytes 524288 | tf_op jit(solution)/shard_map/all_to_all | solution.py:349
  57.6 0.0 copy-done
  57.6 1.4 shard_map.61
  59.0 6.7 %all-to-all-start.5 = ((bf16[32,32,128]{2,1,0:T(8,128)(2,1)}), bf16[32,32,128]{2,1,0:T(8,128)(2,1)S(1)}, u32[]{:S(2)}, u32[]{:S(2)}) async-start(bf16[32,32,128]{2,1,0:T(8,128)(2,1)} %get-tuple-element.30), calls=%async_computation.5 | async-start | bytes 524288 | tf_op jit(solution)/shard_map/all_to_all | solution.py:349
  65.7 11.1 %all-to-all-done.5.got = bf16[32,32,128]{2,1,0:T(8,128)(2,1)S(1)} async-done(((bf16[32,32,128]{2,1,0:T(8,128)(2,1)}), bf16[32,32,128]{2,1,0:T(8,128)(2,1)S(1)}, u32[]{:S(2)}, u32[]{:S(2)}) %all-to-all-start.5) | async-done | bytes 262176 | tf_op jit(solution)/shard_map/all_to_all | solution.py:349
  76.7 0.0 slice-start
  76.7 6.3 %shard_map.62 = bf16[16,112,128]{2,1,0:T(8,128)(2,1)S(1)} custom-call(s32[1]{0:T(128)} %bitcast.3.sender, bf16[32,32,128]{2,1,0:T(8,128)(2,1)S(1)} %all-to-all-done.5.got, bf16[2304,1024]{1,0:T(8,128)(2,1)} %tel.9), custom_call_target="tpu_custom_call" | custom-call | flops 301989888 | bytes 4718592 | tf_op jit(solution)/shard_map/pallas_call | solution.py:337
  83.0 15.0 %all_to_all.66.got = bf16[16,112,128]{2,1,0:T(8,128)(2,1)S(1)} all-to-all(bf16[16,112,128]{2,1,0:T(8,128)(2,1)S(1)} %shard_map.62), channel_id=1, replica_groups=mesh['pairs'=16,'core'=2,'samples'=16] {'samples'}, dimensions={0} | all-to-all | bytes 917504 | tf_op jit(solution)/shard_map/all_to_all | solution.py:349
  98.0 1.5 shard_map.63
  99.6 0.0 slice-start.1
  99.6 17.4 %all_to_all.67.got = bf16[16,112,128]{2,1,0:T(8,128)(2,1)S(1)} all-to-all(bf16[16,112,128]{2,1,0:T(8,128)(2,1)S(1)} %get-tuple-element.31), channel_id=1, replica_groups=mesh['pairs'=16,'core'=2,'samples'=16] {'samples'}, dimensions={0} | all-to-all | bytes 917504 | tf_op jit(solution)/shard_map/all_to_all | solution.py:349
  117.0 4.6 %shard_map.64 = (bf16[16,64,128]{2,1,0:T(8,128)(2,1)S(1)}, bf16[16,64,128]{2,1,0:T(8,128)(2,1)S(1)}) custom-call(s32[1]{0:T(128)} %bitcast.4.core, bf16[16,112,128]{2,1,0:T(8,128)(2,1)S(1)} %all_to_all.67.got, bf16[2304,1024]{1,0:T(8,128)(2,1)} %tel.9), custom_call_target="tpu_custom_call" | custom-call | flops 301989888 | bytes 4718592 | tf_op jit(solution)/shard_map/pallas_call | solution.py:316
  121.6 8.9 %collective-permute-start.1 = (bf16[16,64,128]{2,1,0:T(8,128)(2,1)S(1)}, bf16[16,64,128]{2,1,0:T(8,128)(2,1)S(1)}, u32[]{:S(2)}, u32[]{:S(2)}) collective-permute-start(bf16[16,64,128]{2,1,0:T(8,128)(2,1)S(1)} %get-tuple-element.33), channel_id=1, source_target_pairs={{0,16},{16,0},{1,17},{17,1},{2,18},{18,2},{3,19},{19,3},{4,20},{20... | collective-permute-start | bytes 786440 | tf_op jit(solution)/shard_map/ppermute | solution.py:375
  130.5 1.1 collective-permute-done.1.got
  131.7 0.3 shard_map.65
  131.9 14.1 %all_to_all.68.got = bf16[16,64,128]{2,1,0:T(8,128)(2,1)S(1)} all-to-all(bf16[16,64,128]{2,1,0:T(8,128)(2,1)S(1)} %shard_map.65), channel_id=1, replica_groups=mesh['pairs'=16,'core'=2,'samples'=16] {'pairs'}, dimensions={0} | all-to-all | bytes 524288 | tf_op jit(solution)/shard_map/all_to_all | solution.py:349
  146.0 1.2 shard_map.66
  147.3 17.6 %all_to_all.69.got = bf16[32,32,128]{2,1,0:T(8,128)(2,1)S(1)} all-to-all(bf16[32,32,128]{2,1,0:T(8,128)(2,1)S(1)} %get-tuple-element.35), channel_id=1, replica_groups=mesh['pairs'=16,'core'=2,'samples'=16] {'pairs','core'}, dimensions={0} | all-to-all | bytes 524288 | tf_op jit(solution)/shard_map/all_to_all | solution.py:349
  164.9 0.0 slice-done
  164.9 0.0 slice-done.1
  164.9 4.6 %shard_map.67 = bf16[16,144,128]{2,1,0:T(8,128)(2,1)} custom-call(s32[1]{0:T(128)} %bitcast.3.sender, bf16[32,32,128]{2,1,0:T(8,128)(2,1)S(1)} %all_to_all.69.got, bf16[2304,1024]{1,0:T(8,128)(2,1)S(1)} %bitcast.18), custom_call_target="tpu_custom_call" | custom-call | flops 301989888 | bytes 4718592 | tf_op jit(solution)/shard_map/pallas_call | solution.py:337
  169.5 4.0 %all-to-all-start.10 = ((bf16[16,144,128]{2,1,0:T(8,128)(2,1)}), bf16[16,144,128]{2,1,0:T(8,128)(2,1)S(1)}, u32[]{:S(2)}, u32[]{:S(2)}) async-start(bf16[16,144,128]{2,1,0:T(8,128)(2,1)} %shard_map.67), calls=%async_computation.10 | async-start | bytes 1179648 | tf_op jit(solution)/shard_map/all_to_all | solution.py:349
  173.5 2.8 %shard_map.68.energy = f32[1,128]{1,0:T(1,128)S(1)} custom-call(bf16[2304,1024]{1,0:T(8,128)(2,1)} %tel.9), custom_call_target="tpu_custom_call" | custom-call | flops 4718592 | bytes 4718592 | tf_op jit(solution)/shard_map/pallas_call | solution.py:302
  176.3 10.4 %all-to-all-done.10.got = bf16[16,144,128]{2,1,0:T(8,128)(2,1)S(1)} async-done(((bf16[16,144,128]{2,1,0:T(8,128)(2,1)}), bf16[16,144,128]{2,1,0:T(8,128)(2,1)S(1)}, u32[]{:S(2)}, u32[]{:S(2)}) %all-to-all-start.10) | async-done | bytes 589856 | tf_op jit(solution)/shard_map/all_to_all | solution.py:349
  186.7 1.5 shard_map.69
  188.2 14.4 %all_to_all.70 = f32[16,1,128]{2,1,0:T(1,128)S(1)} all-to-all(f32[16,1,128]{2,1,0:T(1,128)S(1)} %get-tuple-element.39), channel_id=1, replica_groups=mesh['pairs'=16,'core'=2,'samples'=16] {'samples'}, dimensions={0} | all-to-all | bytes 16384 | tf_op jit(solution)/shard_map/all_to_all | solution.py:349
  202.6 0.6 broadcast_in_dim.4
  203.2 10.6 %all-to-all-start.12 = ((f32[32,1,128]{2,1,0:T(1,128)}), f32[32,1,128]{2,1,0:T(1,128)S(1)}, u32[]{:S(2)}, u32[]{:S(2)}) async-start(f32[32,1,128]{2,1,0:T(1,128)} %broadcast_in_dim.4), calls=%async_computation.12 | async-start | bytes 32768 | tf_op jit(solution)/shard_map/all_to_all | solution.py:349
  213.8 0.7 copy.13
  214.5 7.1 %all-to-all-done.12 = f32[32,1,128]{2,1,0:T(1,128)S(1)} async-done(((f32[32,1,128]{2,1,0:T(1,128)}), f32[32,1,128]{2,1,0:T(1,128)S(1)}, u32[]{:S(2)}, u32[]{:S(2)}) %all-to-all-start.12) | async-done | bytes 16416 | tf_op jit(solution)/shard_map/all_to_all | solution.py:349
  221.7 0.6 fusion
  (4 shorter events, 0.1 us)
Async XLA Ops:
  0.6 57.0 %copy-start = (f32[64,32]{0,1:T(8,128)S(1)}, f32[64,32]{0,1:T(8,128)}, u32[]{:S(2)}) copy-start(f32[64,32]{0,1:T(8,128)} %param.7) | copy-start | bytes 24580
  2.9 25.6 %all-to-all-start.3 = ((bf16[16,112,128]{2,1,0:T(8,128)(2,1)}), bf16[16,112,128]{2,1,0:T(8,128)(2,1)S(1)}, u32[]{:S(2)}, u32[]{:S(2)}) async-start(bf16[16,112,128]{2,1,0:T(8,128)(2,1)} %shard_map.58), calls=%async_computation.3 | async-start | bytes 917504 | tf_op jit(solution)/shard_map/all_to_all | solution.py:349
  33.0 5.4 %collective-permute-start = (bf16[16,64,128]{2,1,0:T(8,128)(2,1)S(1)}, bf16[16,64,128]{2,1,0:T(8,128)(2,1)S(1)}, u32[]{:S(2)}, u32[]{:S(2)}) collective-permute-start(bf16[16,64,128]{2,1,0:T(8,128)(2,1)S(1)} %get-tuple-element.29), channel_id=1, source_target_pairs={{0,16},{16,0},{1,17},{17,1},{2,18},{18,2},{3,19},{19,3},{4,20},{20... | collective-permute-start | bytes 786440 | tf_op jit(solution)/shard_map/ppermute | solution.py:375
  59.0 17.8 %all-to-all-start.5 = ((bf16[32,32,128]{2,1,0:T(8,128)(2,1)}), bf16[32,32,128]{2,1,0:T(8,128)(2,1)S(1)}, u32[]{:S(2)}, u32[]{:S(2)}) async-start(bf16[32,32,128]{2,1,0:T(8,128)(2,1)} %get-tuple-element.30), calls=%async_computation.5 | async-start | bytes 524288 | tf_op jit(solution)/shard_map/all_to_all | solution.py:349
  76.7 88.1 %slice-start = ((s8[4718592]{0:T(1024)(128)(4,1)}), s8[4194304]{0:T(1024)(128)(4,1)S(1)}, s32[]{:S(2)}) async-start(s8[4718592]{0:T(1024)(128)(4,1)} %bitcast.17), calls=%async_computation.13 | async-start | bytes 8388608
  99.6 65.3 %slice-start.1 = ((s8[4718592]{0:T(1024)(128)(4,1)}), s8[524288]{0:T(1024)(128)(4,1)S(1)}, s32[]{:S(2)}) async-start(s8[4718592]{0:T(1024)(128)(4,1)} %bitcast.17), calls=%async_computation.14 | async-start | bytes 1048576
  121.6 10.1 %collective-permute-start.1 = (bf16[16,64,128]{2,1,0:T(8,128)(2,1)S(1)}, bf16[16,64,128]{2,1,0:T(8,128)(2,1)S(1)}, u32[]{:S(2)}, u32[]{:S(2)}) collective-permute-start(bf16[16,64,128]{2,1,0:T(8,128)(2,1)S(1)} %get-tuple-element.33), channel_id=1, source_target_pairs={{0,16},{16,0},{1,17},{17,1},{2,18},{18,2},{3,19},{19,3},{4,20},{20... | collective-permute-start | bytes 786440 | tf_op jit(solution)/shard_map/ppermute | solution.py:375
  169.5 17.2 %all-to-all-start.10 = ((bf16[16,144,128]{2,1,0:T(8,128)(2,1)}), bf16[16,144,128]{2,1,0:T(8,128)(2,1)S(1)}, u32[]{:S(2)}, u32[]{:S(2)}) async-start(bf16[16,144,128]{2,1,0:T(8,128)(2,1)} %shard_map.67), calls=%async_computation.10 | async-start | bytes 1179648 | tf_op jit(solution)/shard_map/all_to_all | solution.py:349
  203.2 18.4 %all-to-all-start.12 = ((f32[32,1,128]{2,1,0:T(1,128)}), f32[32,1,128]{2,1,0:T(1,128)S(1)}, u32[]{:S(2)}, u32[]{:S(2)}) async-start(f32[32,1,128]{2,1,0:T(1,128)} %broadcast_in_dim.4), calls=%async_computation.12 | async-start | bytes 32768 | tf_op jit(solution)/shard_map/all_to_all | solution.py:349

commit v5 on v4

--- a/solution.py
+++ b/solution.py
@@ -108,21 +108,48 @@
     return jnp.concatenate([both[:, :K], both[: W_OWN - W_HALF, K:]], axis=0)
 
 
-TOP = 14.0
+TOP = 6.0
+BLOCK = 16
+LEFT = W_HALF // BLOCK
 
 
 def sender_factor(i):
     return 1.0 + i / 32.0
 
 
-def eighth_power(x):
-    x = x * x
-    x = x * x
-    return x * x
-
-
-def eighth_root(x):
-    return jnp.sqrt(jnp.sqrt(jnp.sqrt(x)))
+def encode(sums, factor):
+    blocks = [sums[j * BLOCK : (j + 1) * BLOCK] for j in range(W_OWN // BLOCK)]
+    largest = jnp.concatenate(
+        [jnp.max(x, axis=0, keepdims=True) for x in blocks]
+        + [jnp.zeros((BLOCK - len(blocks), K), F32)],
+        axis=0,
+    )
+    largest = jnp.max(largest, axis=1, keepdims=True)
+    power = jnp.floor(jnp.log2(jnp.maximum(largest, 1e-30)))
+    scale = jnp.exp2(TOP - power) * factor
+    coded = []
+    for j, x in enumerate(blocks):
+        x = x * scale[j : j + 1]
+        x = x * x
+        x = x * x
+        x = x * x
+        coded.append(x * x)
+    coded.append(jnp.broadcast_to(power, (BLOCK, K)))
+    return jnp.concatenate(
+        [jnp.concatenate(coded[:LEFT], axis=0), jnp.concatenate(coded[LEFT:], axis=0)], axis=1
+    ).astype(BF16)
+
+
+def decode(message, factor):
+    lane = lax.broadcasted_iota(jnp.int32, (BLOCK, 128), 1)
+    message = message.astype(F32)
+    scale = jnp.exp2(message[W_HALF - BLOCK :, 127:] - TOP) * (1.0 / factor)
+    roots = jnp.sqrt(jnp.sqrt(jnp.sqrt(jnp.sqrt(jnp.abs(message)))))
+    return [
+        roots[j * BLOCK : (j + 1) * BLOCK]
+        * jnp.where(lane < K, scale[j : j + 1], scale[LEFT + j : LEFT + j + 1])
+        for j in range(LEFT)
+    ]
 
 
 def fill_w(w, out):
@@ -187,49 +214,36 @@
         out[i] = halves
 
 
-def w_numer_kernel(sender, got, tel, out, sums):
+def w_numer_kernel(sender, got, tel, out):
     halves = got[...].reshape(COLS, 128)
     four = products(halves)
     gram = pack_gram(quarters(four))
     if out.shape[1] > W_MSG:
         gram = jnp.concatenate([gram, pack_gram(four[:K, :K])], axis=0)
     high = halves[:, :K]
-    block = 4 * W_OWN
-
-    def multiply(b, largest):
+    per = 4
+    block = per * W_OWN
+    factor = sender_factor(sender[0].astype(F32))
+
+    def step(b, carry):
         rows = pl.ds(pl.multiple_of(b * block, block), block)
         part = jnp.dot(tel[rows, :], high, preferred_element_type=F32)
-        sums[rows, :] = part
-        return jnp.maximum(largest, jnp.max(part.reshape(block // 8, 8, K), axis=0))
-
-    largest = lax.fori_loop(0, ROWS // block, multiply, jnp.zeros((8, K), F32))
-    largest = jnp.max(jnp.max(largest, axis=0, keepdims=True), axis=1, keepdims=True)
-    power = jnp.floor(jnp.log2(jnp.maximum(largest, 1e-30)))
-    scale = jnp.exp2(TOP - 1.0 - power) * sender_factor(sender[0].astype(F32))
-    row = lax.broadcasted_iota(jnp.int32, (W_HALF, 128), 0)
-    lane = lax.broadcasted_iota(jnp.int32, (W_HALF, 128), 1)
-    free = (row >= W_OWN - W_HALF) & (lane >= K)
-
-    def code(i, carry):
-        rows = pl.ds(pl.multiple_of(i * W_OWN, W_OWN), W_OWN)
-        coded = eighth_power(two_halves(sums[rows, :]) * scale)
-        out[i, :W_HALF, :] = jnp.where(free, power, coded).astype(BF16)
-        out[i, W_HALF:, :] = gram
+        for q in range(per):
+            out[b * per + q, :W_HALF, :] = encode(part[q * W_OWN : (q + 1) * W_OWN], factor)
+            out[b * per + q, W_HALF:, :] = gram
         return carry
 
-    lax.fori_loop(0, SAMPLES, code, 0)
+    lax.fori_loop(0, ROWS // block, step, 0)
 
 
 def w_new(got, w):
-    numer = jnp.zeros((W_HALF, 128), F32)
+    blocks = [jnp.zeros((BLOCK, 128), F32)] * LEFT
     rest = jnp.zeros((got.shape[1] - W_HALF, 128), F32)
     for i in range(SAMPLES):
-        coded = got[i, :W_HALF, :].astype(F32)
-        power = coded[W_HALF - 1 :, 127:]
-        scale = jnp.exp2(power - (TOP - 1.0)) * (1.0 / sender_factor(i))
-        numer += eighth_root(jnp.abs(coded)) * scale
+        terms = decode(got[i, :W_HALF, :], sender_factor(i))
+        blocks = [total + term for total, term in zip(blocks, terms)]
         rest += got[i, W_HALF:, :].astype(F32)
-    numer = one_column(numer)
+    numer = one_column(jnp.concatenate(blocks, axis=0))
     gram = unpack_gram(rest[:GRAM])
     old = w[...]
     below = jnp.dot(old, gram, precision=HIGHEST, preferred_element_type=F32) + epsilon
@@ -255,9 +269,10 @@
         out[i] = pair
 
 
-def energy_kernel(tel, out):
+def load_kernel(tel, tile, out):
     def step(i, energy):
         rows = pl.ds(pl.multiple_of(i * W_OWN, W_OWN), W_OWN)
+        tile[rows, :] = tel[rows, :]
         values = tel[rows, :].astype(F32)
         return energy + jnp.sum((values * values).reshape(W_OWN // 8, 8, COLS), axis=0)
 
@@ -296,6 +311,7 @@
 PRODUCT = pl.CostEstimate(
     flops=2 * K * ROWS * COLS, bytes_accessed=2 * ROWS * COLS, transcendentals=0
 )
+LOAD = pl.CostEstimate(flops=2 * ROWS * COLS, bytes_accessed=4 * ROWS * COLS, transcendentals=0)
 
 
 def call(kernel, inputs, outs, cost=None):
@@ -339,7 +355,6 @@
         out_shape=jax.ShapeDtypeStruct((SAMPLES, rows, 128), BF16),
         in_specs=[pl.BlockSpec(memory_space=pltpu.SMEM), VMEM, VMEM],
         out_specs=VMEM,
-        scratch_shapes=[pltpu.VMEM((ROWS, K), F32)],
         compiler_params=LIMIT,
         cost_estimate=PRODUCT,
     )(sender, got_h, telemetry)
@@ -361,17 +376,12 @@
     w, h = chip_factors.T, sample_factors.T
     (sent,) = call(start_kernel, (w,), [((SAMPLES, W_MSG, 128), BF16)])
     got_w = exchange(sent, "samples")
-    (energy,) = call(
-        energy_kernel,
-        (telemetry,),
-        [((1, 128), F32)],
-        pl.CostEstimate(
-            flops=2 * ROWS * COLS, bytes_accessed=2 * ROWS * COLS, transcendentals=0
-        ),
+    tile, energy = call(
+        load_kernel, (telemetry,), [((ROWS, COLS), BF16), ((1, 128), F32)], LOAD
     )
     for sweep in range(ITERS):
         last = sweep == ITERS - 1
-        keep, give = h_numer(core, got_w, telemetry)
+        keep, give = h_numer(core, got_w, tile)
         taken = lax.ppermute(give, "core", [(0, 1), (1, 0)])
         (sent,) = call(pair_kernel, (keep, taken), [((PAIRS, H_RED, 128), BF16)])
         got = exchange(sent, "pairs")
@@ -379,7 +389,7 @@
             h_update_kernel, (got, h), [((H_OWN, K), F32), ((CHIPS, H_OWN, 128), BF16)]
         )
         got_h = exchange(sent, ("pairs", "core"))
-        sent = w_numer(sender, got_h, telemetry, W_MSG + GRAM if last else W_MSG)
+        sent = w_numer(sender, got_h, tile, W_MSG + GRAM if last else W_MSG)
         got = exchange(sent, "samples")
         if not last:
             w, sent = call(
@@ -393,11 +403,11 @@
     total = sums[0, K]
     expanded = sums[0, 0] + total
 
-    def direct(w, got_h, telemetry):
+    def direct(w, got_h, tile):
         (sent,) = call(last_rows_kernel, (w,), [((SAMPLES, W_HALF, 128), BF16)])
         (shares,) = call(
             error_kernel,
-            (exchange(sent, "samples"), got_h, telemetry),
+            (exchange(sent, "samples"), got_h, tile),
             [((SAMPLES, 1, 128), F32)],
             PRODUCT,
         )
@@ -409,7 +419,7 @@
         lambda *operands: expanded,
         w,
         got_h,
-        telemetry,
+        tile,
     )
     return w.T, h.T, jnp.sqrt(fit_error / total)
 

time: 227 us -> 225 us (level)
  blocking collectives: 97.4 us -> 115 us
  waiting for transfers between devices: 46.2 us -> 30.9 us
  starting transfers between devices: 44.6 us -> 40.3 us
  local copies, waits for them, and re-layouts: 2.86 us -> 5.2 us
    all_to_all x6 -> x7, blocking collectives: 97.4 us -> 115 us  [exchange(): return lax.all_to_all(x, axis, 0, 0, tiled=True)]
    all_to_all x4 -> x3, waiting for transfers between devices: 43.9 us -> 28.6 us  [exchange(): return lax.all_to_all(x, axis, 0, 0, tiled=True)]
    all_to_all x4 -> x3, starting transfers between devices: 31.5 us -> 27.1 us  [exchange(): return lax.all_to_all(x, axis, 0, 0, tiled=True)]
    unnamed x8 -> x10, local copies, waits for them, and re-layouts: 1.67 us -> 3.99 us
  transfers between devices with their start and end apart: 6 -> 5, of which waited for: 6 -> 5; matrix products, arithmetic and copies ran while one was open for 0% -> 0% of each run, Pallas kernels for 1% -> 1%
where the time goes in v5:
time: 225 us; the launch traced here: 224 us
  blocking collectives  115 us (51%)
  starting transfers between devices  40.3 us (18%)
  waiting for transfers between devices  30.9 us (14%)
  Pallas kernels  28.2 us (13%)
  local copies, waits for them, and re-layouts  5.2 us (2%)
  between operations  4.6 us (2%)
    all_to_all x7, blocking collectives, exchange(): return lax.all_to_all(x, axis, 0, 0, tiled=True)  115 us
    all_to_all x3, waiting for transfers between devices, exchange(): return lax.all_to_all(x, axis, 0, 0, tiled=True)  28.6 us
    all_to_all x3, starting transfers between devices, exchange(): return lax.all_to_all(x, axis, 0, 0, tiled=True)  27.1 us
    ppermute x2, starting transfers between devices, body(): taken = lax.ppermute(give, 'core', [(0, 1), (1, 0)])  13.2 us
    pallas_call x8, Pallas kernels, call(): pl.pallas_call(kernel, out_shape=[jax.ShapeDtypeStruct(shape, dtype) for...  10.3 us
    pallas_call x2, Pallas kernels, h_numer(): pl.pallas_call(h_numer_kernel, grid=(COLS // H_WIDTH,), out_shape=[messag...  9.18 us
    pallas_call x2, Pallas kernels, w_numer(): pl.pallas_call(w_numer_kernel, out_shape=jax.ShapeDtypeStruct((SAMPLES, r...  8.68 us
  transfers between devices with their start and end apart: 5, of which 5 were waited for; matrix products, arithmetic and copies ran while one was open for 0% of the time, Pallas kernels for 1%

profile of v5, /device:TPU:1, one launch (start us, length us, event | category | flops | bytes accessed | tf_op | source)
XLA Modules:
  0.0 223.9 jit_solution(16249377754774419379)
XLA Ops:
  0.6 0.9 copy.11
  1.6 1.3 shard_map.58
  2.8 10.2 %all-to-all-start.3 = ((bf16[16,112,128]{2,1,0:T(8,128)(2,1)}), bf16[16,112,128]{2,1,0:T(8,128)(2,1)S(1)}, u32[]{:S(2)}, u32[]{:S(2)}) async-start(bf16[16,112,128]{2,1,0:T(8,128)(2,1)} %shard_map.58), calls=%async_computation.3 | async-start | bytes 917504 | tf_op jit(solution)/shard_map/all_to_all | solution.py:364
  13.1 0.0 copy-start
  13.1 2.3 %copy-done = bf16[2304,1024]{1,0:T(8,128)(2,1)S(1)} copy-done((bf16[2304,1024]{1,0:T(8,128)(2,1)S(1)}, bf16[2304,1024]{1,0:T(8,128)(2,1)}, u32[]{:S(2)}) %copy-start) | copy-done | bytes 4718616
  15.4 0.0 copy-start.1
  15.4 2.6 %shard_map.59 = (bf16[2304,1024]{1,0:T(8,128)(2,1)}, f32[1,128]{1,0:T(1,128)S(1)}) custom-call(bf16[2304,1024]{1,0:T(8,128)(2,1)S(1)} %copy-done), custom_call_target="tpu_custom_call" | custom-call | flops 4718592 | bytes 9437184 | tf_op jit(solution)/shard_map/pallas_call | solution.py:318
  18.0 10.4 %all-to-all-done.3.got = bf16[16,112,128]{2,1,0:T(8,128)(2,1)S(1)} async-done(((bf16[16,112,128]{2,1,0:T(8,128)(2,1)}), bf16[16,112,128]{2,1,0:T(8,128)(2,1)S(1)}, u32[]{:S(2)}, u32[]{:S(2)}) %all-to-all-start.3) | async-done | bytes 458784 | tf_op jit(solution)/shard_map/all_to_all | solution.py:364
  28.4 4.6 %shard_map.60 = (bf16[16,64,128]{2,1,0:T(8,128)(2,1)S(1)}, bf16[16,64,128]{2,1,0:T(8,128)(2,1)S(1)}) custom-call(s32[1]{0:T(128)} %bitcast.4.core, bf16[16,112,128]{2,1,0:T(8,128)(2,1)S(1)} %all-to-all-done.3.got, bf16[2304,1024]{1,0:T(8,128)(2,1)} %get-tuple-element.30.tel), custom_call_target="tpu_custom_call" | custom-call | flops 301989888 | bytes 4718592 | tf_op jit(solution)/shard_map/pallas_call | solution.py:332
  33.0 4.2 %collective-permute-start = (bf16[16,64,128]{2,1,0:T(8,128)(2,1)S(1)}, bf16[16,64,128]{2,1,0:T(8,128)(2,1)S(1)}, u32[]{:S(2)}, u32[]{:S(2)}) collective-permute-start(bf16[16,64,128]{2,1,0:T(8,128)(2,1)S(1)} %get-tuple-element.32), channel_id=1, source_target_pairs={{0,16},{16,0},{1,17},{17,1},{2,18},{18,2},{3,19},{19,3},{4,20},{20... | collective-permute-start | bytes 786440 | tf_op jit(solution)/shard_map/ppermute | solution.py:385
  37.2 1.1 collective-permute-done.got
  38.4 0.3 shard_map.61
  38.6 18.9 %all_to_all.65.got = bf16[16,64,128]{2,1,0:T(8,128)(2,1)S(1)} all-to-all(bf16[16,64,128]{2,1,0:T(8,128)(2,1)S(1)} %shard_map.61), channel_id=1, replica_groups=mesh['pairs'=16,'core'=2,'samples'=16] {'pairs'}, dimensions={0} | all-to-all | bytes 524288 | tf_op jit(solution)/shard_map/all_to_all | solution.py:364
  57.5 0.0 copy-done.1
  57.5 1.4 shard_map.62
  59.0 6.7 %all-to-all-start.5 = ((bf16[32,32,128]{2,1,0:T(8,128)(2,1)}), bf16[32,32,128]{2,1,0:T(8,128)(2,1)S(1)}, u32[]{:S(2)}, u32[]{:S(2)}) async-start(bf16[32,32,128]{2,1,0:T(8,128)(2,1)} %get-tuple-element.33), calls=%async_computation.5 | async-start | bytes 524288 | tf_op jit(solution)/shard_map/all_to_all | solution.py:364
  65.6 11.1 %all-to-all-done.5.got = bf16[32,32,128]{2,1,0:T(8,128)(2,1)S(1)} async-done(((bf16[32,32,128]{2,1,0:T(8,128)(2,1)}), bf16[32,32,128]{2,1,0:T(8,128)(2,1)S(1)}, u32[]{:S(2)}, u32[]{:S(2)}) %all-to-all-start.5) | async-done | bytes 262176 | tf_op jit(solution)/shard_map/all_to_all | solution.py:364
  76.7 0.0 slice-start
  76.7 5.6 %shard_map.63 = bf16[16,112,128]{2,1,0:T(8,128)(2,1)S(1)} custom-call(s32[1]{0:T(128)} %bitcast.3.sender, bf16[32,32,128]{2,1,0:T(8,128)(2,1)S(1)} %all-to-all-done.5.got, bf16[2304,1024]{1,0:T(8,128)(2,1)} %get-tuple-element.30.tel), custom_call_target="tpu_custom_call" | custom-call | flops 301989888 | bytes 4718592 | tf_op jit(solution)/shard_map/pallas_call | solution.py:353
  82.3 15.0 %all_to_all.66.got = bf16[16,112,128]{2,1,0:T(8,128)(2,1)S(1)} all-to-all(bf16[16,112,128]{2,1,0:T(8,128)(2,1)S(1)} %shard_map.63), channel_id=1, replica_groups=mesh['pairs'=16,'core'=2,'samples'=16] {'samples'}, dimensions={0} | all-to-all | bytes 917504 | tf_op jit(solution)/shard_map/all_to_all | solution.py:364
  97.3 1.7 shard_map.64
  99.0 0.0 slice-start.1
  99.0 17.4 %all_to_all.67.got = bf16[16,112,128]{2,1,0:T(8,128)(2,1)S(1)} all-to-all(bf16[16,112,128]{2,1,0:T(8,128)(2,1)S(1)} %get-tuple-element.34), channel_id=1, replica_groups=mesh['pairs'=16,'core'=2,'samples'=16] {'samples'}, dimensions={0} | all-to-all | bytes 917504 | tf_op jit(solution)/shard_map/all_to_all | solution.py:364
  116.4 4.6 %shard_map.65 = (bf16[16,64,128]{2,1,0:T(8,128)(2,1)S(1)}, bf16[16,64,128]{2,1,0:T(8,128)(2,1)S(1)}) custom-call(s32[1]{0:T(128)} %bitcast.4.core, bf16[16,112,128]{2,1,0:T(8,128)(2,1)S(1)} %all_to_all.67.got, bf16[2304,1024]{1,0:T(8,128)(2,1)} %get-tuple-element.30.tel), custom_call_target="tpu_custom_call" | custom-call | flops 301989888 | bytes 4718592 | tf_op jit(solution)/shard_map/pallas_call | solution.py:332
  121.0 9.0 %collective-permute-start.1 = (bf16[16,64,128]{2,1,0:T(8,128)(2,1)S(1)}, bf16[16,64,128]{2,1,0:T(8,128)(2,1)S(1)}, u32[]{:S(2)}, u32[]{:S(2)}) collective-permute-start(bf16[16,64,128]{2,1,0:T(8,128)(2,1)S(1)} %get-tuple-element.36), channel_id=1, source_target_pairs={{0,16},{16,0},{1,17},{17,1},{2,18},{18,2},{3,19},{19,3},{4,20},{20... | collective-permute-start | bytes 786440 | tf_op jit(solution)/shard_map/ppermute | solution.py:385
  130.0 1.1 collective-permute-done.1.got
  131.1 0.3 shard_map.66
  131.4 14.0 %all_to_all.68.got = bf16[16,64,128]{2,1,0:T(8,128)(2,1)S(1)} all-to-all(bf16[16,64,128]{2,1,0:T(8,128)(2,1)S(1)} %shard_map.66), channel_id=1, replica_groups=mesh['pairs'=16,'core'=2,'samples'=16] {'pairs'}, dimensions={0} | all-to-all | bytes 524288 | tf_op jit(solution)/shard_map/all_to_all | solution.py:364
  145.4 1.2 shard_map.67
  146.6 17.6 %all_to_all.69.got = bf16[32,32,128]{2,1,0:T(8,128)(2,1)S(1)} all-to-all(bf16[32,32,128]{2,1,0:T(8,128)(2,1)S(1)} %get-tuple-element.38), channel_id=1, replica_groups=mesh['pairs'=16,'core'=2,'samples'=16] {'pairs','core'}, dimensions={0} | all-to-all | bytes 524288 | tf_op jit(solution)/shard_map/all_to_all | solution.py:364
  164.3 0.0 slice-done
  164.3 0.0 slice-done.1
  164.3 3.1 %shard_map.68 = bf16[16,144,128]{2,1,0:T(8,128)(2,1)S(1)} custom-call(s32[1]{0:T(128)} %bitcast.3.sender, bf16[32,32,128]{2,1,0:T(8,128)(2,1)S(1)} %all_to_all.69.got, bf16[2304,1024]{1,0:T(8,128)(2,1)S(1)} %bitcast.18), custom_call_target="tpu_custom_call" | custom-call | flops 301989888 | bytes 4718592 | tf_op jit(solution)/shard_map/pallas_call | solution.py:353
  167.4 19.7 %all_to_all.70.got = bf16[16,144,128]{2,1,0:T(8,128)(2,1)S(1)} all-to-all(bf16[16,144,128]{2,1,0:T(8,128)(2,1)S(1)} %shard_map.68), channel_id=1, replica_groups=mesh['pairs'=16,'core'=2,'samples'=16] {'samples'}, dimensions={0} | all-to-all | bytes 1179648 | tf_op jit(solution)/shard_map/all_to_all | solution.py:364
  187.1 1.6 shard_map.69
  188.7 12.0 %all_to_all.71 = f32[16,1,128]{2,1,0:T(1,128)S(1)} all-to-all(f32[16,1,128]{2,1,0:T(1,128)S(1)} %get-tuple-element.43), channel_id=1, replica_groups=mesh['pairs'=16,'core'=2,'samples'=16] {'samples'}, dimensions={0} | all-to-all | bytes 16384 | tf_op jit(solution)/shard_map/all_to_all | solution.py:364
  200.7 0.6 broadcast_in_dim.4
  201.4 10.3 %all-to-all-start.12 = ((f32[32,1,128]{2,1,0:T(1,128)}), f32[32,1,128]{2,1,0:T(1,128)S(1)}, u32[]{:S(2)}, u32[]{:S(2)}) async-start(f32[32,1,128]{2,1,0:T(1,128)} %broadcast_in_dim.4), calls=%async_computation.12 | async-start | bytes 32768 | tf_op jit(solution)/shard_map/all_to_all | solution.py:364
  211.6 0.7 copy.13
  212.3 7.1 %all-to-all-done.12 = f32[32,1,128]{2,1,0:T(1,128)S(1)} async-done(((f32[32,1,128]{2,1,0:T(1,128)}), f32[32,1,128]{2,1,0:T(1,128)S(1)}, u32[]{:S(2)}, u32[]{:S(2)}) %all-to-all-start.12) | async-done | bytes 16416 | tf_op jit(solution)/shard_map/all_to_all | solution.py:364
  219.4 0.6 fusion
  (4 shorter events, 0.1 us)
Async XLA Ops:
  2.8 25.6 %all-to-all-start.3 = ((bf16[16,112,128]{2,1,0:T(8,128)(2,1)}), bf16[16,112,128]{2,1,0:T(8,128)(2,1)S(1)}, u32[]{:S(2)}, u32[]{:S(2)}) async-start(bf16[16,112,128]{2,1,0:T(8,128)(2,1)} %shard_map.58), calls=%async_computation.3 | async-start | bytes 917504 | tf_op jit(solution)/shard_map/all_to_all | solution.py:364
  13.1 2.3 %copy-start = (bf16[2304,1024]{1,0:T(8,128)(2,1)S(1)}, bf16[2304,1024]{1,0:T(8,128)(2,1)}, u32[]{:S(2)}) copy-start(bf16[2304,1024]{1,0:T(8,128)(2,1)} %tel.1) | copy-start | bytes 14155780
  15.4 42.1 %copy-start.1 = (f32[64,32]{0,1:T(8,128)S(1)}, f32[64,32]{0,1:T(8,128)}, u32[]{:S(2)}) copy-start(f32[64,32]{0,1:T(8,128)} %param.7) | copy-start | bytes 24580
  33.0 5.4 %collective-permute-start = (bf16[16,64,128]{2,1,0:T(8,128)(2,1)S(1)}, bf16[16,64,128]{2,1,0:T(8,128)(2,1)S(1)}, u32[]{:S(2)}, u32[]{:S(2)}) collective-permute-start(bf16[16,64,128]{2,1,0:T(8,128)(2,1)S(1)} %get-tuple-element.32), channel_id=1, source_target_pairs={{0,16},{16,0},{1,17},{17,1},{2,18},{18,2},{3,19},{19,3},{4,20},{20... | collective-permute-start | bytes 786440 | tf_op jit(solution)/shard_map/ppermute | solution.py:385
  59.0 17.8 %all-to-all-start.5 = ((bf16[32,32,128]{2,1,0:T(8,128)(2,1)}), bf16[32,32,128]{2,1,0:T(8,128)(2,1)S(1)}, u32[]{:S(2)}, u32[]{:S(2)}) async-start(bf16[32,32,128]{2,1,0:T(8,128)(2,1)} %get-tuple-element.33), calls=%async_computation.5 | async-start | bytes 524288 | tf_op jit(solution)/shard_map/all_to_all | solution.py:364
  76.7 87.5 %slice-start = ((s8[4718592]{0:T(1024)(128)(4,1)}), s8[4194304]{0:T(1024)(128)(4,1)S(1)}, s32[]{:S(2)}) async-start(s8[4718592]{0:T(1024)(128)(4,1)} %bitcast.17), calls=%async_computation.13 | async-start | bytes 8388608
  99.0 65.3 %slice-start.1 = ((s8[4718592]{0:T(1024)(128)(4,1)}), s8[524288]{0:T(1024)(128)(4,1)S(1)}, s32[]{:S(2)}) async-start(s8[4718592]{0:T(1024)(128)(4,1)} %bitcast.17), calls=%async_computation.14 | async-start | bytes 1048576
  121.0 10.1 %collective-permute-start.1 = (bf16[16,64,128]{2,1,0:T(8,128)(2,1)S(1)}, bf16[16,64,128]{2,1,0:T(8,128)(2,1)S(1)}, u32[]{:S(2)}, u32[]{:S(2)}) collective-permute-start(bf16[16,64,128]{2,1,0:T(8,128)(2,1)S(1)} %get-tuple-element.36), channel_id=1, source_target_pairs={{0,16},{16,0},{1,17},{17,1},{2,18},{18,2},{3,19},{19,3},{4,20},{20... | collective-permute-start | bytes 786440 | tf_op jit(solution)/shard_map/ppermute | solution.py:385
  201.4 18.1 %all-to-all-start.12 = ((f32[32,1,128]{2,1,0:T(1,128)}), f32[32,1,128]{2,1,0:T(1,128)S(1)}, u32[]{:S(2)}, u32[]{:S(2)}) async-start(f32[32,1,128]{2,1,0:T(1,128)} %broadcast_in_dim.4), calls=%async_computation.12 | async-start | bytes 32768 | tf_op jit(solution)/shard_map/all_to_all | solution.py:364

commit v6 on v1

v6 whole, which is shorter than its diff:
```python
import jax
import jax.numpy as jnp
from jax import lax
from jax.experimental import pallas as pl
from jax.experimental.pallas import tpu as pltpu
from jax.sharding import PartitionSpec as P

ITERS = 2

epsilon = 1e-09

F32 = jnp.float32
BF16 = jnp.bfloat16
HIGHEST = lax.Precision.HIGHEST

K = 64
CHIPS = 32
SAMPLES = 16
ROWS = 2304
COLS = 1024
W_OWN = ROWS // SAMPLES
H_OWN = COLS // CHIPS
H_WIDTH = 256
W_STEP = 4
BLOCK = 16
W_HALF = 80
GRAM = 16
W_MSG = W_HALF + GRAM
PAIR = 32
H_MSG = BLOCK + GRAM + 8
LEFT = W_HALF // BLOCK
W_BLOCKS = W_OWN // BLOCK


def split(x):
    high = x.astype(BF16).astype(F32)
    return jnp.concatenate([high, x - high], axis=1).astype(BF16)


def join(x):
    return x[:, :K] + x[:, K:]


def squares():
    row = lax.broadcasted_iota(jnp.int32, (32, 32), 0)
    col = lax.broadcasted_iota(jnp.int32, (32, 32), 1)
    return row, col


TOP = 6.0


def peak(x):
    return jnp.max(jnp.max(x, axis=0, keepdims=True), axis=1, keepdims=True)


def power_of(largest):
    return jnp.floor(jnp.log2(jnp.maximum(largest, 1e-30)))


def code(x, power, factor):
    x = x * (jnp.exp2(TOP - power) * factor)
    x = x * x
    x = x * x
    x = x * x
    return x * x


def root(x):
    return jnp.sqrt(jnp.sqrt(jnp.sqrt(jnp.sqrt(jnp.abs(x)))))


def scale_of(power, factor):
    return jnp.exp2(power - TOP) * (1.0 / factor)


def sample_factor(i):
    return 1.0 + i / 32.0


def chip_factor(i):
    return 1.0 + i / 64.0


def gram_parts(gram):
    row, col = squares()
    first, block, last = gram[:32, :32], gram[:32, 32:], gram[32:, 32:]
    parts = jnp.concatenate([jnp.where(row <= col, first, last), block], axis=1)
    return parts, jnp.sum(jnp.where(row == col, last, 0.0), axis=0, keepdims=True)


def gram_whole(parts, diagonal):
    row, col = squares()
    mixed, block = parts[:, :32], parts[:, 32:]
    turned = lax.dot_general(
        (row == col).astype(F32),
        jnp.concatenate([mixed, block], axis=0),
        (((1,), (1,)), ((), ())),
        precision=HIGHEST,
        preferred_element_type=F32,
    )
    mixed_t, block_t = turned[:, :32], turned[:, 32:]
    one = jnp.where(row <= col, mixed, mixed_t)
    two = jnp.where(row > col, mixed, jnp.where(row < col, mixed_t, diagonal))
    return jnp.concatenate(
        [jnp.concatenate([one, block], axis=1), jnp.concatenate([block_t, two], axis=1)], axis=0
    )


def encode_gram(parts, diagonal, factor):
    power = power_of(jnp.maximum(peak(parts), peak(diagonal)))
    coded = code(parts, power, factor)
    return (
        jnp.concatenate([coded[:GRAM], coded[GRAM:]], axis=1),
        code(diagonal, power, factor),
        power,
    )


def one_above(x):
    return jnp.concatenate([x[:, :K], x[:, K:]], axis=0)


def pair_of(gram):
    row, col = squares()
    parts, diagonal = gram_parts(gram)
    high = parts.astype(BF16).astype(F32)
    low = parts - high
    own = row == col
    first = jnp.where(own, parts[:, :32], high[:, :32])
    third = jnp.where(own, diagonal, low[:, :32])
    return jnp.concatenate([first, high[:, 32:], third, low[:, 32:]], axis=1).astype(BF16)


def of_pair(total):
    row, col = squares()
    own = row == col
    first, third = total[:, :32], total[:, 64:96]
    mixed = jnp.where(own, first, first + third)
    diagonal = jnp.sum(jnp.where(own, third, 0.0), axis=0, keepdims=True)
    block = total[:, 32:64] + total[:, 96:]
    return gram_whole(jnp.concatenate([mixed, block], axis=1), diagonal)


def products(halves):
    return lax.dot_general(halves, halves, (((0,), (0,)), ((), ())), preferred_element_type=F32)


def quarters(four):
    two = four[:K] + four[K:]
    return two[:, :K] + two[:, K:]


def spare_rows(powers, diagonal, power):
    return jnp.concatenate(
        [
            jnp.broadcast_to(powers, (W_BLOCKS, K)),
            jnp.broadcast_to(power, (1, K)),
            jnp.concatenate([diagonal, jnp.zeros((1, K - 32), F32)], axis=1),
            jnp.zeros((BLOCK - W_BLOCKS - 2, K), F32),
        ],
        axis=0,
    )


def w_message(w, gram):
    coded, diagonal, power = gram
    right = jnp.concatenate(
        [w[W_HALF:], spare_rows(jnp.zeros((W_BLOCKS, 1), F32), diagonal, power)], axis=0
    )
    return jnp.concatenate(
        [jnp.concatenate([w[:W_HALF], right], axis=1), coded], axis=0
    ).astype(BF16)


def sums_message(sums, gram, factor):
    coded, diagonal, power = gram
    blocks = [sums[j * BLOCK : (j + 1) * BLOCK] for j in range(W_BLOCKS)]
    largest = jnp.concatenate([jnp.max(x, axis=0, keepdims=True) for x in blocks], axis=0)
    powers = power_of(jnp.max(largest, axis=1, keepdims=True))
    blocks = [code(x, powers[j : j + 1], factor) for j, x in enumerate(blocks)]
    left = jnp.concatenate(blocks[:LEFT], axis=0)
    right = jnp.concatenate(blocks[LEFT:] + [spare_rows(powers, diagonal, power)], axis=0)
    return jnp.concatenate(
        [jnp.concatenate([left, right], axis=1), coded], axis=0
    ).astype(BF16)


def read_gram(message, factor):
    roots = root(message)
    scale = scale_of(message[W_BLOCKS : W_BLOCKS + 1, 127:], factor)
    return roots[BLOCK:] * scale, roots[W_BLOCKS + 1 : W_BLOCKS + 2] * scale


def read_sums(message, factor):
    lane = lax.broadcasted_iota(jnp.int32, (BLOCK, 128), 1)
    scale = scale_of(message[W_HALF - BLOCK :, 127:], factor)
    roots = root(message)
    return [
        roots[j * BLOCK : (j + 1) * BLOCK]
        * jnp.where(lane < K, scale[j : j + 1], scale[LEFT + j : LEFT + j + 1])
        for j in range(LEFT)
    ]


def one_column(both):
    return jnp.concatenate([both[:, :K], both[: W_OWN - W_HALF, K:]], axis=0)


def fill_w(w, factor, out):
    gram = gram_parts(quarters(products(split(w))))
    message = w_message(w, encode_gram(*gram, factor))
    for i in range(SAMPLES):
        out[i] = message


def start_kernel(me, w, out):
    fill_w(w[...], sample_factor(me[1].astype(F32)), out)


def h_numer_kernel(me, got, tel, out, tile, w_turned, w_all, arrived):
    copy = pltpu.make_async_copy(tel, tile, arrived)
    copy.start()
    gram = jnp.zeros((GRAM, 128), F32)
    diagonal = jnp.zeros((1, 128), F32)
    for i in range(SAMPLES):
        message = got[i].astype(F32)
        w_all[i * W_OWN : (i + 1) * W_OWN, :] = one_column(message[:W_HALF])
        more, ends = read_gram(message[W_HALF - BLOCK :], sample_factor(i))
        gram += more
        diagonal += ends
    for j in range(ROWS // 128):
        w_turned[:, j * 128 : (j + 1) * 128] = w_all[j * 128 : (j + 1) * 128, :].T.astype(BF16)
    factor = chip_factor(me[0].astype(F32))
    coded, ends, power = encode_gram(one_above(gram), diagonal[:, K : K + 32], factor)
    ends = jnp.concatenate([ends, jnp.zeros((1, 96), F32)], axis=1)
    power = jnp.broadcast_to(power, (1, 128))
    copy.wait()
    per = H_WIDTH // H_OWN

    def step(n, carry):
        cols = pl.ds(pl.multiple_of(n * H_WIDTH, H_WIDTH), H_WIDTH)
        part = jnp.dot(w_turned[...], tile[:, cols], preferred_element_type=F32).T
        for q in range(per):
            halves = [part[q * H_OWN + r : q * H_OWN + r + BLOCK] for r in (0, BLOCK)]
            powers = [power_of(peak(x)) for x in halves]
            out[n * per + q] = jnp.concatenate(
                [
                    jnp.concatenate([code(x, p, factor) for x, p in zip(halves, powers)], axis=1),
                    coded,
                    ends,
                    power,
                    jnp.broadcast_to(powers[0], (1, 128)),
                    jnp.broadcast_to(powers[1], (1, 128)),
                    jnp.zeros((4, 128), F32),
                ],
                axis=0,
            ).astype(BF16)
        return carry

    lax.fori_loop(0, COLS // H_WIDTH, step, 0)


def h_update_kernel(got, h, h_out, out):
    lane = lax.broadcasted_iota(jnp.int32, (BLOCK, 128), 1)
    numer = jnp.zeros((BLOCK, 128), F32)
    gram = jnp.zeros((GRAM, 128), F32)
    diagonal = jnp.zeros((1, 128), F32)
    for i in range(CHIPS):
        message = got[i].astype(F32)
        roots = root(message)
        scales = scale_of(message[H_MSG - 8 :, 127:], chip_factor(i))
        numer += roots[:BLOCK] * jnp.where(lane < K, scales[2:3], scales[3:4])
        gram += roots[BLOCK : BLOCK + GRAM] * scales[1:2]
        diagonal += roots[H_MSG - 8 : H_MSG - 7] * scales[1:2]
    gram = gram_whole(one_above(gram), diagonal[:, :32])
    old = h[...]
    below = jnp.dot(old, gram, precision=HIGHEST, preferred_element_type=F32) + epsilon
    new = old * one_above(numer) / below
    h_out[...] = new
    halves = split(new)
    for i in range(CHIPS):
        out[i] = halves


def w_numer_kernel(me, got, tel, out, tile, arrived):
    block = W_STEP * W_OWN

    def copy(b):
        rows = pl.ds(pl.multiple_of(b * block, block), block)
        return pltpu.make_async_copy(tel.at[rows], tile.at[rows], arrived.at[b])

    for b in range(ROWS // block):
        copy(b).start()
    halves = got[...].reshape(COLS, 128)
    four = products(halves)
    factor = sample_factor(me[1].astype(F32))
    gram = encode_gram(*gram_parts(quarters(four)), factor)
    last = out.shape[1] > W_MSG
    if last:
        pair = pair_of(four[:K, :K])
    high = halves[:, :K]

    def step(b, carry):
        copy(b).wait()
        rows = pl.ds(pl.multiple_of(b * block, block), block)
        part = jnp.dot(tile[rows, :], high, preferred_element_type=F32)
        for q in range(W_STEP):
            message = sums_message(part[q * W_OWN : (q + 1) * W_OWN], gram, factor)
            if last:
                message = jnp.concatenate([message, pair], axis=0)
            out[b * W_STEP + q] = message
        return carry

    lax.fori_loop(0, ROWS // block, step, 0)


def w_new(got, w):
    blocks = [jnp.zeros((BLOCK, 128), F32)] * LEFT
    gram = jnp.zeros((GRAM, 128), F32)
    diagonal = jnp.zeros((1, 128), F32)
    rest = jnp.zeros((got.shape[1] - W_MSG, 128), F32) if got.shape[1] > W_MSG else None
    for i in range(SAMPLES):
        message = got[i].astype(F32)
        terms = read_sums(message[:W_HALF], sample_factor(i))
        blocks = [total + term for total, term in zip(blocks, terms)]
        more, ends = read_gram(message[W_HALF - BLOCK : W_MSG], sample_factor(i))
        gram += more
        diagonal += ends
        if rest is not None:
            rest += message[W_MSG:]
    numer = one_column(jnp.concatenate(blocks, axis=0))
    gram = gram_whole(one_above(gram), diagonal[:, K : K + 32])
    old = w[...]
    below = jnp.dot(old, gram, precision=HIGHEST, preferred_element_type=F32) + epsilon
    return old * numer / below, numer, rest


def w_update_kernel(me, got, w, w_out, out):
    new, _, _ = w_new(got, w)
    w_out[...] = new
    fill_w(new, sample_factor(me[1].astype(F32)), out)


def w_last_kernel(got, w, energy, w_out, out):
    new, numer, rest = w_new(got, w)
    w_out[...] = new
    rounded = new.astype(BF16).astype(F32)
    gram = of_pair(rest)
    fitted = jnp.dot(rounded, gram, precision=HIGHEST, preferred_element_type=F32)
    share = jnp.sum(rounded * (fitted - 2.0 * numer))
    lane = lax.broadcasted_iota(jnp.int32, (1, 128), 1)
    pair = jnp.where(lane < K, share, energy[...])
    for i in range(SAMPLES):
        out[i] = pair


def energy_kernel(tel, out):
    def step(i, energy):
        rows = pl.ds(pl.multiple_of(i * W_OWN, W_OWN), W_OWN)
        values = tel[rows, :].astype(F32)
        return energy + jnp.sum((values * values).reshape(W_OWN // 8, 8, COLS), axis=0)

    energy = lax.fori_loop(0, SAMPLES, step, jnp.zeros((8, COLS), F32))
    out[...] = jnp.full((1, 128), jnp.sum(energy), F32)


def last_rows_kernel(w, out):
    rows = w[...]
    right = jnp.concatenate([rows[W_HALF:], jnp.zeros((BLOCK, K), F32)], axis=0)
    message = jnp.concatenate([rows[:W_HALF], right], axis=1).astype(BF16)
    for i in range(SAMPLES):
        out[i] = message


def error_kernel(got_w, got_h, tel, out):
    high = got_h[...].reshape(COLS, 128)[:, :K]

    def step(i, error):
        rows = pl.ds(pl.multiple_of(i * W_OWN, W_OWN), W_OWN)
        rebuilt = lax.dot_general(
            one_column(got_w[i].astype(F32)).astype(BF16),
            high,
            (((1,), (1,)), ((), ())),
            preferred_element_type=F32,
        )
        difference = tel[rows, :].astype(F32) - rebuilt
        return error + jnp.sum((difference * difference).reshape(W_OWN // 8, 8, COLS), axis=0)

    error = lax.fori_loop(0, SAMPLES, step, jnp.zeros((8, COLS), F32))
    share = jnp.full((1, 128), jnp.sum(error), F32)
    for i in range(SAMPLES):
        out[i] = share


VMEM = pl.BlockSpec(memory_space=pltpu.VMEM)
SMEM = pl.BlockSpec(memory_space=pltpu.SMEM)
HBM = pl.BlockSpec(memory_space=pltpu.HBM)
LIMIT = pltpu.CompilerParams(vmem_limit_bytes=32 * 1024 * 1024)
PRODUCT = pl.CostEstimate(
    flops=2 * K * ROWS * COLS, bytes_accessed=2 * ROWS * COLS, transcendentals=0
)
ENERGY = pl.CostEstimate(flops=2 * ROWS * COLS, bytes_accessed=2 * ROWS * COLS, transcendentals=0)


def call(kernel, inputs, outs, cost=None, specs=None, scratch=()):
    return pl.pallas_call(
        kernel,
        out_shape=[jax.ShapeDtypeStruct(shape, dtype) for shape, dtype in outs],
        in_specs=[VMEM] * len(inputs) if specs is None else specs,
        out_specs=[VMEM] * len(outs),
        scratch_shapes=list(scratch),
        compiler_params=LIMIT,
        cost_estimate=cost,
    )(*inputs)


def exchange(x, axis):
    return lax.all_to_all(x, axis, 0, 0, tiled=True)


def sum_everywhere(shares):
    part = jnp.sum(exchange(shares, "samples"), axis=0)
    part = exchange(jnp.broadcast_to(part[None], (CHIPS, 1, 128)), "chips")
    return jnp.sum(part, axis=0)


def body(telemetry, chip_factors, sample_factors):
    me = jnp.stack([lax.axis_index("chips"), lax.axis_index("samples")])
    tile = pltpu.VMEM((ROWS, COLS), BF16)
    w, h = chip_factors.T, sample_factors.T
    w_sent = ((SAMPLES, W_MSG, 128), BF16)
    (sent,) = call(start_kernel, (me, w), [w_sent], None, [SMEM, VMEM])
    got_w = exchange(sent, "samples")
    (energy,) = call(energy_kernel, (telemetry,), [((1, 128), F32)], ENERGY)
    for sweep in range(ITERS):
        last = sweep == ITERS - 1
        (sent,) = call(
            h_numer_kernel,
            (me, got_w, telemetry),
            [((CHIPS, H_MSG, 128), BF16)],
            PRODUCT,
            [SMEM, VMEM, HBM],
            [
                tile,
                pltpu.VMEM((K, ROWS), BF16),
                pltpu.VMEM((ROWS, K), F32),
                pltpu.SemaphoreType.DMA,
            ],
        )
        got = exchange(sent, "chips")
        h, sent = call(
            h_update_kernel, (got, h), [((H_OWN, K), F32), ((CHIPS, H_OWN, 128), BF16)]
        )
        got_h = exchange(sent, "chips")
        (sent,) = call(
            w_numer_kernel,
            (me, got_h, telemetry),
            [((SAMPLES, W_MSG + PAIR if last else W_MSG, 128), BF16)],
            PRODUCT,
            [SMEM, VMEM, HBM],
            [tile, pltpu.SemaphoreType.DMA((SAMPLES // W_STEP,))],
        )
        got = exchange(sent, "samples")
        if not last:
            w, sent = call(
                w_update_kernel,
                (me, got, w),
                [((W_OWN, K), F32), w_sent],
                None,
                [SMEM, VMEM, VMEM],
            )
            got_w = exchange(sent, "samples")
    w, shares = call(
        w_last_kernel, (got, w, energy), [((W_OWN, K), F32), ((SAMPLES, 1, 128), F32)]
    )
    sums = sum_everywhere(shares)
    total = sums[0, K]
    expanded = sums[0, 0] + total

    def direct(w, got_h, telemetry):
        (sent,) = call(last_rows_kernel, (w,), [((SAMPLES, W_HALF, 128), BF16)])
        (shares,) = call(
            error_kernel,
            (exchange(sent, "samples"), got_h, telemetry),
            [((SAMPLES, 1, 128), F32)],
            PRODUCT,
        )
        return sum_everywhere(shares)[0, 0]

    fit_error = lax.cond(
        expanded < 0.02 * total,
        direct,
        lambda *operands: expanded,
        w,
        got_h,
        telemetry,
    )
    return w.T, h.T, jnp.sqrt(fit_error / total)


def solution(mesh):
    return jax.shard_map(
        body,
        mesh=mesh,
        in_specs=(
            P("chips", "samples"),
            P(None, ("chips", "samples")),
            P(None, ("samples", "chips")),
        ),
        out_specs=(P(None, ("chips", "samples")), P(None, ("samples", "chips")), P()),
        check_vma=False,
    )
```

time: 253 us -> 219 us (0.87)
  blocking collectives: 201 us -> 149 us
  Pallas kernels: 19.5 us -> 31.7 us
  waiting for transfers between devices: 7.88 us -> 16.9 us
    all_to_all x10 -> x8, blocking collectives: 201 us -> 149 us  [exchange(): return lax.all_to_all(x, axis, 0, 0, tiled=True)]
    pallas_call x10, Pallas kernels: 19.5 us -> 31.7 us  [call(): pl.pallas_call(kernel, out_shape=[jax.ShapeDtypeStruct(shape, dtype) for...]
    all_to_all x1 -> x2, waiting for transfers between devices: 7.88 us -> 16.9 us  [exchange(): return lax.all_to_all(x, axis, 0, 0, tiled=True)]
    all_to_all x1 -> x2, starting transfers between devices: 15.7 us -> 13.7 us  [exchange(): return lax.all_to_all(x, axis, 0, 0, tiled=True)]
  transfers between devices with their start and end apart: 1 -> 2, of which waited for: 1 -> 2; matrix products, arithmetic and copies ran while one was open for 0% -> 0% of each run, Pallas kernels for 0% -> 1%
where the time goes in v6:
time: 219 us
  blocking collectives  149 us (68%)
  Pallas kernels  31.7 us (14%)
  waiting for transfers between devices  16.9 us (8%)
  starting transfers between devices  13.7 us (6%)
  between operations  4.54 us (2%)
  local copies, waits for them, and re-layouts  2.86 us (1%)
    all_to_all x8, blocking collectives, exchange(): return lax.all_to_all(x, axis, 0, 0, tiled=True)  149 us
    pallas_call x10, Pallas kernels, call(): pl.pallas_call(kernel, out_shape=[jax.ShapeDtypeStruct(shape, dtype) for...  31.7 us
    all_to_all x2, waiting for transfers between devices, exchange(): return lax.all_to_all(x, axis, 0, 0, tiled=True)  16.9 us
    all_to_all x2, starting transfers between devices, exchange(): return lax.all_to_all(x, axis, 0, 0, tiled=True)  13.7 us
  transfers between devices with their start and end apart: 2, of which 2 were waited for; matrix products, arithmetic and copies ran while one was open for 0% of the time, Pallas kernels for 1%

profile of v6, /device:TPU:1, one launch (start us, length us, event | category | flops | bytes accessed | tf_op | source)
XLA Modules:
  0.0 218.7 jit_solution(7759998757791377436)
XLA Ops:
  0.6 0.0 copy-start
  0.6 0.9 copy.11
  1.6 0.0 copy-start.1
  1.6 0.1 pad_add_fusion.me
  1.7 1.1 shard_map.58
  2.8 23.9 %all_to_all.65.got = bf16[16,96,128]{2,1,0:T(8,128)(2,1)S(1)} all-to-all(bf16[16,96,128]{2,1,0:T(8,128)(2,1)S(1)} %shard_map.58), channel_id=1, replica_groups=mesh['chips'=32,'samples'=16] {'samples'}, dimensions={0} | all-to-all | bytes 786432 | tf_op jit(solution)/shard_map/all_to_all | solution.py:419
  26.7 5.9 %shard_map.59 = bf16[32,40,128]{2,1,0:T(8,128)(2,1)S(1)} custom-call(s32[2]{0:T(128)S(1)} %pad_add_fusion.me, bf16[16,96,128]{2,1,0:T(8,128)(2,1)S(1)} %all_to_all.65.got, bf16[2304,1024]{1,0:T(8,128)(2,1)} %tel.9), custom_call_target="tpu_custom_call" | custom-call | flops 301989888 | bytes 4718592 | tf_op jit(solution)/shard_map/pallas_call | solution.py:407
  32.6 24.8 %all_to_all.66.got = bf16[32,40,128]{2,1,0:T(8,128)(2,1)S(1)} all-to-all(bf16[32,40,128]{2,1,0:T(8,128)(2,1)S(1)} %shard_map.59), channel_id=1, replica_groups=mesh['chips'=32,'samples'=16] {'chips'}, dimensions={0} | all-to-all | bytes 655360 | tf_op jit(solution)/shard_map/all_to_all | solution.py:419
  57.4 0.0 copy-done
  57.5 1.3 shard_map.60
  58.8 15.6 %all_to_all.67.got = bf16[32,32,128]{2,1,0:T(8,128)(2,1)S(1)} all-to-all(bf16[32,32,128]{2,1,0:T(8,128)(2,1)S(1)} %get-tuple-element.24), channel_id=1, replica_groups=mesh['chips'=32,'samples'=16] {'chips'}, dimensions={0} | all-to-all | bytes 524288 | tf_op jit(solution)/shard_map/all_to_all | solution.py:419
  74.4 0.0 copy-done.1
  74.4 4.7 %shard_map.61 = bf16[16,96,128]{2,1,0:T(8,128)(2,1)S(1)} custom-call(s32[2]{0:T(128)S(1)} %pad_add_fusion.me, bf16[32,32,128]{2,1,0:T(8,128)(2,1)S(1)} %all_to_all.67.got, bf16[2304,1024]{1,0:T(8,128)(2,1)S(1)} %copy-done.1), custom_call_target="tpu_custom_call" | custom-call | flops 301989888 | bytes 4718592 | tf_op jit(solution)/shard_map/pallas_call | solution.py:407
  79.1 15.0 %all_to_all.68.got = bf16[16,96,128]{2,1,0:T(8,128)(2,1)S(1)} all-to-all(bf16[16,96,128]{2,1,0:T(8,128)(2,1)S(1)} %shard_map.61), channel_id=1, replica_groups=mesh['chips'=32,'samples'=16] {'samples'}, dimensions={0} | all-to-all | bytes 786432 | tf_op jit(solution)/shard_map/all_to_all | solution.py:419
  94.1 2.6 %shard_map.62 = (f32[144,64]{1,0:T(8,128)S(1)}, bf16[16,96,128]{2,1,0:T(8,128)(2,1)S(1)}) custom-call(s32[2]{0:T(128)S(1)} %pad_add_fusion.me, bf16[16,96,128]{2,1,0:T(8,128)(2,1)S(1)} %all_to_all.68.got, f32[144,64]{1,0:T(8,128)S(1)} %bitcast.15), custom_call_target="tpu_custom_call" | custom-call | tf_op jit(solution)/shard_map/pallas_call | solution.py:407
  96.8 16.7 %all_to_all.69.got = bf16[16,96,128]{2,1,0:T(8,128)(2,1)S(1)} all-to-all(bf16[16,96,128]{2,1,0:T(8,128)(2,1)S(1)} %get-tuple-element.25), channel_id=1, replica_groups=mesh['chips'=32,'samples'=16] {'samples'}, dimensions={0} | all-to-all | bytes 786432 | tf_op jit(solution)/shard_map/all_to_all | solution.py:419
  113.5 4.0 %shard_map.63 = bf16[32,40,128]{2,1,0:T(8,128)(2,1)S(1)} custom-call(s32[2]{0:T(128)S(1)} %pad_add_fusion.me, bf16[16,96,128]{2,1,0:T(8,128)(2,1)S(1)} %all_to_all.69.got, bf16[2304,1024]{1,0:T(8,128)(2,1)S(1)} %copy-done.1), custom_call_target="tpu_custom_call" | custom-call | flops 301989888 | bytes 4718592 | tf_op jit(solution)/shard_map/pallas_call | solution.py:407
  117.5 22.9 %all_to_all.70.got = bf16[32,40,128]{2,1,0:T(8,128)(2,1)S(1)} all-to-all(bf16[32,40,128]{2,1,0:T(8,128)(2,1)S(1)} %shard_map.63), channel_id=1, replica_groups=mesh['chips'=32,'samples'=16] {'chips'}, dimensions={0} | all-to-all | bytes 655360 | tf_op jit(solution)/shard_map/all_to_all | solution.py:419
  140.4 1.8 shard_map.64
  142.2 15.6 %all_to_all.71.got = bf16[32,32,128]{2,1,0:T(8,128)(2,1)S(1)} all-to-all(bf16[32,32,128]{2,1,0:T(8,128)(2,1)S(1)} %get-tuple-element.27), channel_id=1, replica_groups=mesh['chips'=32,'samples'=16] {'chips'}, dimensions={0} | all-to-all | bytes 524288 | tf_op jit(solution)/shard_map/all_to_all | solution.py:419
  157.8 5.5 %shard_map.65 = bf16[16,128,128]{2,1,0:T(8,128)(2,1)} custom-call(s32[2]{0:T(128)S(1)} %pad_add_fusion.me, bf16[32,32,128]{2,1,0:T(8,128)(2,1)S(1)} %all_to_all.71.got, bf16[2304,1024]{1,0:T(8,128)(2,1)S(1)} %copy-done.1), custom_call_target="tpu_custom_call" | custom-call | flops 301989888 | bytes 4718592 | tf_op jit(solution)/shard_map/pallas_call | solution.py:407
  163.3 4.0 %all-to-all-start.10 = ((bf16[16,128,128]{2,1,0:T(8,128)(2,1)}), bf16[16,128,128]{2,1,0:T(8,128)(2,1)S(1)}, u32[]{:S(2)}, u32[]{:S(2)}) async-start(bf16[16,128,128]{2,1,0:T(8,128)(2,1)} %shard_map.65), calls=%async_computation.10 | async-start | bytes 1048576 | tf_op jit(solution)/shard_map/all_to_all | solution.py:419
  167.3 2.8 %shard_map.66.energy = f32[1,128]{1,0:T(1,128)S(1)} custom-call(bf16[2304,1024]{1,0:T(8,128)(2,1)} %tel.9), custom_call_target="tpu_custom_call" | custom-call | flops 4718592 | bytes 4718592 | tf_op jit(solution)/shard_map/pallas_call | solution.py:407
  170.1 9.8 %all-to-all-done.10.got = bf16[16,128,128]{2,1,0:T(8,128)(2,1)S(1)} async-done(((bf16[16,128,128]{2,1,0:T(8,128)(2,1)}), bf16[16,128,128]{2,1,0:T(8,128)(2,1)S(1)}, u32[]{:S(2)}, u32[]{:S(2)}) %all-to-all-start.10) | async-done | bytes 524320 | tf_op jit(solution)/shard_map/all_to_all | solution.py:419
  179.9 1.9 shard_map.67
  181.8 14.3 %all_to_all.72 = f32[16,1,128]{2,1,0:T(1,128)S(1)} all-to-all(f32[16,1,128]{2,1,0:T(1,128)S(1)} %get-tuple-element.31), channel_id=1, replica_groups=mesh['chips'=32,'samples'=16] {'samples'}, dimensions={0} | all-to-all | bytes 16384 | tf_op jit(solution)/shard_map/all_to_all | solution.py:419
  196.2 0.6 broadcast_in_dim.4
  196.8 9.6 %all-to-all-start.12 = ((f32[32,1,128]{2,1,0:T(1,128)}), f32[32,1,128]{2,1,0:T(1,128)S(1)}, u32[]{:S(2)}, u32[]{:S(2)}) async-start(f32[32,1,128]{2,1,0:T(1,128)} %broadcast_in_dim.4), calls=%async_computation.12 | async-start | bytes 32768 | tf_op jit(solution)/shard_map/all_to_all | solution.py:419
  206.4 0.7 copy.13
  207.2 7.1 %all-to-all-done.12 = f32[32,1,128]{2,1,0:T(1,128)S(1)} async-done(((f32[32,1,128]{2,1,0:T(1,128)}), f32[32,1,128]{2,1,0:T(1,128)S(1)}, u32[]{:S(2)}, u32[]{:S(2)}) %all-to-all-start.12) | async-done | bytes 16416 | tf_op jit(solution)/shard_map/all_to_all | solution.py:419
  214.3 0.6 fusion
  (3 shorter events, 0.1 us)
Async XLA Ops:
  0.6 56.8 %copy-start = (f32[64,32]{0,1:T(8,128)S(1)}, f32[64,32]{0,1:T(8,128)}, u32[]{:S(2)}) copy-start(f32[64,32]{0,1:T(8,128)} %param.7) | copy-start | bytes 24580
  1.6 72.8 %copy-start.1 = (bf16[2304,1024]{1,0:T(8,128)(2,1)S(1)}, bf16[2304,1024]{1,0:T(8,128)(2,1)}, u32[]{:S(2)}) copy-start(bf16[2304,1024]{1,0:T(8,128)(2,1)} %tel.9) | copy-start | bytes 14155780
  163.3 16.6 %all-to-all-start.10 = ((bf16[16,128,128]{2,1,0:T(8,128)(2,1)}), bf16[16,128,128]{2,1,0:T(8,128)(2,1)S(1)}, u32[]{:S(2)}, u32[]{:S(2)}) async-start(bf16[16,128,128]{2,1,0:T(8,128)(2,1)} %shard_map.65), calls=%async_computation.10 | async-start | bytes 1048576 | tf_op jit(solution)/shard_map/all_to_all | solution.py:419
  196.8 17.5 %all-to-all-start.12 = ((f32[32,1,128]{2,1,0:T(1,128)}), f32[32,1,128]{2,1,0:T(1,128)S(1)}, u32[]{:S(2)}, u32[]{:S(2)}) async-start(f32[32,1,128]{2,1,0:T(1,128)} %broadcast_in_dim.4), calls=%async_computation.12 | async-start | bytes 32768 | tf_op jit(solution)/shard_map/all_to_all | solution.py:419

commit v7 on v6

--- a/solution.py
+++ b/solution.py
@@ -21,7 +21,7 @@
 W_OWN = ROWS // SAMPLES
 H_OWN = COLS // CHIPS
 H_WIDTH = 256
-W_STEP = 4
+W_STEP = 16
 BLOCK = 16
 W_HALF = 80
 GRAM = 16
@@ -58,28 +58,39 @@
     return jnp.floor(jnp.log2(jnp.maximum(largest, 1e-30)))
 
 
-def code(x, power, factor):
-    x = x * (jnp.exp2(TOP - power) * factor)
+def sixteenth(x):
     x = x * x
     x = x * x
     x = x * x
     return x * x
 
 
+def code(x, power, factor):
+    return sixteenth(x * (jnp.exp2(TOP - power) * factor))
+
+
 def root(x):
-    return jnp.sqrt(jnp.sqrt(jnp.sqrt(jnp.sqrt(jnp.abs(x)))))
+    return lax.rsqrt(lax.rsqrt(lax.rsqrt(lax.rsqrt(jnp.abs(x)))))
 
 
 def scale_of(power, factor):
-    return jnp.exp2(power - TOP) * (1.0 / factor)
+    return jnp.exp2(power - TOP) / factor
+
+
+def copies(message, out):
+    def step(i, carry):
+        out[i] = message
+        return carry
+
+    lax.fori_loop(0, out.shape[0], step, 0, unroll=True)
 
 
 def sample_factor(i):
-    return 1.0 + i / 32.0
+    return 1.0 + jnp.full((1, 1), i, jnp.int32).astype(F32) * (1.0 / 32.0)
 
 
 def chip_factor(i):
-    return 1.0 + i / 64.0
+    return 1.0 + jnp.full((1, 1), i, jnp.int32).astype(F32) * (1.0 / 64.0)
 
 
 def gram_parts(gram):
@@ -151,10 +162,11 @@
     return two[:, :K] + two[:, K:]
 
 
-def spare_rows(powers, diagonal, power):
+def spare_rows(left, right, diagonal, power):
     return jnp.concatenate(
         [
-            jnp.broadcast_to(powers, (W_BLOCKS, K)),
+            jnp.broadcast_to(left, (LEFT, K)),
+            jnp.broadcast_to(right, (LEFT - 1, K)),
             jnp.broadcast_to(power, (1, K)),
             jnp.concatenate([diagonal, jnp.zeros((1, K - 32), F32)], axis=1),
             jnp.zeros((BLOCK - W_BLOCKS - 2, K), F32),
@@ -165,8 +177,9 @@
 
 def w_message(w, gram):
     coded, diagonal, power = gram
+    none = jnp.zeros((LEFT, 1), F32)
     right = jnp.concatenate(
-        [w[W_HALF:], spare_rows(jnp.zeros((W_BLOCKS, 1), F32), diagonal, power)], axis=0
+        [w[W_HALF:], spare_rows(none, none[1:], diagonal, power)], axis=0
     )
     return jnp.concatenate(
         [jnp.concatenate([w[:W_HALF], right], axis=1), coded], axis=0
@@ -175,15 +188,25 @@
 
 def sums_message(sums, gram, factor):
     coded, diagonal, power = gram
-    blocks = [sums[j * BLOCK : (j + 1) * BLOCK] for j in range(W_BLOCKS)]
-    largest = jnp.concatenate([jnp.max(x, axis=0, keepdims=True) for x in blocks], axis=0)
-    powers = power_of(jnp.max(largest, axis=1, keepdims=True))
-    blocks = [code(x, powers[j : j + 1], factor) for j, x in enumerate(blocks)]
-    left = jnp.concatenate(blocks[:LEFT], axis=0)
-    right = jnp.concatenate(blocks[LEFT:] + [spare_rows(powers, diagonal, power)], axis=0)
-    return jnp.concatenate(
-        [jnp.concatenate([left, right], axis=1), coded], axis=0
-    ).astype(BF16)
+    both = jnp.concatenate(
+        [sums[:W_HALF], jnp.concatenate([sums[W_HALF:], jnp.zeros((BLOCK, K), F32)], axis=0)],
+        axis=1,
+    )
+    blocks = [both[j * BLOCK : (j + 1) * BLOCK] for j in range(LEFT)]
+    largest = jnp.concatenate(
+        [jnp.max(x, axis=0, keepdims=True) for x in blocks] + [jnp.zeros((8 - LEFT, 128), F32)],
+        axis=0,
+    )
+    lane = lax.broadcasted_iota(jnp.int32, (8, 128), 1)
+    left = power_of(jnp.max(jnp.where(lane < K, largest, 0.0), axis=1, keepdims=True))
+    right = power_of(jnp.max(jnp.where(lane < K, 0.0, largest), axis=1, keepdims=True))
+    powers = jnp.where(lane < K, left, right)
+    scale = jnp.exp2(TOP - powers) * factor
+    blocks = [sixteenth(x * scale[j : j + 1]) for j, x in enumerate(blocks)]
+    free = jnp.concatenate(
+        [blocks[-1][:, :K], spare_rows(left[:LEFT], right[: LEFT - 1], diagonal, power)], axis=1
+    )
+    return jnp.concatenate(blocks[:-1] + [free, coded], axis=0).astype(BF16)
 
 
 def read_gram(message, factor):
@@ -209,29 +232,37 @@
 
 def fill_w(w, factor, out):
     gram = gram_parts(quarters(products(split(w))))
-    message = w_message(w, encode_gram(*gram, factor))
-    for i in range(SAMPLES):
-        out[i] = message
-
-
-def start_kernel(me, w, out):
-    fill_w(w[...], sample_factor(me[1].astype(F32)), out)
+    copies(w_message(w, encode_gram(*gram, factor)), out)
+
+
+def start_kernel(me, w, w_out, out):
+    wide = jnp.concatenate([w[...], jnp.zeros((K, 256 - W_OWN), F32)], axis=1)
+    turned = wide.T[:W_OWN]
+    w_out[...] = turned
+    fill_w(turned, sample_factor(me[1]), out)
 
 
 def h_numer_kernel(me, got, tel, out, tile, w_turned, w_all, arrived):
     copy = pltpu.make_async_copy(tel, tile, arrived)
     copy.start()
-    gram = jnp.zeros((GRAM, 128), F32)
-    diagonal = jnp.zeros((1, 128), F32)
-    for i in range(SAMPLES):
+
+    def gather(i, carry):
+        gram, diagonal = carry
         message = got[i].astype(F32)
-        w_all[i * W_OWN : (i + 1) * W_OWN, :] = one_column(message[:W_HALF])
+        w_all[pl.ds(pl.multiple_of(i * W_OWN, BLOCK), W_OWN), :] = one_column(message[:W_HALF])
         more, ends = read_gram(message[W_HALF - BLOCK :], sample_factor(i))
-        gram += more
-        diagonal += ends
-    for j in range(ROWS // 128):
-        w_turned[:, j * 128 : (j + 1) * 128] = w_all[j * 128 : (j + 1) * 128, :].T.astype(BF16)
-    factor = chip_factor(me[0].astype(F32))
+        return gram + more, diagonal + ends
+
+    zero = (jnp.zeros((GRAM, 128), F32), jnp.zeros((1, 128), F32))
+    gram, diagonal = lax.fori_loop(0, SAMPLES, gather, zero, unroll=True)
+
+    def turn(j, carry):
+        at = pl.ds(pl.multiple_of(j * 128, 128), 128)
+        w_turned[:, at] = w_all[at, :].T.astype(BF16)
+        return carry
+
+    lax.fori_loop(0, ROWS // 128, turn, 0, unroll=True)
+    factor = chip_factor(me[0])
     coded, ends, power = encode_gram(one_above(gram), diagonal[:, K : K + 32], factor)
     ends = jnp.concatenate([ends, jnp.zeros((1, 96), F32)], axis=1)
     power = jnp.broadcast_to(power, (1, 128))
@@ -258,29 +289,32 @@
             ).astype(BF16)
         return carry
 
-    lax.fori_loop(0, COLS // H_WIDTH, step, 0)
+    lax.fori_loop(0, COLS // H_WIDTH, step, 0, unroll=True)
 
 
 def h_update_kernel(got, h, h_out, out):
     lane = lax.broadcasted_iota(jnp.int32, (BLOCK, 128), 1)
-    numer = jnp.zeros((BLOCK, 128), F32)
-    gram = jnp.zeros((GRAM, 128), F32)
-    diagonal = jnp.zeros((1, 128), F32)
-    for i in range(CHIPS):
+
+    def add(i, carry):
+        numer, gram, diagonal = carry
         message = got[i].astype(F32)
         roots = root(message)
         scales = scale_of(message[H_MSG - 8 :, 127:], chip_factor(i))
         numer += roots[:BLOCK] * jnp.where(lane < K, scales[2:3], scales[3:4])
         gram += roots[BLOCK : BLOCK + GRAM] * scales[1:2]
         diagonal += roots[H_MSG - 8 : H_MSG - 7] * scales[1:2]
+        return numer, gram, diagonal
+
+    zero = jnp.zeros((BLOCK, 128), F32)
+    numer, gram, diagonal = lax.fori_loop(
+        0, CHIPS, add, (zero, zero, jnp.zeros((1, 128), F32)), unroll=True
+    )
     gram = gram_whole(one_above(gram), diagonal[:, :32])
     old = h[...]
     below = jnp.dot(old, gram, precision=HIGHEST, preferred_element_type=F32) + epsilon
     new = old * one_above(numer) / below
     h_out[...] = new
-    halves = split(new)
-    for i in range(CHIPS):
-        out[i] = halves
+    copies(split(new), out)
 
 
 def w_numer_kernel(me, got, tel, out, tile, arrived):
@@ -294,7 +328,7 @@
         copy(b).start()
     halves = got[...].reshape(COLS, 128)
     four = products(halves)
-    factor = sample_factor(me[1].astype(F32))
+    factor = sample_factor(me[1])
     gram = encode_gram(*gram_parts(quarters(four)), factor)
     last = out.shape[1] > W_MSG
     if last:
@@ -316,19 +350,26 @@
 
 
 def w_new(got, w):
-    blocks = [jnp.zeros((BLOCK, 128), F32)] * LEFT
-    gram = jnp.zeros((GRAM, 128), F32)
-    diagonal = jnp.zeros((1, 128), F32)
-    rest = jnp.zeros((got.shape[1] - W_MSG, 128), F32) if got.shape[1] > W_MSG else None
-    for i in range(SAMPLES):
+    last = got.shape[1] > W_MSG
+
+    def add(i, carry):
+        blocks, gram, diagonal, rest = carry
         message = got[i].astype(F32)
         terms = read_sums(message[:W_HALF], sample_factor(i))
-        blocks = [total + term for total, term in zip(blocks, terms)]
         more, ends = read_gram(message[W_HALF - BLOCK : W_MSG], sample_factor(i))
-        gram += more
-        diagonal += ends
-        if rest is not None:
+        if last:
             rest += message[W_MSG:]
+        blocks = tuple(total + term for total, term in zip(blocks, terms))
+        return blocks, gram + more, diagonal + ends, rest
+
+    zero = jnp.zeros((BLOCK, 128), F32)
+    blocks, gram, diagonal, rest = lax.fori_loop(
+        0,
+        SAMPLES,
+        add,
+        ((zero,) * LEFT, zero, jnp.zeros((1, 128), F32), jnp.zeros((PAIR, 128), F32)),
+        unroll=True,
+    )
     numer = one_column(jnp.concatenate(blocks, axis=0))
     gram = gram_whole(one_above(gram), diagonal[:, K : K + 32])
     old = w[...]
@@ -339,7 +380,7 @@
 def w_update_kernel(me, got, w, w_out, out):
     new, _, _ = w_new(got, w)
     w_out[...] = new
-    fill_w(new, sample_factor(me[1].astype(F32)), out)
+    fill_w(new, sample_factor(me[1]), out)
 
 
 def w_last_kernel(got, w, energy, w_out, out):
@@ -351,8 +392,7 @@
     share = jnp.sum(rounded * (fitted - 2.0 * numer))
     lane = lax.broadcasted_iota(jnp.int32, (1, 128), 1)
     pair = jnp.where(lane < K, share, energy[...])
-    for i in range(SAMPLES):
-        out[i] = pair
+    copies(pair, out)
 
 
 def energy_kernel(tel, out):
@@ -369,8 +409,7 @@
     rows = w[...]
     right = jnp.concatenate([rows[W_HALF:], jnp.zeros((BLOCK, K), F32)], axis=0)
     message = jnp.concatenate([rows[:W_HALF], right], axis=1).astype(BF16)
-    for i in range(SAMPLES):
-        out[i] = message
+    copies(message, out)
 
 
 def error_kernel(got_w, got_h, tel, out):
@@ -389,8 +428,7 @@
 
     error = lax.fori_loop(0, SAMPLES, step, jnp.zeros((8, COLS), F32))
     share = jnp.full((1, 128), jnp.sum(error), F32)
-    for i in range(SAMPLES):
-        out[i] = share
+    copies(share, out)
 
 
 VMEM = pl.BlockSpec(memory_space=pltpu.VMEM)
@@ -428,9 +466,9 @@
 def body(telemetry, chip_factors, sample_factors):
     me = jnp.stack([lax.axis_index("chips"), lax.axis_index("samples")])
     tile = pltpu.VMEM((ROWS, COLS), BF16)
-    w, h = chip_factors.T, sample_factors.T
-    w_sent = ((SAMPLES, W_MSG, 128), BF16)
-    (sent,) = call(start_kernel, (me, w), [w_sent], None, [SMEM, VMEM])
+    h = sample_factors.T
+    w_sent = [((W_OWN, K), F32), ((SAMPLES, W_MSG, 128), BF16)]
+    w, sent = call(start_kernel, (me, chip_factors), w_sent, None, [SMEM, VMEM])
     got_w = exchange(sent, "samples")
     (energy,) = call(energy_kernel, (telemetry,), [((1, 128), F32)], ENERGY)
     for sweep in range(ITERS):
@@ -466,7 +504,7 @@
             w, sent = call(
                 w_update_kernel,
                 (me, got, w),
-                [((W_OWN, K), F32), w_sent],
+                w_sent,
                 None,
                 [SMEM, VMEM, VMEM],
             )

time: 219 us -> 212 us (0.968)
  Pallas kernels: 31.7 us -> 24.3 us
    pallas_call x10, Pallas kernels: 31.7 us -> 24.3 us  [call(): pl.pallas_call(kernel, out_shape=[jax.ShapeDtypeStruct(shape, dtype) for...]
where the time goes in v7:
time: 212 us; the launch traced here: 211 us
  blocking collectives  149 us (70%)
  Pallas kernels  24.3 us (11%)
  waiting for transfers between devices  16.8 us (8%)
  starting transfers between devices  13.7 us (6%)
  between operations  4.52 us (2%)
  local copies, waits for them, and re-layouts  2.76 us (1%)
    all_to_all x8, blocking collectives, exchange(): return lax.all_to_all(x, axis, 0, 0, tiled=True)  149 us
    pallas_call x10, Pallas kernels, call(): pl.pallas_call(kernel, out_shape=[jax.ShapeDtypeStruct(shape, dtype) for...  24.3 us
    all_to_all x2, waiting for transfers between devices, exchange(): return lax.all_to_all(x, axis, 0, 0, tiled=True)  16.8 us
    all_to_all x2, starting transfers between devices, exchange(): return lax.all_to_all(x, axis, 0, 0, tiled=True)  13.7 us
  transfers between devices with their start and end apart: 2, of which 2 were waited for; matrix products, arithmetic and copies ran while one was open for 0% of the time, Pallas kernels for 1%

profile of v7, /device:TPU:1, one launch (start us, length us, event | category | flops | bytes accessed | tf_op | source)
XLA Modules:
  0.0 211.1 jit_solution(15477935565776321292)
XLA Ops:
  0.6 0.0 copy-start.1
  0.6 0.1 pad_add_fusion.me
  0.7 0.0 copy-start
  0.7 0.8 copy-done
  1.6 0.0 copy-start.2
  1.6 1.2 shard_map.58
  2.8 23.9 %all_to_all.65.got = bf16[16,96,128]{2,1,0:T(8,128)(2,1)S(1)} all-to-all(bf16[16,96,128]{2,1,0:T(8,128)(2,1)S(1)} %get-tuple-element.26), channel_id=1, replica_groups=mesh['chips'=32,'samples'=16] {'samples'}, dimensions={0} | all-to-all | bytes 786432 | tf_op jit(solution)/shard_map/all_to_all | solution.py:457
  26.7 4.3 %shard_map.59 = bf16[32,40,128]{2,1,0:T(8,128)(2,1)S(1)} custom-call(s32[2]{0:T(128)S(1)} %pad_add_fusion.me, bf16[16,96,128]{2,1,0:T(8,128)(2,1)S(1)} %all_to_all.65.got, bf16[2304,1024]{1,0:T(8,128)(2,1)} %tel.9), custom_call_target="tpu_custom_call" | custom-call | flops 301989888 | bytes 4718592 | tf_op jit(solution)/shard_map/pallas_call | solution.py:445
  31.0 24.8 %all_to_all.66.got = bf16[32,40,128]{2,1,0:T(8,128)(2,1)S(1)} all-to-all(bf16[32,40,128]{2,1,0:T(8,128)(2,1)S(1)} %shard_map.59), channel_id=1, replica_groups=mesh['chips'=32,'samples'=16] {'chips'}, dimensions={0} | all-to-all | bytes 655360 | tf_op jit(solution)/shard_map/all_to_all | solution.py:457
  55.8 0.0 copy-done.1
  55.8 1.0 shard_map.60
  56.9 15.6 %all_to_all.67.got = bf16[32,32,128]{2,1,0:T(8,128)(2,1)S(1)} all-to-all(bf16[32,32,128]{2,1,0:T(8,128)(2,1)S(1)} %get-tuple-element.27), channel_id=1, replica_groups=mesh['chips'=32,'samples'=16] {'chips'}, dimensions={0} | all-to-all | bytes 524288 | tf_op jit(solution)/shard_map/all_to_all | solution.py:457
  72.4 0.0 copy-done.2
  72.4 3.1 %shard_map.61 = bf16[16,96,128]{2,1,0:T(8,128)(2,1)S(1)} custom-call(s32[2]{0:T(128)S(1)} %pad_add_fusion.me, bf16[32,32,128]{2,1,0:T(8,128)(2,1)S(1)} %all_to_all.67.got, bf16[2304,1024]{1,0:T(8,128)(2,1)S(1)} %copy-done.2), custom_call_target="tpu_custom_call" | custom-call | flops 301989888 | bytes 4718592 | tf_op jit(solution)/shard_map/pallas_call | solution.py:445
  75.5 15.0 %all_to_all.68.got = bf16[16,96,128]{2,1,0:T(8,128)(2,1)S(1)} all-to-all(bf16[16,96,128]{2,1,0:T(8,128)(2,1)S(1)} %shard_map.61), channel_id=1, replica_groups=mesh['chips'=32,'samples'=16] {'samples'}, dimensions={0} | all-to-all | bytes 786432 | tf_op jit(solution)/shard_map/all_to_all | solution.py:457
  90.5 2.3 %shard_map.62 = (f32[144,64]{1,0:T(8,128)S(1)}, bf16[16,96,128]{2,1,0:T(8,128)(2,1)S(1)}) custom-call(s32[2]{0:T(128)S(1)} %pad_add_fusion.me, bf16[16,96,128]{2,1,0:T(8,128)(2,1)S(1)} %all_to_all.68.got, f32[144,64]{1,0:T(8,128)S(1)} %get-tuple-element.28.w), custom_call_target="tpu_custom_call" | custom-call | tf_op jit(solution)/shard_map/pallas_call | solution.py:445
  92.8 16.7 %all_to_all.69.got = bf16[16,96,128]{2,1,0:T(8,128)(2,1)S(1)} all-to-all(bf16[16,96,128]{2,1,0:T(8,128)(2,1)S(1)} %get-tuple-element.29), channel_id=1, replica_groups=mesh['chips'=32,'samples'=16] {'samples'}, dimensions={0} | all-to-all | bytes 786432 | tf_op jit(solution)/shard_map/all_to_all | solution.py:457
  109.5 2.7 %shard_map.63 = bf16[32,40,128]{2,1,0:T(8,128)(2,1)S(1)} custom-call(s32[2]{0:T(128)S(1)} %pad_add_fusion.me, bf16[16,96,128]{2,1,0:T(8,128)(2,1)S(1)} %all_to_all.69.got, bf16[2304,1024]{1,0:T(8,128)(2,1)S(1)} %copy-done.2), custom_call_target="tpu_custom_call" | custom-call | flops 301989888 | bytes 4718592 | tf_op jit(solution)/shard_map/pallas_call | solution.py:445
  112.2 22.9 %all_to_all.70.got = bf16[32,40,128]{2,1,0:T(8,128)(2,1)S(1)} all-to-all(bf16[32,40,128]{2,1,0:T(8,128)(2,1)S(1)} %shard_map.63), channel_id=1, replica_groups=mesh['chips'=32,'samples'=16] {'chips'}, dimensions={0} | all-to-all | bytes 655360 | tf_op jit(solution)/shard_map/all_to_all | solution.py:457
  135.1 1.5 shard_map.64
  136.7 15.6 %all_to_all.71.got = bf16[32,32,128]{2,1,0:T(8,128)(2,1)S(1)} all-to-all(bf16[32,32,128]{2,1,0:T(8,128)(2,1)S(1)} %get-tuple-element.31), channel_id=1, replica_groups=mesh['chips'=32,'samples'=16] {'chips'}, dimensions={0} | all-to-all | bytes 524288 | tf_op jit(solution)/shard_map/all_to_all | solution.py:457
  152.2 3.9 %shard_map.65 = bf16[16,128,128]{2,1,0:T(8,128)(2,1)} custom-call(s32[2]{0:T(128)S(1)} %pad_add_fusion.me, bf16[32,32,128]{2,1,0:T(8,128)(2,1)S(1)} %all_to_all.71.got, bf16[2304,1024]{1,0:T(8,128)(2,1)S(1)} %copy-done.2), custom_call_target="tpu_custom_call" | custom-call | flops 301989888 | bytes 4718592 | tf_op jit(solution)/shard_map/pallas_call | solution.py:445
  156.1 4.0 %all-to-all-start.10 = ((bf16[16,128,128]{2,1,0:T(8,128)(2,1)}), bf16[16,128,128]{2,1,0:T(8,128)(2,1)S(1)}, u32[]{:S(2)}, u32[]{:S(2)}) async-start(bf16[16,128,128]{2,1,0:T(8,128)(2,1)} %shard_map.65), calls=%async_computation.10 | async-start | bytes 1048576 | tf_op jit(solution)/shard_map/all_to_all | solution.py:457
  160.1 2.8 %shard_map.66.energy = f32[1,128]{1,0:T(1,128)S(1)} custom-call(bf16[2304,1024]{1,0:T(8,128)(2,1)} %tel.9), custom_call_target="tpu_custom_call" | custom-call | flops 4718592 | bytes 4718592 | tf_op jit(solution)/shard_map/pallas_call | solution.py:445
  163.0 9.8 %all-to-all-done.10.got = bf16[16,128,128]{2,1,0:T(8,128)(2,1)S(1)} async-done(((bf16[16,128,128]{2,1,0:T(8,128)(2,1)}), bf16[16,128,128]{2,1,0:T(8,128)(2,1)S(1)}, u32[]{:S(2)}, u32[]{:S(2)}) %all-to-all-start.10) | async-done | bytes 524320 | tf_op jit(solution)/shard_map/all_to_all | solution.py:457
  172.7 1.6 shard_map.67
  174.3 14.3 %all_to_all.72 = f32[16,1,128]{2,1,0:T(1,128)S(1)} all-to-all(f32[16,1,128]{2,1,0:T(1,128)S(1)} %get-tuple-element.35), channel_id=1, replica_groups=mesh['chips'=32,'samples'=16] {'samples'}, dimensions={0} | all-to-all | bytes 16384 | tf_op jit(solution)/shard_map/all_to_all | solution.py:457
  188.7 0.6 broadcast_in_dim.4
  189.3 9.6 %all-to-all-start.12 = ((f32[32,1,128]{2,1,0:T(1,128)}), f32[32,1,128]{2,1,0:T(1,128)S(1)}, u32[]{:S(2)}, u32[]{:S(2)}) async-start(f32[32,1,128]{2,1,0:T(1,128)} %broadcast_in_dim.4), calls=%async_computation.12 | async-start | bytes 32768 | tf_op jit(solution)/shard_map/all_to_all | solution.py:457
  198.9 0.7 copy.10
  199.6 7.1 %all-to-all-done.12 = f32[32,1,128]{2,1,0:T(1,128)S(1)} async-done(((f32[32,1,128]{2,1,0:T(1,128)}), f32[32,1,128]{2,1,0:T(1,128)S(1)}, u32[]{:S(2)}, u32[]{:S(2)}) %all-to-all-start.12) | async-done | bytes 16416 | tf_op jit(solution)/shard_map/all_to_all | solution.py:457
  206.7 0.6 fusion
  (3 shorter events, 0.1 us)
Async XLA Ops:
  0.6 55.2 %copy-start.1 = (f32[64,32]{0,1:T(8,128)S(1)}, f32[64,32]{0,1:T(8,128)}, u32[]{:S(2)}) copy-start(f32[64,32]{0,1:T(8,128)} %param.7) | copy-start | bytes 24580
  0.7 0.8 copy-start
  1.6 70.9 %copy-start.2 = (bf16[2304,1024]{1,0:T(8,128)(2,1)S(1)}, bf16[2304,1024]{1,0:T(8,128)(2,1)}, u32[]{:S(2)}) copy-start(bf16[2304,1024]{1,0:T(8,128)(2,1)} %tel.9) | copy-start | bytes 14155780
  156.1 16.6 %all-to-all-start.10 = ((bf16[16,128,128]{2,1,0:T(8,128)(2,1)}), bf16[16,128,128]{2,1,0:T(8,128)(2,1)S(1)}, u32[]{:S(2)}, u32[]{:S(2)}) async-start(bf16[16,128,128]{2,1,0:T(8,128)(2,1)} %shard_map.65), calls=%async_computation.10 | async-start | bytes 1048576 | tf_op jit(solution)/shard_map/all_to_all | solution.py:457
  189.3 17.5 %all-to-all-start.12 = ((f32[32,1,128]{2,1,0:T(1,128)}), f32[32,1,128]{2,1,0:T(1,128)S(1)}, u32[]{:S(2)}, u32[]{:S(2)}) async-start(f32[32,1,128]{2,1,0:T(1,128)} %broadcast_in_dim.4), calls=%async_computation.12 | async-start | bytes 32768 | tf_op jit(solution)/shard_map/all_to_all | solution.py:457

commit v8 on v7

--- a/solution.py
+++ b/solution.py
@@ -21,7 +21,8 @@
 W_OWN = ROWS // SAMPLES
 H_OWN = COLS // CHIPS
 H_WIDTH = 256
-W_STEP = 16
+PARTS = 2
+TOUCH = 1152
 BLOCK = 16
 W_HALF = 80
 GRAM = 16
@@ -235,11 +236,24 @@
     copies(w_message(w, encode_gram(*gram, factor)), out)
 
 
-def start_kernel(me, w, w_out, out):
-    wide = jnp.concatenate([w[...], jnp.zeros((K, 256 - W_OWN), F32)], axis=1)
+def start_kernel(me, w, tel, w_out, out, touched, arrived, own, own_arrived):
+    touches = [
+        pltpu.make_async_copy(
+            tel.at[pl.ds(j * TOUCH, BLOCK)], touched.at[pl.ds(j * BLOCK, BLOCK)], arrived.at[j]
+        )
+        for j in range(ROWS // TOUCH)
+    ]
+    own_copy = pltpu.make_async_copy(w, own, own_arrived)
+    own_copy.start()
+    for copy in touches:
+        copy.start()
+    own_copy.wait()
+    wide = jnp.concatenate([own[...], jnp.zeros((K, 256 - W_OWN), F32)], axis=1)
     turned = wide.T[:W_OWN]
     w_out[...] = turned
     fill_w(turned, sample_factor(me[1]), out)
+    for copy in touches:
+        copy.wait()
 
 
 def h_numer_kernel(me, got, tel, out, tile, w_turned, w_all, arrived):
@@ -317,15 +331,17 @@
     copies(split(new), out)
 
 
-def w_numer_kernel(me, got, tel, out, tile, arrived):
-    block = W_STEP * W_OWN
-
-    def copy(b):
-        rows = pl.ds(pl.multiple_of(b * block, block), block)
-        return pltpu.make_async_copy(tel.at[rows], tile.at[rows], arrived.at[b])
-
-    for b in range(ROWS // block):
-        copy(b).start()
+def w_numer(me, got, tel, out, tile, arrived, energy=None):
+    parts = arrived.shape[0]
+    block = ROWS // parts
+    copies_in = [
+        pltpu.make_async_copy(
+            tel.at[pl.ds(b * block, block)], tile.at[pl.ds(b * block, block)], arrived.at[b]
+        )
+        for b in range(parts)
+    ]
+    for copy in copies_in:
+        copy.start()
     halves = got[...].reshape(COLS, 128)
     four = products(halves)
     factor = sample_factor(me[1])
@@ -333,20 +349,33 @@
     last = out.shape[1] > W_MSG
     if last:
         pair = pair_of(four[:K, :K])
-    high = halves[:, :K]
-
-    def step(b, carry):
-        copy(b).wait()
-        rows = pl.ds(pl.multiple_of(b * block, block), block)
-        part = jnp.dot(tile[rows, :], high, preferred_element_type=F32)
-        for q in range(W_STEP):
-            message = sums_message(part[q * W_OWN : (q + 1) * W_OWN], gram, factor)
-            if last:
-                message = jnp.concatenate([message, pair], axis=0)
-            out[b * W_STEP + q] = message
-        return carry
-
-    lax.fori_loop(0, ROWS // block, step, 0)
+    squares_sum = jnp.zeros((8, COLS), F32)
+    for b, copy in enumerate(copies_in):
+        copy.wait()
+        if energy is not None:
+
+            def add(i, total):
+                rows = pl.ds(pl.multiple_of(b * block + i * W_OWN, W_OWN), W_OWN)
+                values = tile[rows, :].astype(F32)
+                return total + jnp.sum((values * values).reshape(W_OWN // 8, 8, COLS), axis=0)
+
+            squares_sum = lax.fori_loop(0, block // W_OWN, add, squares_sum)
+    if energy is not None:
+        energy[...] = jnp.full((1, 128), jnp.sum(squares_sum), F32)
+    sums = jnp.dot(tile[...], halves[:, :K], preferred_element_type=F32)
+    for q in range(SAMPLES):
+        message = sums_message(sums[q * W_OWN : (q + 1) * W_OWN], gram, factor)
+        if last:
+            message = jnp.concatenate([message, pair], axis=0)
+        out[q] = message
+
+
+def w_numer_kernel(me, got, tel, out, tile, arrived):
+    w_numer(me, got, tel, out, tile, arrived)
+
+
+def w_numer_energy_kernel(me, got, tel, out, energy, tile, arrived):
+    w_numer(me, got, tel, out, tile, arrived, energy)
 
 
 def w_new(got, w):
@@ -395,14 +424,17 @@
     copies(pair, out)
 
 
-def energy_kernel(tel, out):
-    def step(i, energy):
-        rows = pl.ds(pl.multiple_of(i * W_OWN, W_OWN), W_OWN)
-        values = tel[rows, :].astype(F32)
-        return energy + jnp.sum((values * values).reshape(W_OWN // 8, 8, COLS), axis=0)
-
-    energy = lax.fori_loop(0, SAMPLES, step, jnp.zeros((8, COLS), F32))
-    out[...] = jnp.full((1, 128), jnp.sum(energy), F32)
+def share_kernel(got, out):
+    copies(jnp.sum(got[...], axis=0), out)
+
+
+def ratio_kernel(got, ratio, close, total_out):
+    sums = jnp.sum(got[...], axis=0)
+    total = sums[:, K : K + 1]
+    expanded = sums[:, :1] + total
+    ratio[0, 0] = jnp.sum(jnp.sqrt(jnp.maximum(expanded, 0.0) / total))
+    close[0, 0] = jnp.sum((expanded < 0.02 * total).astype(F32)).astype(jnp.int32)
+    total_out[0, 0] = jnp.sum(total)
 
 
 def last_rows_kernel(w, out):
@@ -438,15 +470,14 @@
 PRODUCT = pl.CostEstimate(
     flops=2 * K * ROWS * COLS, bytes_accessed=2 * ROWS * COLS, transcendentals=0
 )
-ENERGY = pl.CostEstimate(flops=2 * ROWS * COLS, bytes_accessed=2 * ROWS * COLS, transcendentals=0)
-
-
-def call(kernel, inputs, outs, cost=None, specs=None, scratch=()):
+
+
+def call(kernel, inputs, outs, cost=None, specs=None, scratch=(), out_spec=VMEM):
     return pl.pallas_call(
         kernel,
         out_shape=[jax.ShapeDtypeStruct(shape, dtype) for shape, dtype in outs],
         in_specs=[VMEM] * len(inputs) if specs is None else specs,
-        out_specs=[VMEM] * len(outs),
+        out_specs=[out_spec] * len(outs),
         scratch_shapes=list(scratch),
         compiler_params=LIMIT,
         cost_estimate=cost,
@@ -468,9 +499,21 @@
     tile = pltpu.VMEM((ROWS, COLS), BF16)
     h = sample_factors.T
     w_sent = [((W_OWN, K), F32), ((SAMPLES, W_MSG, 128), BF16)]
-    w, sent = call(start_kernel, (me, chip_factors), w_sent, None, [SMEM, VMEM])
+    touches = ROWS // TOUCH
+    w, sent = call(
+        start_kernel,
+        (me, chip_factors, telemetry),
+        w_sent,
+        None,
+        [SMEM, HBM, HBM],
+        [
+            pltpu.VMEM((touches * BLOCK, COLS), BF16),
+            pltpu.SemaphoreType.DMA((touches,)),
+            pltpu.VMEM((K, W_OWN), F32),
+            pltpu.SemaphoreType.DMA,
+        ],
+    )
     got_w = exchange(sent, "samples")
-    (energy,) = call(energy_kernel, (telemetry,), [((1, 128), F32)], ENERGY)
     for sweep in range(ITERS):
         last = sweep == ITERS - 1
         (sent,) = call(
@@ -491,14 +534,21 @@
             h_update_kernel, (got, h), [((H_OWN, K), F32), ((CHIPS, H_OWN, 128), BF16)]
         )
         got_h = exchange(sent, "chips")
-        (sent,) = call(
-            w_numer_kernel,
-            (me, got_h, telemetry),
-            [((SAMPLES, W_MSG + PAIR if last else W_MSG, 128), BF16)],
-            PRODUCT,
-            [SMEM, VMEM, HBM],
-            [tile, pltpu.SemaphoreType.DMA((SAMPLES // W_STEP,))],
-        )
+        w_sums = [((SAMPLES, W_MSG + PAIR if last else W_MSG, 128), BF16)]
+        specs, scratch = [SMEM, VMEM, HBM], [tile, pltpu.SemaphoreType.DMA((PARTS,))]
+        if sweep == 0:
+            sent, energy = call(
+                w_numer_energy_kernel,
+                (me, got_h, telemetry),
+                [*w_sums, ((1, 128), F32)],
+                PRODUCT,
+                specs,
+                scratch,
+            )
+        else:
+            (sent,) = call(
+                w_numer_kernel, (me, got_h, telemetry), w_sums, PRODUCT, specs, scratch
+            )
         got = exchange(sent, "samples")
         if not last:
             w, sent = call(
@@ -512,11 +562,17 @@
     w, shares = call(
         w_last_kernel, (got, w, energy), [((W_OWN, K), F32), ((SAMPLES, 1, 128), F32)]
     )
-    sums = sum_everywhere(shares)
-    total = sums[0, K]
-    expanded = sums[0, 0] + total
-
-    def direct(w, got_h, telemetry):
+    (shares,) = call(
+        share_kernel, (exchange(shares, "samples"),), [((CHIPS, 1, 128), F32)]
+    )
+    ratio, close, total = call(
+        ratio_kernel,
+        (exchange(shares, "chips"),),
+        [((1, 1), F32), ((1, 1), jnp.int32), ((1, 1), F32)],
+        out_spec=SMEM,
+    )
+
+    def direct(ratio, total, w, got_h, telemetry):
         (sent,) = call(last_rows_kernel, (w,), [((SAMPLES, W_HALF, 128), BF16)])
         (shares,) = call(
             error_kernel,
@@ -524,17 +580,19 @@
             [((SAMPLES, 1, 128), F32)],
             PRODUCT,
         )
-        return sum_everywhere(shares)[0, 0]
-
-    fit_error = lax.cond(
-        expanded < 0.02 * total,
+        return jnp.sqrt(sum_everywhere(shares)[:1, :1] / total)
+
+    ratio = lax.cond(
+        close[0, 0] > 0,
         direct,
-        lambda *operands: expanded,
+        lambda ratio, *operands: ratio,
+        ratio,
+        total,
         w,
         got_h,
         telemetry,
     )
-    return w.T, h.T, jnp.sqrt(fit_error / total)
+    return w.T, h.T, ratio[0, 0]
 
 
 def solution(mesh):

time: 212 us -> 207 us (0.976)
  blocking collectives: 149 us -> 165 us
  waiting for transfers between devices: 16.8 us -> 7.08 us
  starting transfers between devices: 13.7 us -> 9.65 us
  between operations: 4.52 us -> 1.35 us
  Pallas kernels: 24.3 us -> 21.4 us
    all_to_all x8 -> x9, blocking collectives: 149 us -> 165 us  [exchange(): return lax.all_to_all(x, axis, 0, 0, tiled=True)]
    all_to_all x2 -> x1, waiting for transfers between devices: 16.8 us -> 7.08 us  [exchange(): return lax.all_to_all(x, axis, 0, 0, tiled=True)]
    all_to_all x2 -> x1, starting transfers between devices: 13.7 us -> 9.65 us  [exchange(): return lax.all_to_all(x, axis, 0, 0, tiled=True)]
    pallas_call x10 -> x11, Pallas kernels: 24.3 us -> 21.4 us  [call(): pl.pallas_call(kernel, out_shape=[jax.ShapeDtypeStruct(shape, dtype) for...]
  transfers between devices with their start and end apart: 2 -> 1, of which waited for: 2 -> 1; matrix products, arithmetic and copies ran while one was open for 0% -> 0% of each run, Pallas kernels for 1% -> 0%
where the time goes in v8:
time: 207 us; the launch traced here: 206 us
  blocking collectives  165 us (80%)
  Pallas kernels  21.4 us (10%)
  starting transfers between devices  9.65 us (5%)
  waiting for transfers between devices  7.08 us (3%)
    all_to_all x9, blocking collectives, exchange(): return lax.all_to_all(x, axis, 0, 0, tiled=True)  165 us
    pallas_call x11, Pallas kernels, call(): pl.pallas_call(kernel, out_shape=[jax.ShapeDtypeStruct(shape, dtype) for...  21.4 us
    all_to_all x1, starting transfers between devices, exchange(): return lax.all_to_all(x, axis, 0, 0, tiled=True)  9.65 us
    all_to_all x1, waiting for transfers between devices, exchange(): return lax.all_to_all(x, axis, 0, 0, tiled=True)  7.08 us
  transfers between devices with their start and end apart: 1, of which 1 were waited for; matrix products, arithmetic and copies ran while one was open for 0% of the time, Pallas kernels for 0%

profile of v8, /device:TPU:1, one launch (start us, length us, event | category | flops | bytes accessed | tf_op | source)
XLA Modules:
  0.0 206.2 jit_solution(13715977869077223911)
XLA Ops:
  0.6 0.1 pad_add_fusion.me
  0.7 0.0 copy-start
  0.7 0.8 copy-done
  1.6 0.0 copy-start.2
  1.6 0.0 copy-start.1
  1.6 1.7 shard_map.58
  3.3 23.8 %all_to_all.65.got = bf16[16,96,128]{2,1,0:T(8,128)(2,1)S(1)} all-to-all(bf16[16,96,128]{2,1,0:T(8,128)(2,1)S(1)} %get-tuple-element.40), channel_id=1, replica_groups=mesh['chips'=32,'samples'=16] {'samples'}, dimensions={0} | all-to-all | bytes 786432 | tf_op jit(solution)/shard_map/all_to_all | solution.py:488
  27.1 0.0 copy-done.2
  27.1 2.7 %shard_map.59 = bf16[32,40,128]{2,1,0:T(8,128)(2,1)S(1)} custom-call(s32[2]{0:T(128)S(1)} %pad_add_fusion.me, bf16[16,96,128]{2,1,0:T(8,128)(2,1)S(1)} %all_to_all.65.got, bf16[2304,1024]{1,0:T(8,128)(2,1)S(1)} %copy-done.2), custom_call_target="tpu_custom_call" | custom-call | flops 301989888 | bytes 4718592 | tf_op jit(solution)/shard_map/pallas_call | solution.py:476
  29.8 24.8 %all_to_all.66.got = bf16[32,40,128]{2,1,0:T(8,128)(2,1)S(1)} all-to-all(bf16[32,40,128]{2,1,0:T(8,128)(2,1)S(1)} %shard_map.59), channel_id=1, replica_groups=mesh['chips'=32,'samples'=16] {'chips'}, dimensions={0} | all-to-all | bytes 655360 | tf_op jit(solution)/shard_map/all_to_all | solution.py:488
  54.6 0.0 copy-done.1
  54.6 1.0 shard_map.60
  55.7 15.6 %all_to_all.67.got = bf16[32,32,128]{2,1,0:T(8,128)(2,1)S(1)} all-to-all(bf16[32,32,128]{2,1,0:T(8,128)(2,1)S(1)} %get-tuple-element.41), channel_id=1, replica_groups=mesh['chips'=32,'samples'=16] {'chips'}, dimensions={0} | all-to-all | bytes 524288 | tf_op jit(solution)/shard_map/all_to_all | solution.py:488
  71.2 3.5 %shard_map.61 = (bf16[16,96,128]{2,1,0:T(8,128)(2,1)S(1)}, f32[1,128]{1,0:T(1,128)S(1)}) custom-call(s32[2]{0:T(128)S(1)} %pad_add_fusion.me, bf16[32,32,128]{2,1,0:T(8,128)(2,1)S(1)} %all_to_all.67.got, bf16[2304,1024]{1,0:T(8,128)(2,1)S(1)} %copy-done.2), custom_call_target="tpu_custom_call" | custom-call | flops 301989888 | bytes 4718592 | tf_op jit(solution)/shard_map/pallas_call | solution.py:476
  74.7 15.0 %all_to_all.68.got = bf16[16,96,128]{2,1,0:T(8,128)(2,1)S(1)} all-to-all(bf16[16,96,128]{2,1,0:T(8,128)(2,1)S(1)} %get-tuple-element.42), channel_id=1, replica_groups=mesh['chips'=32,'samples'=16] {'samples'}, dimensions={0} | all-to-all | bytes 786432 | tf_op jit(solution)/shard_map/all_to_all | solution.py:488
  89.7 2.3 %shard_map.62 = (f32[144,64]{1,0:T(8,128)S(1)}, bf16[16,96,128]{2,1,0:T(8,128)(2,1)S(1)}) custom-call(s32[2]{0:T(128)S(1)} %pad_add_fusion.me, bf16[16,96,128]{2,1,0:T(8,128)(2,1)S(1)} %all_to_all.68.got, f32[144,64]{1,0:T(8,128)S(1)} %get-tuple-element.43.w), custom_call_target="tpu_custom_call" | custom-call | tf_op jit(solution)/shard_map/pallas_call | solution.py:476
  92.0 16.7 %all_to_all.69.got = bf16[16,96,128]{2,1,0:T(8,128)(2,1)S(1)} all-to-all(bf16[16,96,128]{2,1,0:T(8,128)(2,1)S(1)} %get-tuple-element.44), channel_id=1, replica_groups=mesh['chips'=32,'samples'=16] {'samples'}, dimensions={0} | all-to-all | bytes 786432 | tf_op jit(solution)/shard_map/all_to_all | solution.py:488
  108.7 2.7 %shard_map.63 = bf16[32,40,128]{2,1,0:T(8,128)(2,1)S(1)} custom-call(s32[2]{0:T(128)S(1)} %pad_add_fusion.me, bf16[16,96,128]{2,1,0:T(8,128)(2,1)S(1)} %all_to_all.69.got, bf16[2304,1024]{1,0:T(8,128)(2,1)S(1)} %copy-done.2), custom_call_target="tpu_custom_call" | custom-call | flops 301989888 | bytes 4718592 | tf_op jit(solution)/shard_map/pallas_call | solution.py:476
  111.4 22.9 %all_to_all.70.got = bf16[32,40,128]{2,1,0:T(8,128)(2,1)S(1)} all-to-all(bf16[32,40,128]{2,1,0:T(8,128)(2,1)S(1)} %shard_map.63), channel_id=1, replica_groups=mesh['chips'=32,'samples'=16] {'chips'}, dimensions={0} | all-to-all | bytes 655360 | tf_op jit(solution)/shard_map/all_to_all | solution.py:488
  134.3 1.5 shard_map.64
  135.8 15.6 %all_to_all.71.got = bf16[32,32,128]{2,1,0:T(8,128)(2,1)S(1)} all-to-all(bf16[32,32,128]{2,1,0:T(8,128)(2,1)S(1)} %get-tuple-element.46), channel_id=1, replica_groups=mesh['chips'=32,'samples'=16] {'chips'}, dimensions={0} | all-to-all | bytes 524288 | tf_op jit(solution)/shard_map/all_to_all | solution.py:488
  151.4 3.1 %shard_map.65 = bf16[16,128,128]{2,1,0:T(8,128)(2,1)S(1)} custom-call(s32[2]{0:T(128)S(1)} %pad_add_fusion.me, bf16[32,32,128]{2,1,0:T(8,128)(2,1)S(1)} %all_to_all.71.got, bf16[2304,1024]{1,0:T(8,128)(2,1)S(1)} %copy-done.2), custom_call_target="tpu_custom_call" | custom-call | flops 301989888 | bytes 4718592 | tf_op jit(solution)/shard_map/pallas_call | solution.py:476
  154.5 16.4 %all_to_all.72.got = bf16[16,128,128]{2,1,0:T(8,128)(2,1)S(1)} all-to-all(bf16[16,128,128]{2,1,0:T(8,128)(2,1)S(1)} %shard_map.65), channel_id=1, replica_groups=mesh['chips'=32,'samples'=16] {'samples'}, dimensions={0} | all-to-all | bytes 1048576 | tf_op jit(solution)/shard_map/all_to_all | solution.py:488
  170.9 1.6 shard_map.66
  172.5 14.3 %all_to_all.73.got = f32[16,1,128]{2,1,0:T(1,128)S(1)} all-to-all(f32[16,1,128]{2,1,0:T(1,128)S(1)} %get-tuple-element.51), channel_id=1, replica_groups=mesh['chips'=32,'samples'=16] {'samples'}, dimensions={0} | all-to-all | bytes 16384 | tf_op jit(solution)/shard_map/all_to_all | solution.py:488
  186.8 0.6 shard_map.67
  187.4 9.6 %all-to-all-start.12 = ((f32[32,1,128]{2,1,0:T(1,128)}), f32[32,1,128]{2,1,0:T(1,128)S(1)}, u32[]{:S(2)}, u32[]{:S(2)}) async-start(f32[32,1,128]{2,1,0:T(1,128)} %shard_map.67), calls=%async_computation.12 | async-start | bytes 32768 | tf_op jit(solution)/shard_map/all_to_all | solution.py:488
  197.1 0.7 copy.9
  197.8 7.1 %all-to-all-done.12.got = f32[32,1,128]{2,1,0:T(1,128)S(1)} async-done(((f32[32,1,128]{2,1,0:T(1,128)}), f32[32,1,128]{2,1,0:T(1,128)S(1)}, u32[]{:S(2)}, u32[]{:S(2)}) %all-to-all-start.12) | async-done | bytes 16416 | tf_op jit(solution)/shard_map/all_to_all | solution.py:488
  204.9 0.7 shard_map.68
  (1 shorter events, 0.0 us)
Async XLA Ops:
  0.7 0.8 copy-start
  1.6 25.5 %copy-start.2 = (bf16[2304,1024]{1,0:T(8,128)(2,1)S(1)}, bf16[2304,1024]{1,0:T(8,128)(2,1)}, u32[]{:S(2)}) copy-start(bf16[2304,1024]{1,0:T(8,128)(2,1)} %tel.9) | copy-start | bytes 14155780
  1.6 53.1 %copy-start.1 = (f32[64,32]{0,1:T(8,128)S(1)}, f32[64,32]{0,1:T(8,128)}, u32[]{:S(2)}) copy-start(f32[64,32]{0,1:T(8,128)} %param.7) | copy-start | bytes 24580
  187.4 17.5 %all-to-all-start.12 = ((f32[32,1,128]{2,1,0:T(1,128)}), f32[32,1,128]{2,1,0:T(1,128)S(1)}, u32[]{:S(2)}, u32[]{:S(2)}) async-start(f32[32,1,128]{2,1,0:T(1,128)} %shard_map.67), calls=%async_computation.12 | async-start | bytes 32768 | tf_op jit(solution)/shard_map/all_to_all | solution.py:488

commit v9 on v8

--- a/solution.py
+++ b/solution.py
@@ -21,8 +21,6 @@
 W_OWN = ROWS // SAMPLES
 H_OWN = COLS // CHIPS
 H_WIDTH = 256
-PARTS = 2
-TOUCH = 1152
 BLOCK = 16
 W_HALF = 80
 GRAM = 16
@@ -236,29 +234,15 @@
     copies(w_message(w, encode_gram(*gram, factor)), out)
 
 
-def start_kernel(me, w, tel, w_out, out, touched, arrived, own, own_arrived):
-    touches = [
-        pltpu.make_async_copy(
-            tel.at[pl.ds(j * TOUCH, BLOCK)], touched.at[pl.ds(j * BLOCK, BLOCK)], arrived.at[j]
-        )
-        for j in range(ROWS // TOUCH)
-    ]
-    own_copy = pltpu.make_async_copy(w, own, own_arrived)
-    own_copy.start()
-    for copy in touches:
-        copy.start()
-    own_copy.wait()
-    wide = jnp.concatenate([own[...], jnp.zeros((K, 256 - W_OWN), F32)], axis=1)
+def start_kernel(me, w, tel, w_out, out):
+    del tel
+    wide = jnp.concatenate([w[...], jnp.zeros((K, 256 - W_OWN), F32)], axis=1)
     turned = wide.T[:W_OWN]
     w_out[...] = turned
     fill_w(turned, sample_factor(me[1]), out)
-    for copy in touches:
-        copy.wait()
-
-
-def h_numer_kernel(me, got, tel, out, tile, w_turned, w_all, arrived):
-    copy = pltpu.make_async_copy(tel, tile, arrived)
-    copy.start()
+
+
+def h_numer_kernel(me, got, tile, out, w_turned, w_all):
 
     def gather(i, carry):
         gram, diagonal = carry
@@ -280,7 +264,6 @@
     coded, ends, power = encode_gram(one_above(gram), diagonal[:, K : K + 32], factor)
     ends = jnp.concatenate([ends, jnp.zeros((1, 96), F32)], axis=1)
     power = jnp.broadcast_to(power, (1, 128))
-    copy.wait()
     per = H_WIDTH // H_OWN
 
     def step(n, carry):
@@ -331,17 +314,7 @@
     copies(split(new), out)
 
 
-def w_numer(me, got, tel, out, tile, arrived, energy=None):
-    parts = arrived.shape[0]
-    block = ROWS // parts
-    copies_in = [
-        pltpu.make_async_copy(
-            tel.at[pl.ds(b * block, block)], tile.at[pl.ds(b * block, block)], arrived.at[b]
-        )
-        for b in range(parts)
-    ]
-    for copy in copies_in:
-        copy.start()
+def w_numer(me, got, tile, out, energy=None):
     halves = got[...].reshape(COLS, 128)
     four = products(halves)
     factor = sample_factor(me[1])
@@ -349,18 +322,14 @@
     last = out.shape[1] > W_MSG
     if last:
         pair = pair_of(four[:K, :K])
-    squares_sum = jnp.zeros((8, COLS), F32)
-    for b, copy in enumerate(copies_in):
-        copy.wait()
-        if energy is not None:
-
-            def add(i, total):
-                rows = pl.ds(pl.multiple_of(b * block + i * W_OWN, W_OWN), W_OWN)
-                values = tile[rows, :].astype(F32)
-                return total + jnp.sum((values * values).reshape(W_OWN // 8, 8, COLS), axis=0)
-
-            squares_sum = lax.fori_loop(0, block // W_OWN, add, squares_sum)
     if energy is not None:
+
+        def add(i, total):
+            rows = pl.ds(pl.multiple_of(i * W_OWN, W_OWN), W_OWN)
+            values = tile[rows, :].astype(F32)
+            return total + jnp.sum((values * values).reshape(W_OWN // 8, 8, COLS), axis=0)
+
+        squares_sum = lax.fori_loop(0, SAMPLES, add, jnp.zeros((8, COLS), F32))
         energy[...] = jnp.full((1, 128), jnp.sum(squares_sum), F32)
     sums = jnp.dot(tile[...], halves[:, :K], preferred_element_type=F32)
     for q in range(SAMPLES):
@@ -370,12 +339,12 @@
         out[q] = message
 
 
-def w_numer_kernel(me, got, tel, out, tile, arrived):
-    w_numer(me, got, tel, out, tile, arrived)
-
-
-def w_numer_energy_kernel(me, got, tel, out, energy, tile, arrived):
-    w_numer(me, got, tel, out, tile, arrived, energy)
+def w_numer_kernel(me, got, tile, out):
+    w_numer(me, got, tile, out)
+
+
+def w_numer_energy_kernel(me, got, tile, out, energy):
+    w_numer(me, got, tile, out, energy)
 
 
 def w_new(got, w):
@@ -496,22 +465,11 @@
 
 def body(telemetry, chip_factors, sample_factors):
     me = jnp.stack([lax.axis_index("chips"), lax.axis_index("samples")])
-    tile = pltpu.VMEM((ROWS, COLS), BF16)
+    specs = [SMEM, VMEM, VMEM]
     h = sample_factors.T
     w_sent = [((W_OWN, K), F32), ((SAMPLES, W_MSG, 128), BF16)]
-    touches = ROWS // TOUCH
     w, sent = call(
-        start_kernel,
-        (me, chip_factors, telemetry),
-        w_sent,
-        None,
-        [SMEM, HBM, HBM],
-        [
-            pltpu.VMEM((touches * BLOCK, COLS), BF16),
-            pltpu.SemaphoreType.DMA((touches,)),
-            pltpu.VMEM((K, W_OWN), F32),
-            pltpu.SemaphoreType.DMA,
-        ],
+        start_kernel, (me, chip_factors, telemetry), w_sent, None, [SMEM, VMEM, HBM]
     )
     got_w = exchange(sent, "samples")
     for sweep in range(ITERS):
@@ -521,13 +479,8 @@
             (me, got_w, telemetry),
             [((CHIPS, H_MSG, 128), BF16)],
             PRODUCT,
-            [SMEM, VMEM, HBM],
-            [
-                tile,
-                pltpu.VMEM((K, ROWS), BF16),
-                pltpu.VMEM((ROWS, K), F32),
-                pltpu.SemaphoreType.DMA,
-            ],
+            specs,
+            [pltpu.VMEM((K, ROWS), BF16), pltpu.VMEM((ROWS, K), F32)],
         )
         got = exchange(sent, "chips")
         h, sent = call(
@@ -535,7 +488,6 @@
         )
         got_h = exchange(sent, "chips")
         w_sums = [((SAMPLES, W_MSG + PAIR if last else W_MSG, 128), BF16)]
-        specs, scratch = [SMEM, VMEM, HBM], [tile, pltpu.SemaphoreType.DMA((PARTS,))]
         if sweep == 0:
             sent, energy = call(
                 w_numer_energy_kernel,
@@ -543,11 +495,10 @@
                 [*w_sums, ((1, 128), F32)],
                 PRODUCT,
                 specs,
-                scratch,
             )
         else:
             (sent,) = call(
-                w_numer_kernel, (me, got_h, telemetry), w_sums, PRODUCT, specs, scratch
+                w_numer_kernel, (me, got_h, telemetry), w_sums, PRODUCT, specs
             )
         got = exchange(sent, "samples")
         if not last:

time: 207 us -> 204 us (0.986)
  Pallas kernels: 21.4 us -> 18.4 us
    pallas_call x11, Pallas kernels: 21.4 us -> 18.4 us  [call(): pl.pallas_call(kernel, out_shape=[jax.ShapeDtypeStruct(shape, dtype) for...]
where the time goes in v9:
time: 204 us; the launch traced here: 203 us
  blocking collectives  165 us (81%)
  Pallas kernels  18.4 us (9%)
  starting transfers between devices  9.64 us (5%)
  waiting for transfers between devices  7.08 us (3%)
    all_to_all x9, blocking collectives, exchange(): return lax.all_to_all(x, axis, 0, 0, tiled=True)  165 us
    pallas_call x11, Pallas kernels, call(): pl.pallas_call(kernel, out_shape=[jax.ShapeDtypeStruct(shape, dtype) for...  18.4 us
    all_to_all x1, starting transfers between devices, exchange(): return lax.all_to_all(x, axis, 0, 0, tiled=True)  9.64 us
    all_to_all x1, waiting for transfers between devices, exchange(): return lax.all_to_all(x, axis, 0, 0, tiled=True)  7.08 us
  transfers between devices with their start and end apart: 1, of which 1 were waited for; matrix products, arithmetic and copies ran while one was open for 0% of the time, Pallas kernels for 0%

profile of v9, /device:TPU:1, one launch (start us, length us, event | category | flops | bytes accessed | tf_op | source)
XLA Modules:
  0.0 203.3 jit_solution(16973898742248327290)
XLA Ops:
  0.6 0.1 pad_add_fusion.me
  0.7 0.0 copy-start
  0.7 0.8 copy-done
  1.6 0.0 copy-start.2
  1.6 0.0 copy-start.1
  1.6 1.2 shard_map.58
  2.8 23.9 %all_to_all.65.got = bf16[16,96,128]{2,1,0:T(8,128)(2,1)S(1)} all-to-all(bf16[16,96,128]{2,1,0:T(8,128)(2,1)S(1)} %get-tuple-element.40), channel_id=1, replica_groups=mesh['chips'=32,'samples'=16] {'samples'}, dimensions={0} | all-to-all | bytes 786432 | tf_op jit(solution)/shard_map/all_to_all | solution.py:457
  26.7 0.0 copy-done.2
  26.7 2.0 shard_map.59
  28.7 24.8 %all_to_all.66.got = bf16[32,40,128]{2,1,0:T(8,128)(2,1)S(1)} all-to-all(bf16[32,40,128]{2,1,0:T(8,128)(2,1)S(1)} %shard_map.59), channel_id=1, replica_groups=mesh['chips'=32,'samples'=16] {'chips'}, dimensions={0} | all-to-all | bytes 655360 | tf_op jit(solution)/shard_map/all_to_all | solution.py:457
  53.6 0.0 copy-done.1
  53.6 1.0 shard_map.60
  54.6 15.6 %all_to_all.67.got = bf16[32,32,128]{2,1,0:T(8,128)(2,1)S(1)} all-to-all(bf16[32,32,128]{2,1,0:T(8,128)(2,1)S(1)} %get-tuple-element.41), channel_id=1, replica_groups=mesh['chips'=32,'samples'=16] {'chips'}, dimensions={0} | all-to-all | bytes 524288 | tf_op jit(solution)/shard_map/all_to_all | solution.py:457
  70.2 3.2 %shard_map.61 = (bf16[16,96,128]{2,1,0:T(8,128)(2,1)S(1)}, f32[1,128]{1,0:T(1,128)S(1)}) custom-call(s32[2]{0:T(128)S(1)} %pad_add_fusion.me, bf16[32,32,128]{2,1,0:T(8,128)(2,1)S(1)} %all_to_all.67.got, bf16[2304,1024]{1,0:T(8,128)(2,1)S(1)} %copy-done.2), custom_call_target="tpu_custom_call" | custom-call | flops 301989888 | bytes 4718592 | tf_op jit(solution)/shard_map/pallas_call | solution.py:445
  73.3 15.0 %all_to_all.68.got = bf16[16,96,128]{2,1,0:T(8,128)(2,1)S(1)} all-to-all(bf16[16,96,128]{2,1,0:T(8,128)(2,1)S(1)} %get-tuple-element.42), channel_id=1, replica_groups=mesh['chips'=32,'samples'=16] {'samples'}, dimensions={0} | all-to-all | bytes 786432 | tf_op jit(solution)/shard_map/all_to_all | solution.py:457
  88.3 2.3 %shard_map.62 = (f32[144,64]{1,0:T(8,128)S(1)}, bf16[16,96,128]{2,1,0:T(8,128)(2,1)S(1)}) custom-call(s32[2]{0:T(128)S(1)} %pad_add_fusion.me, bf16[16,96,128]{2,1,0:T(8,128)(2,1)S(1)} %all_to_all.68.got, f32[144,64]{1,0:T(8,128)S(1)} %get-tuple-element.43.w), custom_call_target="tpu_custom_call" | custom-call | tf_op jit(solution)/shard_map/pallas_call | solution.py:445
  90.6 16.7 %all_to_all.69.got = bf16[16,96,128]{2,1,0:T(8,128)(2,1)S(1)} all-to-all(bf16[16,96,128]{2,1,0:T(8,128)(2,1)S(1)} %get-tuple-element.44), channel_id=1, replica_groups=mesh['chips'=32,'samples'=16] {'samples'}, dimensions={0} | all-to-all | bytes 786432 | tf_op jit(solution)/shard_map/all_to_all | solution.py:457
  107.3 2.0 shard_map.63
  109.4 22.9 %all_to_all.70.got = bf16[32,40,128]{2,1,0:T(8,128)(2,1)S(1)} all-to-all(bf16[32,40,128]{2,1,0:T(8,128)(2,1)S(1)} %shard_map.63), channel_id=1, replica_groups=mesh['chips'=32,'samples'=16] {'chips'}, dimensions={0} | all-to-all | bytes 655360 | tf_op jit(solution)/shard_map/all_to_all | solution.py:457
  132.3 1.5 shard_map.64
  133.8 15.6 %all_to_all.71.got = bf16[32,32,128]{2,1,0:T(8,128)(2,1)S(1)} all-to-all(bf16[32,32,128]{2,1,0:T(8,128)(2,1)S(1)} %get-tuple-element.46), channel_id=1, replica_groups=mesh['chips'=32,'samples'=16] {'chips'}, dimensions={0} | all-to-all | bytes 524288 | tf_op jit(solution)/shard_map/all_to_all | solution.py:457
  149.4 2.3 %shard_map.65 = bf16[16,128,128]{2,1,0:T(8,128)(2,1)S(1)} custom-call(s32[2]{0:T(128)S(1)} %pad_add_fusion.me, bf16[32,32,128]{2,1,0:T(8,128)(2,1)S(1)} %all_to_all.71.got, bf16[2304,1024]{1,0:T(8,128)(2,1)S(1)} %copy-done.2), custom_call_target="tpu_custom_call" | custom-call | flops 301989888 | bytes 4718592 | tf_op jit(solution)/shard_map/pallas_call | solution.py:445
  151.7 16.4 %all_to_all.72.got = bf16[16,128,128]{2,1,0:T(8,128)(2,1)S(1)} all-to-all(bf16[16,128,128]{2,1,0:T(8,128)(2,1)S(1)} %shard_map.65), channel_id=1, replica_groups=mesh['chips'=32,'samples'=16] {'samples'}, dimensions={0} | all-to-all | bytes 1048576 | tf_op jit(solution)/shard_map/all_to_all | solution.py:457
  168.0 1.6 shard_map.66
  169.6 14.3 %all_to_all.73.got = f32[16,1,128]{2,1,0:T(1,128)S(1)} all-to-all(f32[16,1,128]{2,1,0:T(1,128)S(1)} %get-tuple-element.51), channel_id=1, replica_groups=mesh['chips'=32,'samples'=16] {'samples'}, dimensions={0} | all-to-all | bytes 16384 | tf_op jit(solution)/shard_map/all_to_all | solution.py:457
  183.9 0.6 shard_map.67
  184.6 9.6 %all-to-all-start.12 = ((f32[32,1,128]{2,1,0:T(1,128)}), f32[32,1,128]{2,1,0:T(1,128)S(1)}, u32[]{:S(2)}, u32[]{:S(2)}) async-start(f32[32,1,128]{2,1,0:T(1,128)} %shard_map.67), calls=%async_computation.12 | async-start | bytes 32768 | tf_op jit(solution)/shard_map/all_to_all | solution.py:457
  194.2 0.7 copy.9
  194.9 7.1 %all-to-all-done.12.got = f32[32,1,128]{2,1,0:T(1,128)S(1)} async-done(((f32[32,1,128]{2,1,0:T(1,128)}), f32[32,1,128]{2,1,0:T(1,128)S(1)}, u32[]{:S(2)}, u32[]{:S(2)}) %all-to-all-start.12) | async-done | bytes 16416 | tf_op jit(solution)/shard_map/all_to_all | solution.py:457
  202.0 0.7 shard_map.68
  (1 shorter events, 0.0 us)
Async XLA Ops:
  0.7 0.8 copy-start
  1.6 25.1 %copy-start.2 = (bf16[2304,1024]{1,0:T(8,128)(2,1)S(1)}, bf16[2304,1024]{1,0:T(8,128)(2,1)}, u32[]{:S(2)}) copy-start(bf16[2304,1024]{1,0:T(8,128)(2,1)} %tile.7) | copy-start | bytes 14155780
  1.6 52.0 %copy-start.1 = (f32[64,32]{0,1:T(8,128)S(1)}, f32[64,32]{0,1:T(8,128)}, u32[]{:S(2)}) copy-start(f32[64,32]{0,1:T(8,128)} %param.7) | copy-start | bytes 24580
  184.6 17.4 %all-to-all-start.12 = ((f32[32,1,128]{2,1,0:T(1,128)}), f32[32,1,128]{2,1,0:T(1,128)S(1)}, u32[]{:S(2)}, u32[]{:S(2)}) async-start(f32[32,1,128]{2,1,0:T(1,128)} %shard_map.67), calls=%async_computation.12 | async-start | bytes 32768 | tf_op jit(solution)/shard_map/all_to_all | solution.py:457

commit v10 on v9

--- a/solution.py
+++ b/solution.py
@@ -25,7 +25,6 @@
 W_HALF = 80
 GRAM = 16
 W_MSG = W_HALF + GRAM
-PAIR = 32
 H_MSG = BLOCK + GRAM + 8
 LEFT = W_HALF // BLOCK
 W_BLOCKS = W_OWN // BLOCK
@@ -117,39 +116,46 @@
     )
 
 
+GRAM_TOP = 13.0
+
+
+def grain():
+    row = lax.broadcasted_iota(jnp.int32, (32, K), 0)
+    col = lax.broadcasted_iota(jnp.int32, (32, K), 1)
+    return 1.0 + ((row * 11 + col * 23) & 31).astype(F32) * (1.0 / 64.0)
+
+
+def eighth(x):
+    x = x * x
+    x = x * x
+    return x * x
+
+
+def eighth_root(x):
+    return jnp.sqrt(lax.rsqrt(lax.rsqrt(jnp.abs(x))))
+
+
 def encode_gram(parts, diagonal, factor):
     power = power_of(jnp.maximum(peak(parts), peak(diagonal)))
-    coded = code(parts, power, factor)
+    scale = jnp.exp2(GRAM_TOP - power) * factor
+    coded = eighth(parts * grain() * scale)
     return (
         jnp.concatenate([coded[:GRAM], coded[GRAM:]], axis=1),
-        code(diagonal, power, factor),
+        eighth(diagonal * scale),
         power,
     )
+
+
+def gram_scale(power, factor):
+    return jnp.exp2(power - GRAM_TOP) / factor
 
 
 def one_above(x):
     return jnp.concatenate([x[:, :K], x[:, K:]], axis=0)
 
 
-def pair_of(gram):
-    row, col = squares()
-    parts, diagonal = gram_parts(gram)
-    high = parts.astype(BF16).astype(F32)
-    low = parts - high
-    own = row == col
-    first = jnp.where(own, parts[:, :32], high[:, :32])
-    third = jnp.where(own, diagonal, low[:, :32])
-    return jnp.concatenate([first, high[:, 32:], third, low[:, 32:]], axis=1).astype(BF16)
-
-
-def of_pair(total):
-    row, col = squares()
-    own = row == col
-    first, third = total[:, :32], total[:, 64:96]
-    mixed = jnp.where(own, first, first + third)
-    diagonal = jnp.sum(jnp.where(own, third, 0.0), axis=0, keepdims=True)
-    block = total[:, 32:64] + total[:, 96:]
-    return gram_whole(jnp.concatenate([mixed, block], axis=1), diagonal)
+def added_parts(total):
+    return one_above(total) / grain()
 
 
 def products(halves):
@@ -161,32 +167,33 @@
     return two[:, :K] + two[:, K:]
 
 
-def spare_rows(left, right, diagonal, power):
+def spare_rows(left, right, grams):
+    rows = []
+    for _, diagonal, power in grams:
+        rows.append(jnp.broadcast_to(power, (1, K)))
+        rows.append(jnp.concatenate([diagonal, jnp.zeros((1, K - 32), F32)], axis=1))
     return jnp.concatenate(
         [
             jnp.broadcast_to(left, (LEFT, K)),
             jnp.broadcast_to(right, (LEFT - 1, K)),
-            jnp.broadcast_to(power, (1, K)),
-            jnp.concatenate([diagonal, jnp.zeros((1, K - 32), F32)], axis=1),
-            jnp.zeros((BLOCK - W_BLOCKS - 2, K), F32),
+            *rows,
+            jnp.zeros((BLOCK - W_BLOCKS - len(rows), K), F32),
         ],
         axis=0,
     )
 
 
 def w_message(w, gram):
-    coded, diagonal, power = gram
     none = jnp.zeros((LEFT, 1), F32)
     right = jnp.concatenate(
-        [w[W_HALF:], spare_rows(none, none[1:], diagonal, power)], axis=0
+        [w[W_HALF:], spare_rows(none, none[1:], [gram])], axis=0
     )
     return jnp.concatenate(
-        [jnp.concatenate([w[:W_HALF], right], axis=1), coded], axis=0
+        [jnp.concatenate([w[:W_HALF], right], axis=1), gram[0]], axis=0
     ).astype(BF16)
 
 
-def sums_message(sums, gram, factor):
-    coded, diagonal, power = gram
+def sums_message(sums, grams, factor):
     both = jnp.concatenate(
         [sums[:W_HALF], jnp.concatenate([sums[W_HALF:], jnp.zeros((BLOCK, K), F32)], axis=0)],
         axis=1,
@@ -203,15 +210,18 @@
     scale = jnp.exp2(TOP - powers) * factor
     blocks = [sixteenth(x * scale[j : j + 1]) for j, x in enumerate(blocks)]
     free = jnp.concatenate(
-        [blocks[-1][:, :K], spare_rows(left[:LEFT], right[: LEFT - 1], diagonal, power)], axis=1
-    )
-    return jnp.concatenate(blocks[:-1] + [free, coded], axis=0).astype(BF16)
-
-
-def read_gram(message, factor):
-    roots = root(message)
-    scale = scale_of(message[W_BLOCKS : W_BLOCKS + 1, 127:], factor)
-    return roots[BLOCK:] * scale, roots[W_BLOCKS + 1 : W_BLOCKS + 2] * scale
+        [blocks[-1][:, :K], spare_rows(left[:LEFT], right[: LEFT - 1], grams)], axis=1
+    )
+    return jnp.concatenate(
+        blocks[:-1] + [free] + [coded for coded, _, _ in grams], axis=0
+    ).astype(BF16)
+
+
+def read_gram(message, factor, which=0):
+    at = W_BLOCKS + 2 * which
+    scale = gram_scale(message[at : at + 1, 127:], factor)
+    coded = message[BLOCK + GRAM * which : BLOCK + GRAM * (which + 1)]
+    return eighth_root(coded) * scale, eighth_root(message[at + 1 : at + 2]) * scale
 
 
 def read_sums(message, factor):
@@ -261,7 +271,7 @@
 
     lax.fori_loop(0, ROWS // 128, turn, 0, unroll=True)
     factor = chip_factor(me[0])
-    coded, ends, power = encode_gram(one_above(gram), diagonal[:, K : K + 32], factor)
+    coded, ends, power = encode_gram(added_parts(gram), diagonal[:, K : K + 32], factor)
     ends = jnp.concatenate([ends, jnp.zeros((1, 96), F32)], axis=1)
     power = jnp.broadcast_to(power, (1, 128))
     per = H_WIDTH // H_OWN
@@ -295,18 +305,19 @@
     def add(i, carry):
         numer, gram, diagonal = carry
         message = got[i].astype(F32)
-        roots = root(message)
-        scales = scale_of(message[H_MSG - 8 :, 127:], chip_factor(i))
-        numer += roots[:BLOCK] * jnp.where(lane < K, scales[2:3], scales[3:4])
-        gram += roots[BLOCK : BLOCK + GRAM] * scales[1:2]
-        diagonal += roots[H_MSG - 8 : H_MSG - 7] * scales[1:2]
+        powers = message[H_MSG - 8 :, 127:]
+        scales = scale_of(powers, chip_factor(i))
+        numer += root(message[:BLOCK]) * jnp.where(lane < K, scales[2:3], scales[3:4])
+        scale = gram_scale(powers[1:2], chip_factor(i))
+        gram += eighth_root(message[BLOCK : BLOCK + GRAM]) * scale
+        diagonal += eighth_root(message[H_MSG - 8 : H_MSG - 7]) * scale
         return numer, gram, diagonal
 
     zero = jnp.zeros((BLOCK, 128), F32)
     numer, gram, diagonal = lax.fori_loop(
         0, CHIPS, add, (zero, zero, jnp.zeros((1, 128), F32)), unroll=True
     )
-    gram = gram_whole(one_above(gram), diagonal[:, :32])
+    gram = gram_whole(added_parts(gram), diagonal[:, :32])
     old = h[...]
     below = jnp.dot(old, gram, precision=HIGHEST, preferred_element_type=F32) + epsilon
     new = old * one_above(numer) / below
@@ -318,10 +329,9 @@
     halves = got[...].reshape(COLS, 128)
     four = products(halves)
     factor = sample_factor(me[1])
-    gram = encode_gram(*gram_parts(quarters(four)), factor)
-    last = out.shape[1] > W_MSG
-    if last:
-        pair = pair_of(four[:K, :K])
+    grams = [encode_gram(*gram_parts(quarters(four)), factor)]
+    if out.shape[1] > W_MSG:
+        grams.append(encode_gram(*gram_parts(four[:K, :K]), factor))
     if energy is not None:
 
         def add(i, total):
@@ -329,14 +339,11 @@
             values = tile[rows, :].astype(F32)
             return total + jnp.sum((values * values).reshape(W_OWN // 8, 8, COLS), axis=0)
 
-        squares_sum = lax.fori_loop(0, SAMPLES, add, jnp.zeros((8, COLS), F32))
+        squares_sum = lax.fori_loop(0, SAMPLES, add, jnp.zeros((8, COLS), F32), unroll=True)
         energy[...] = jnp.full((1, 128), jnp.sum(squares_sum), F32)
     sums = jnp.dot(tile[...], halves[:, :K], preferred_element_type=F32)
     for q in range(SAMPLES):
-        message = sums_message(sums[q * W_OWN : (q + 1) * W_OWN], gram, factor)
-        if last:
-            message = jnp.concatenate([message, pair], axis=0)
-        out[q] = message
+        out[q] = sums_message(sums[q * W_OWN : (q + 1) * W_OWN], grams, factor)
 
 
 def w_numer_kernel(me, got, tile, out):
@@ -348,31 +355,27 @@
 
 
 def w_new(got, w):
-    last = got.shape[1] > W_MSG
+    count = (got.shape[1] - W_HALF) // GRAM
 
     def add(i, carry):
-        blocks, gram, diagonal, rest = carry
+        blocks, grams = carry
         message = got[i].astype(F32)
         terms = read_sums(message[:W_HALF], sample_factor(i))
-        more, ends = read_gram(message[W_HALF - BLOCK : W_MSG], sample_factor(i))
-        if last:
-            rest += message[W_MSG:]
         blocks = tuple(total + term for total, term in zip(blocks, terms))
-        return blocks, gram + more, diagonal + ends, rest
+        more = [read_gram(message[W_HALF - BLOCK :], sample_factor(i), n) for n in range(count)]
+        return blocks, tuple((x + u, y + v) for (x, y), (u, v) in zip(grams, more))
 
     zero = jnp.zeros((BLOCK, 128), F32)
-    blocks, gram, diagonal, rest = lax.fori_loop(
-        0,
-        SAMPLES,
-        add,
-        ((zero,) * LEFT, zero, jnp.zeros((1, 128), F32), jnp.zeros((PAIR, 128), F32)),
-        unroll=True,
+    empty = (zero, jnp.zeros((1, 128), F32))
+    blocks, grams = lax.fori_loop(
+        0, SAMPLES, add, ((zero,) * LEFT, (empty,) * count), unroll=True
     )
     numer = one_column(jnp.concatenate(blocks, axis=0))
-    gram = gram_whole(one_above(gram), diagonal[:, K : K + 32])
+    grams = [gram_whole(added_parts(x), y[:, K : K + 32]) for x, y in grams]
+    gram = grams[0]
     old = w[...]
     below = jnp.dot(old, gram, precision=HIGHEST, preferred_element_type=F32) + epsilon
-    return old * numer / below, numer, rest
+    return old * numer / below, numer, grams[-1]
 
 
 def w_update_kernel(me, got, w, w_out, out):
@@ -382,10 +385,9 @@
 
 
 def w_last_kernel(got, w, energy, w_out, out):
-    new, numer, rest = w_new(got, w)
+    new, numer, gram = w_new(got, w)
     w_out[...] = new
     rounded = new.astype(BF16).astype(F32)
-    gram = of_pair(rest)
     fitted = jnp.dot(rounded, gram, precision=HIGHEST, preferred_element_type=F32)
     share = jnp.sum(rounded * (fitted - 2.0 * numer))
     lane = lax.broadcasted_iota(jnp.int32, (1, 128), 1)
@@ -487,7 +489,7 @@
             h_update_kernel, (got, h), [((H_OWN, K), F32), ((CHIPS, H_OWN, 128), BF16)]
         )
         got_h = exchange(sent, "chips")
-        w_sums = [((SAMPLES, W_MSG + PAIR if last else W_MSG, 128), BF16)]
+        w_sums = [((SAMPLES, W_MSG + GRAM if last else W_MSG, 128), BF16)]
         if sweep == 0:
             sent, energy = call(
                 w_numer_energy_kernel,

time: 204 us -> 202 us (level)
  no operation moved by 1% of the time
where the time goes in v10:
time: 202 us; the launch traced here: 201 us
  blocking collectives  165 us (82%)
  Pallas kernels  17.6 us (9%)
  starting transfers between devices  8.98 us (4%)
  waiting for transfers between devices  7.19 us (4%)
    all_to_all x9, blocking collectives, exchange(): return lax.all_to_all(x, axis, 0, 0, tiled=True)  165 us
    pallas_call x11, Pallas kernels, call(): pl.pallas_call(kernel, out_shape=[jax.ShapeDtypeStruct(shape, dtype) for...  17.6 us
    all_to_all x1, starting transfers between devices, exchange(): return lax.all_to_all(x, axis, 0, 0, tiled=True)  8.98 us
    all_to_all x1, waiting for transfers between devices, exchange(): return lax.all_to_all(x, axis, 0, 0, tiled=True)  7.19 us
  transfers between devices with their start and end apart: 1, of which 1 were waited for; matrix products, arithmetic and copies ran while one was open for 0% of the time, Pallas kernels for 0%

profile of v10, /device:TPU:1, one launch (start us, length us, event | category | flops | bytes accessed | tf_op | source)
XLA Modules:
  0.0 201.3 jit_solution(18125622369247839444)
XLA Ops:
  0.6 0.1 pad_add_fusion.me
  0.7 0.0 copy-start
  0.7 0.8 copy-done
  1.6 0.0 copy-start.2
  1.6 0.0 copy-start.1
  1.6 1.2 shard_map.58
  2.8 23.9 %all_to_all.65.got = bf16[16,96,128]{2,1,0:T(8,128)(2,1)S(1)} all-to-all(bf16[16,96,128]{2,1,0:T(8,128)(2,1)S(1)} %get-tuple-element.40), channel_id=1, replica_groups=mesh['chips'=32,'samples'=16] {'samples'}, dimensions={0} | all-to-all | bytes 786432 | tf_op jit(solution)/shard_map/all_to_all | solution.py:459
  26.7 0.0 copy-done.2
  26.7 2.0 %shard_map.59 = bf16[32,40,128]{2,1,0:T(8,128)(2,1)S(1)} custom-call(s32[2]{0:T(128)S(1)} %pad_add_fusion.me, bf16[16,96,128]{2,1,0:T(8,128)(2,1)S(1)} %all_to_all.65.got, bf16[2304,1024]{1,0:T(8,128)(2,1)S(1)} %copy-done.2), custom_call_target="tpu_custom_call" | custom-call | flops 301989888 | bytes 4718592 | tf_op jit(solution)/shard_map/pallas_call | solution.py:447
  28.7 24.8 %all_to_all.66.got = bf16[32,40,128]{2,1,0:T(8,128)(2,1)S(1)} all-to-all(bf16[32,40,128]{2,1,0:T(8,128)(2,1)S(1)} %shard_map.59), channel_id=1, replica_groups=mesh['chips'=32,'samples'=16] {'chips'}, dimensions={0} | all-to-all | bytes 655360 | tf_op jit(solution)/shard_map/all_to_all | solution.py:459
  53.6 0.0 copy-done.1
  53.6 1.0 shard_map.60
  54.6 15.6 %all_to_all.67.got = bf16[32,32,128]{2,1,0:T(8,128)(2,1)S(1)} all-to-all(bf16[32,32,128]{2,1,0:T(8,128)(2,1)S(1)} %get-tuple-element.41), channel_id=1, replica_groups=mesh['chips'=32,'samples'=16] {'chips'}, dimensions={0} | all-to-all | bytes 524288 | tf_op jit(solution)/shard_map/all_to_all | solution.py:459
  70.2 2.4 %shard_map.61 = (bf16[16,96,128]{2,1,0:T(8,128)(2,1)S(1)}, f32[1,128]{1,0:T(1,128)S(1)}) custom-call(s32[2]{0:T(128)S(1)} %pad_add_fusion.me, bf16[32,32,128]{2,1,0:T(8,128)(2,1)S(1)} %all_to_all.67.got, bf16[2304,1024]{1,0:T(8,128)(2,1)S(1)} %copy-done.2), custom_call_target="tpu_custom_call" | custom-call | flops 301989888 | bytes 4718592 | tf_op jit(solution)/shard_map/pallas_call | solution.py:447
  72.5 15.0 %all_to_all.68.got = bf16[16,96,128]{2,1,0:T(8,128)(2,1)S(1)} all-to-all(bf16[16,96,128]{2,1,0:T(8,128)(2,1)S(1)} %get-tuple-element.42), channel_id=1, replica_groups=mesh['chips'=32,'samples'=16] {'samples'}, dimensions={0} | all-to-all | bytes 786432 | tf_op jit(solution)/shard_map/all_to_all | solution.py:459
  87.5 2.3 %shard_map.62 = (f32[144,64]{1,0:T(8,128)S(1)}, bf16[16,96,128]{2,1,0:T(8,128)(2,1)S(1)}) custom-call(s32[2]{0:T(128)S(1)} %pad_add_fusion.me, bf16[16,96,128]{2,1,0:T(8,128)(2,1)S(1)} %all_to_all.68.got, f32[144,64]{1,0:T(8,128)S(1)} %get-tuple-element.43.w), custom_call_target="tpu_custom_call" | custom-call | tf_op jit(solution)/shard_map/pallas_call | solution.py:447
  89.8 16.7 %all_to_all.69.got = bf16[16,96,128]{2,1,0:T(8,128)(2,1)S(1)} all-to-all(bf16[16,96,128]{2,1,0:T(8,128)(2,1)S(1)} %get-tuple-element.44), channel_id=1, replica_groups=mesh['chips'=32,'samples'=16] {'samples'}, dimensions={0} | all-to-all | bytes 786432 | tf_op jit(solution)/shard_map/all_to_all | solution.py:459
  106.6 2.0 %shard_map.63 = bf16[32,40,128]{2,1,0:T(8,128)(2,1)S(1)} custom-call(s32[2]{0:T(128)S(1)} %pad_add_fusion.me, bf16[16,96,128]{2,1,0:T(8,128)(2,1)S(1)} %all_to_all.69.got, bf16[2304,1024]{1,0:T(8,128)(2,1)S(1)} %copy-done.2), custom_call_target="tpu_custom_call" | custom-call | flops 301989888 | bytes 4718592 | tf_op jit(solution)/shard_map/pallas_call | solution.py:447
  108.6 22.9 %all_to_all.70.got = bf16[32,40,128]{2,1,0:T(8,128)(2,1)S(1)} all-to-all(bf16[32,40,128]{2,1,0:T(8,128)(2,1)S(1)} %shard_map.63), channel_id=1, replica_groups=mesh['chips'=32,'samples'=16] {'chips'}, dimensions={0} | all-to-all | bytes 655360 | tf_op jit(solution)/shard_map/all_to_all | solution.py:459
  131.5 1.5 shard_map.64
  133.0 15.6 %all_to_all.71.got = bf16[32,32,128]{2,1,0:T(8,128)(2,1)S(1)} all-to-all(bf16[32,32,128]{2,1,0:T(8,128)(2,1)S(1)} %get-tuple-element.46), channel_id=1, replica_groups=mesh['chips'=32,'samples'=16] {'chips'}, dimensions={0} | all-to-all | bytes 524288 | tf_op jit(solution)/shard_map/all_to_all | solution.py:459
  148.6 2.3 %shard_map.65 = bf16[16,112,128]{2,1,0:T(8,128)(2,1)S(1)} custom-call(s32[2]{0:T(128)S(1)} %pad_add_fusion.me, bf16[32,32,128]{2,1,0:T(8,128)(2,1)S(1)} %all_to_all.71.got, bf16[2304,1024]{1,0:T(8,128)(2,1)S(1)} %copy-done.2), custom_call_target="tpu_custom_call" | custom-call | flops 301989888 | bytes 4718592 | tf_op jit(solution)/shard_map/pallas_call | solution.py:447
  150.9 15.7 %all_to_all.72.got = bf16[16,112,128]{2,1,0:T(8,128)(2,1)S(1)} all-to-all(bf16[16,112,128]{2,1,0:T(8,128)(2,1)S(1)} %shard_map.65), channel_id=1, replica_groups=mesh['chips'=32,'samples'=16] {'samples'}, dimensions={0} | all-to-all | bytes 917504 | tf_op jit(solution)/shard_map/all_to_all | solution.py:459
  166.6 1.5 shard_map.66
  168.1 14.4 %all_to_all.73.got = f32[16,1,128]{2,1,0:T(1,128)S(1)} all-to-all(f32[16,1,128]{2,1,0:T(1,128)S(1)} %get-tuple-element.51), channel_id=1, replica_groups=mesh['chips'=32,'samples'=16] {'samples'}, dimensions={0} | all-to-all | bytes 16384 | tf_op jit(solution)/shard_map/all_to_all | solution.py:459
  182.5 0.6 shard_map.67
  183.1 9.0 %all-to-all-start.12 = ((f32[32,1,128]{2,1,0:T(1,128)}), f32[32,1,128]{2,1,0:T(1,128)S(1)}, u32[]{:S(2)}, u32[]{:S(2)}) async-start(f32[32,1,128]{2,1,0:T(1,128)} %shard_map.67), calls=%async_computation.12 | async-start | bytes 32768 | tf_op jit(solution)/shard_map/all_to_all | solution.py:459
  192.1 0.7 copy.9
  192.8 7.2 %all-to-all-done.12.got = f32[32,1,128]{2,1,0:T(1,128)S(1)} async-done(((f32[32,1,128]{2,1,0:T(1,128)}), f32[32,1,128]{2,1,0:T(1,128)S(1)}, u32[]{:S(2)}, u32[]{:S(2)}) %all-to-all-start.12) | async-done | bytes 16416 | tf_op jit(solution)/shard_map/all_to_all | solution.py:459
  200.0 0.7 shard_map.68
  (1 shorter events, 0.0 us)
Async XLA Ops:
  0.7 0.8 copy-start
  1.6 25.1 %copy-start.2 = (bf16[2304,1024]{1,0:T(8,128)(2,1)S(1)}, bf16[2304,1024]{1,0:T(8,128)(2,1)}, u32[]{:S(2)}) copy-start(bf16[2304,1024]{1,0:T(8,128)(2,1)} %tile.7) | copy-start | bytes 14155780
  1.6 52.0 %copy-start.1 = (f32[64,32]{0,1:T(8,128)S(1)}, f32[64,32]{0,1:T(8,128)}, u32[]{:S(2)}) copy-start(f32[64,32]{0,1:T(8,128)} %param.7) | copy-start | bytes 24580
  183.1 16.9 %all-to-all-start.12 = ((f32[32,1,128]{2,1,0:T(1,128)}), f32[32,1,128]{2,1,0:T(1,128)S(1)}, u32[]{:S(2)}, u32[]{:S(2)}) async-start(f32[32,1,128]{2,1,0:T(1,128)} %shard_map.67), calls=%async_computation.12 | async-start | bytes 32768 | tf_op jit(solution)/shard_map/all_to_all | solution.py:459

commit v11 on v10

--- a/solution.py
+++ b/solution.py
@@ -392,11 +392,7 @@
     share = jnp.sum(rounded * (fitted - 2.0 * numer))
     lane = lax.broadcasted_iota(jnp.int32, (1, 128), 1)
     pair = jnp.where(lane < K, share, energy[...])
-    copies(pair, out)
-
-
-def share_kernel(got, out):
-    copies(jnp.sum(got[...], axis=0), out)
+    out[...] = jnp.broadcast_to(pair, out.shape)
 
 
 def ratio_kernel(got, ratio, close, total_out):
@@ -513,14 +509,13 @@
             )
             got_w = exchange(sent, "samples")
     w, shares = call(
-        w_last_kernel, (got, w, energy), [((W_OWN, K), F32), ((SAMPLES, 1, 128), F32)]
-    )
-    (shares,) = call(
-        share_kernel, (exchange(shares, "samples"),), [((CHIPS, 1, 128), F32)]
+        w_last_kernel,
+        (got, w, energy),
+        [((W_OWN, K), F32), ((CHIPS * SAMPLES, 1, 128), F32)],
     )
     ratio, close, total = call(
         ratio_kernel,
-        (exchange(shares, "chips"),),
+        (exchange(shares, ("chips", "samples")),),
         [((1, 1), F32), ((1, 1), jnp.int32), ((1, 1), F32)],
         out_spec=SMEM,
     )

time: 202 us -> 202 us (level)
  blocking collectives: 165 us -> 150 us
  waiting for transfers between devices: 7.19 us -> 16.8 us
  starting transfers between devices: 8.98 us -> 13.5 us
    all_to_all x9 -> x8, blocking collectives: 165 us -> 150 us  [exchange(): return lax.all_to_all(x, axis, 0, 0, tiled=True)]
    all_to_all x1, waiting for transfers between devices: 7.19 us -> 16.8 us  [exchange(): return lax.all_to_all(x, axis, 0, 0, tiled=True)]
    all_to_all x1, starting transfers between devices: 8.98 us -> 13.5 us  [exchange(): return lax.all_to_all(x, axis, 0, 0, tiled=True)]
    pallas_call x11 -> x10, Pallas kernels: 17.6 us -> 18.3 us  [call(): pl.pallas_call(kernel, out_shape=[jax.ShapeDtypeStruct(shape, dtype) for...]
where the time goes in v11:
time: 202 us
  blocking collectives  150 us (74%)
  Pallas kernels  18.3 us (9%)
  waiting for transfers between devices  16.8 us (8%)
  starting transfers between devices  13.5 us (7%)
    all_to_all x8, blocking collectives, exchange(): return lax.all_to_all(x, axis, 0, 0, tiled=True)  150 us
    pallas_call x10, Pallas kernels, call(): pl.pallas_call(kernel, out_shape=[jax.ShapeDtypeStruct(shape, dtype) for...  18.3 us
    all_to_all x1, waiting for transfers between devices, exchange(): return lax.all_to_all(x, axis, 0, 0, tiled=True)  16.8 us
    all_to_all x1, starting transfers between devices, exchange(): return lax.all_to_all(x, axis, 0, 0, tiled=True)  13.5 us
  transfers between devices with their start and end apart: 1, of which 1 were waited for; matrix products, arithmetic and copies ran while one was open for 0% of the time, Pallas kernels for 0%

profile of v11, /device:TPU:1, one launch (start us, length us, event | category | flops | bytes accessed | tf_op | source)
XLA Modules:
  0.0 202.0 jit_solution(1307425508790539480)
XLA Ops:
  0.6 0.1 pad_add_fusion.me
  0.7 0.0 copy-start
  0.7 0.8 copy-done
  1.6 0.0 copy-start.2
  1.6 0.0 copy-start.1
  1.6 1.2 shard_map.58
  2.8 23.9 %all_to_all.60.got = bf16[16,96,128]{2,1,0:T(8,128)(2,1)S(1)} all-to-all(bf16[16,96,128]{2,1,0:T(8,128)(2,1)S(1)} %get-tuple-element.40), channel_id=1, replica_groups=mesh['chips'=32,'samples'=16] {'samples'}, dimensions={0} | all-to-all | bytes 786432 | tf_op jit(solution)/shard_map/all_to_all | solution.py:455
  26.7 0.0 copy-done.2
  26.7 2.0 %shard_map.59 = bf16[32,40,128]{2,1,0:T(8,128)(2,1)S(1)} custom-call(s32[2]{0:T(128)S(1)} %pad_add_fusion.me, bf16[16,96,128]{2,1,0:T(8,128)(2,1)S(1)} %all_to_all.60.got, bf16[2304,1024]{1,0:T(8,128)(2,1)S(1)} %copy-done.2), custom_call_target="tpu_custom_call" | custom-call | flops 301989888 | bytes 4718592 | tf_op jit(solution)/shard_map/pallas_call | solution.py:443
  28.7 24.8 %all_to_all.61.got = bf16[32,40,128]{2,1,0:T(8,128)(2,1)S(1)} all-to-all(bf16[32,40,128]{2,1,0:T(8,128)(2,1)S(1)} %shard_map.59), channel_id=1, replica_groups=mesh['chips'=32,'samples'=16] {'chips'}, dimensions={0} | all-to-all | bytes 655360 | tf_op jit(solution)/shard_map/all_to_all | solution.py:455
  53.6 0.0 copy-done.1
  53.6 1.0 shard_map.60
  54.6 15.6 %all_to_all.62.got = bf16[32,32,128]{2,1,0:T(8,128)(2,1)S(1)} all-to-all(bf16[32,32,128]{2,1,0:T(8,128)(2,1)S(1)} %get-tuple-element.41), channel_id=1, replica_groups=mesh['chips'=32,'samples'=16] {'chips'}, dimensions={0} | all-to-all | bytes 524288 | tf_op jit(solution)/shard_map/all_to_all | solution.py:455
  70.2 2.4 %shard_map.61 = (bf16[16,96,128]{2,1,0:T(8,128)(2,1)S(1)}, f32[1,128]{1,0:T(1,128)S(1)}) custom-call(s32[2]{0:T(128)S(1)} %pad_add_fusion.me, bf16[32,32,128]{2,1,0:T(8,128)(2,1)S(1)} %all_to_all.62.got, bf16[2304,1024]{1,0:T(8,128)(2,1)S(1)} %copy-done.2), custom_call_target="tpu_custom_call" | custom-call | flops 301989888 | bytes 4718592 | tf_op jit(solution)/shard_map/pallas_call | solution.py:443
  72.6 15.0 %all_to_all.63.got = bf16[16,96,128]{2,1,0:T(8,128)(2,1)S(1)} all-to-all(bf16[16,96,128]{2,1,0:T(8,128)(2,1)S(1)} %get-tuple-element.42), channel_id=1, replica_groups=mesh['chips'=32,'samples'=16] {'samples'}, dimensions={0} | all-to-all | bytes 786432 | tf_op jit(solution)/shard_map/all_to_all | solution.py:455
  87.6 2.3 %shard_map.62 = (f32[144,64]{1,0:T(8,128)S(1)}, bf16[16,96,128]{2,1,0:T(8,128)(2,1)S(1)}) custom-call(s32[2]{0:T(128)S(1)} %pad_add_fusion.me, bf16[16,96,128]{2,1,0:T(8,128)(2,1)S(1)} %all_to_all.63.got, f32[144,64]{1,0:T(8,128)S(1)} %get-tuple-element.43.w), custom_call_target="tpu_custom_call" | custom-call | tf_op jit(solution)/shard_map/pallas_call | solution.py:443
  89.8 16.7 %all_to_all.64.got = bf16[16,96,128]{2,1,0:T(8,128)(2,1)S(1)} all-to-all(bf16[16,96,128]{2,1,0:T(8,128)(2,1)S(1)} %get-tuple-element.44), channel_id=1, replica_groups=mesh['chips'=32,'samples'=16] {'samples'}, dimensions={0} | all-to-all | bytes 786432 | tf_op jit(solution)/shard_map/all_to_all | solution.py:455
  106.6 2.0 %shard_map.63 = bf16[32,40,128]{2,1,0:T(8,128)(2,1)S(1)} custom-call(s32[2]{0:T(128)S(1)} %pad_add_fusion.me, bf16[16,96,128]{2,1,0:T(8,128)(2,1)S(1)} %all_to_all.64.got, bf16[2304,1024]{1,0:T(8,128)(2,1)S(1)} %copy-done.2), custom_call_target="tpu_custom_call" | custom-call | flops 301989888 | bytes 4718592 | tf_op jit(solution)/shard_map/pallas_call | solution.py:443
  108.6 22.9 %all_to_all.65.got = bf16[32,40,128]{2,1,0:T(8,128)(2,1)S(1)} all-to-all(bf16[32,40,128]{2,1,0:T(8,128)(2,1)S(1)} %shard_map.63), channel_id=1, replica_groups=mesh['chips'=32,'samples'=16] {'chips'}, dimensions={0} | all-to-all | bytes 655360 | tf_op jit(solution)/shard_map/all_to_all | solution.py:455
  131.5 1.5 shard_map.64
  133.0 15.6 %all_to_all.66.got = bf16[32,32,128]{2,1,0:T(8,128)(2,1)S(1)} all-to-all(bf16[32,32,128]{2,1,0:T(8,128)(2,1)S(1)} %get-tuple-element.46), channel_id=1, replica_groups=mesh['chips'=32,'samples'=16] {'chips'}, dimensions={0} | all-to-all | bytes 524288 | tf_op jit(solution)/shard_map/all_to_all | solution.py:455
  148.6 2.3 %shard_map.65 = bf16[16,112,128]{2,1,0:T(8,128)(2,1)S(1)} custom-call(s32[2]{0:T(128)S(1)} %pad_add_fusion.me, bf16[32,32,128]{2,1,0:T(8,128)(2,1)S(1)} %all_to_all.66.got, bf16[2304,1024]{1,0:T(8,128)(2,1)S(1)} %copy-done.2), custom_call_target="tpu_custom_call" | custom-call | flops 301989888 | bytes 4718592 | tf_op jit(solution)/shard_map/pallas_call | solution.py:443
  150.9 15.7 %all_to_all.67.got = bf16[16,112,128]{2,1,0:T(8,128)(2,1)S(1)} all-to-all(bf16[16,112,128]{2,1,0:T(8,128)(2,1)S(1)} %shard_map.65), channel_id=1, replica_groups=mesh['chips'=32,'samples'=16] {'samples'}, dimensions={0} | all-to-all | bytes 917504 | tf_op jit(solution)/shard_map/all_to_all | solution.py:455
  166.6 2.4 %shard_map.66 = (f32[144,64]{1,0:T(8,128)S(1)}, f32[512,1,128]{2,1,0:T(1,128)}) custom-call(bf16[16,112,128]{2,1,0:T(8,128)(2,1)S(1)} %all_to_all.67.got, f32[144,64]{1,0:T(8,128)S(1)} %get-tuple-element.47.w, f32[1,128]{1,0:T(1,128)S(1)} %get-tuple-element.48.energy), custom_call_target="tpu_custom_call" | custom-call | tf_op jit(solution)/shard_map/pallas_call | solution.py:443
  168.9 13.5 %all-to-all-start.11 = ((f32[512,1,128]{2,1,0:T(1,128)}), f32[512,1,128]{2,1,0:T(1,128)S(1)}, u32[]{:S(2)}, u32[]{:S(2)}) async-start(f32[512,1,128]{2,1,0:T(1,128)} %get-tuple-element.51), calls=%async_computation.11 | async-start | bytes 524288 | tf_op jit(solution)/shard_map/all_to_all | solution.py:455
  182.5 0.7 copy.9
  183.2 16.8 %all-to-all-done.11.got = f32[512,1,128]{2,1,0:T(1,128)S(1)} async-done(((f32[512,1,128]{2,1,0:T(1,128)}), f32[512,1,128]{2,1,0:T(1,128)S(1)}, u32[]{:S(2)}, u32[]{:S(2)}) %all-to-all-start.11) | async-done | bytes 262176 | tf_op jit(solution)/shard_map/all_to_all | solution.py:455
  200.0 1.2 shard_map.67
  (1 shorter events, 0.0 us)
Async XLA Ops:
  0.7 0.8 copy-start
  1.6 25.1 %copy-start.2 = (bf16[2304,1024]{1,0:T(8,128)(2,1)S(1)}, bf16[2304,1024]{1,0:T(8,128)(2,1)}, u32[]{:S(2)}) copy-start(bf16[2304,1024]{1,0:T(8,128)(2,1)} %tile.7) | copy-start | bytes 14155780
  1.6 52.0 %copy-start.1 = (f32[64,32]{0,1:T(8,128)S(1)}, f32[64,32]{0,1:T(8,128)}, u32[]{:S(2)}) copy-start(f32[64,32]{0,1:T(8,128)} %param.7) | copy-start | bytes 24580
  168.9 31.1 %all-to-all-start.11 = ((f32[512,1,128]{2,1,0:T(1,128)}), f32[512,1,128]{2,1,0:T(1,128)S(1)}, u32[]{:S(2)}, u32[]{:S(2)}) async-start(f32[512,1,128]{2,1,0:T(1,128)} %get-tuple-element.51), calls=%async_computation.11 | async-start | bytes 524288 | tf_op jit(solution)/shard_map/all_to_all | solution.py:455

commit v12 on v10

--- a/solution.py
+++ b/solution.py
@@ -244,9 +244,12 @@
     copies(w_message(w, encode_gram(*gram, factor)), out)
 
 
-def start_kernel(me, w, tel, w_out, out):
+def start_kernel(me, w, tel, w_out, out, own, arrived):
     del tel
-    wide = jnp.concatenate([w[...], jnp.zeros((K, 256 - W_OWN), F32)], axis=1)
+    copy = pltpu.make_async_copy(w, own, arrived)
+    copy.start()
+    copy.wait()
+    wide = jnp.concatenate([own[...], jnp.zeros((K, 256 - W_OWN), F32)], axis=1)
     turned = wide.T[:W_OWN]
     w_out[...] = turned
     fill_w(turned, sample_factor(me[1]), out)
@@ -471,7 +474,12 @@
     h = sample_factors.T
     w_sent = [((W_OWN, K), F32), ((SAMPLES, W_MSG, 128), BF16)]
     w, sent = call(
-        start_kernel, (me, chip_factors, telemetry), w_sent, None, [SMEM, VMEM, HBM]
+        start_kernel,
+        (me, pltpu.with_memory_space_constraint(chip_factors, pltpu.HBM), telemetry),
+        w_sent,
+        None,
+        [SMEM, HBM, HBM],
+        [pltpu.VMEM((K, W_OWN), F32), pltpu.SemaphoreType.DMA],
     )
     got_w = exchange(sent, "samples")
     for sweep in range(ITERS):

time: 202 us -> 202 us (level)
  no operation moved by 1% of the time
where the time goes in v12:
time: 202 us
  blocking collectives  164 us (81%)
  Pallas kernels  18.8 us (9%)
  starting transfers between devices  8.93 us (4%)
  waiting for transfers between devices  7.19 us (4%)
    all_to_all x9, blocking collectives, exchange(): return lax.all_to_all(x, axis, 0, 0, tiled=True)  164 us
    pallas_call x11, Pallas kernels, call(): pl.pallas_call(kernel, out_shape=[jax.ShapeDtypeStruct(shape, dtype) for...  18.8 us
    all_to_all x1, starting transfers between devices, exchange(): return lax.all_to_all(x, axis, 0, 0, tiled=True)  8.93 us
    all_to_all x1, waiting for transfers between devices, exchange(): return lax.all_to_all(x, axis, 0, 0, tiled=True)  7.19 us
  transfers between devices with their start and end apart: 1, of which 1 were waited for; matrix products, arithmetic and copies ran while one was open for 0% of the time, Pallas kernels for 0%

profile of v12, /device:TPU:1, one launch (start us, length us, event | category | flops | bytes accessed | tf_op | source)
XLA Modules:
  0.0 201.5 jit_solution(6884445718208131756)
XLA Ops:
  0.6 0.0 copy-start.1
  0.6 0.1 pad_add_fusion.me
  0.7 0.0 copy-start
  0.7 2.4 %shard_map.58 = (f32[144,64]{1,0:T(8,128)S(1)}, bf16[16,96,128]{2,1,0:T(8,128)(2,1)S(1)}) custom-call(s32[2]{0:T(128)S(1)} %pad_add_fusion.me, f32[64,144]{1,0:T(8,128)} %w.1, bf16[2304,1024]{1,0:T(8,128)(2,1)} %tile.7), custom_call_target="tpu_custom_call" | custom-call | tf_op jit(solution)/shard_map/pallas_call | solution.py:450
  3.1 23.8 %all_to_all.65.got = bf16[16,96,128]{2,1,0:T(8,128)(2,1)S(1)} all-to-all(bf16[16,96,128]{2,1,0:T(8,128)(2,1)S(1)} %get-tuple-element.40), channel_id=1, replica_groups=mesh['chips'=32,'samples'=16] {'samples'}, dimensions={0} | all-to-all | bytes 786432 | tf_op jit(solution)/shard_map/all_to_all | solution.py:462
  26.9 0.0 copy-done.1
  26.9 2.0 %shard_map.59 = bf16[32,40,128]{2,1,0:T(8,128)(2,1)S(1)} custom-call(s32[2]{0:T(128)S(1)} %pad_add_fusion.me, bf16[16,96,128]{2,1,0:T(8,128)(2,1)S(1)} %all_to_all.65.got, bf16[2304,1024]{1,0:T(8,128)(2,1)S(1)} %copy-done.1), custom_call_target="tpu_custom_call" | custom-call | flops 301989888 | bytes 4718592 | tf_op jit(solution)/shard_map/pallas_call | solution.py:450
  28.9 24.8 %all_to_all.66.got = bf16[32,40,128]{2,1,0:T(8,128)(2,1)S(1)} all-to-all(bf16[32,40,128]{2,1,0:T(8,128)(2,1)S(1)} %shard_map.59), channel_id=1, replica_groups=mesh['chips'=32,'samples'=16] {'chips'}, dimensions={0} | all-to-all | bytes 655360 | tf_op jit(solution)/shard_map/all_to_all | solution.py:462
  53.8 0.0 copy-done
  53.8 1.0 shard_map.60
  54.8 15.6 %all_to_all.67.got = bf16[32,32,128]{2,1,0:T(8,128)(2,1)S(1)} all-to-all(bf16[32,32,128]{2,1,0:T(8,128)(2,1)S(1)} %get-tuple-element.41), channel_id=1, replica_groups=mesh['chips'=32,'samples'=16] {'chips'}, dimensions={0} | all-to-all | bytes 524288 | tf_op jit(solution)/shard_map/all_to_all | solution.py:462
  70.4 2.4 %shard_map.61 = (bf16[16,96,128]{2,1,0:T(8,128)(2,1)S(1)}, f32[1,128]{1,0:T(1,128)S(1)}) custom-call(s32[2]{0:T(128)S(1)} %pad_add_fusion.me, bf16[32,32,128]{2,1,0:T(8,128)(2,1)S(1)} %all_to_all.67.got, bf16[2304,1024]{1,0:T(8,128)(2,1)S(1)} %copy-done.1), custom_call_target="tpu_custom_call" | custom-call | flops 301989888 | bytes 4718592 | tf_op jit(solution)/shard_map/pallas_call | solution.py:450
  72.7 15.0 %all_to_all.68.got = bf16[16,96,128]{2,1,0:T(8,128)(2,1)S(1)} all-to-all(bf16[16,96,128]{2,1,0:T(8,128)(2,1)S(1)} %get-tuple-element.42), channel_id=1, replica_groups=mesh['chips'=32,'samples'=16] {'samples'}, dimensions={0} | all-to-all | bytes 786432 | tf_op jit(solution)/shard_map/all_to_all | solution.py:462
  87.7 2.3 %shard_map.62 = (f32[144,64]{1,0:T(8,128)S(1)}, bf16[16,96,128]{2,1,0:T(8,128)(2,1)S(1)}) custom-call(s32[2]{0:T(128)S(1)} %pad_add_fusion.me, bf16[16,96,128]{2,1,0:T(8,128)(2,1)S(1)} %all_to_all.68.got, f32[144,64]{1,0:T(8,128)S(1)} %get-tuple-element.43.w), custom_call_target="tpu_custom_call" | custom-call | tf_op jit(solution)/shard_map/pallas_call | solution.py:450
  90.0 16.7 %all_to_all.69.got = bf16[16,96,128]{2,1,0:T(8,128)(2,1)S(1)} all-to-all(bf16[16,96,128]{2,1,0:T(8,128)(2,1)S(1)} %get-tuple-element.44), channel_id=1, replica_groups=mesh['chips'=32,'samples'=16] {'samples'}, dimensions={0} | all-to-all | bytes 786432 | tf_op jit(solution)/shard_map/all_to_all | solution.py:462
  106.8 2.0 %shard_map.63 = bf16[32,40,128]{2,1,0:T(8,128)(2,1)S(1)} custom-call(s32[2]{0:T(128)S(1)} %pad_add_fusion.me, bf16[16,96,128]{2,1,0:T(8,128)(2,1)S(1)} %all_to_all.69.got, bf16[2304,1024]{1,0:T(8,128)(2,1)S(1)} %copy-done.1), custom_call_target="tpu_custom_call" | custom-call | flops 301989888 | bytes 4718592 | tf_op jit(solution)/shard_map/pallas_call | solution.py:450
  108.8 22.9 %all_to_all.70.got = bf16[32,40,128]{2,1,0:T(8,128)(2,1)S(1)} all-to-all(bf16[32,40,128]{2,1,0:T(8,128)(2,1)S(1)} %shard_map.63), channel_id=1, replica_groups=mesh['chips'=32,'samples'=16] {'chips'}, dimensions={0} | all-to-all | bytes 655360 | tf_op jit(solution)/shard_map/all_to_all | solution.py:462
  131.7 1.5 shard_map.64
  133.2 15.6 %all_to_all.71.got = bf16[32,32,128]{2,1,0:T(8,128)(2,1)S(1)} all-to-all(bf16[32,32,128]{2,1,0:T(8,128)(2,1)S(1)} %get-tuple-element.46), channel_id=1, replica_groups=mesh['chips'=32,'samples'=16] {'chips'}, dimensions={0} | all-to-all | bytes 524288 | tf_op jit(solution)/shard_map/all_to_all | solution.py:462
  148.8 2.3 %shard_map.65 = bf16[16,112,128]{2,1,0:T(8,128)(2,1)S(1)} custom-call(s32[2]{0:T(128)S(1)} %pad_add_fusion.me, bf16[32,32,128]{2,1,0:T(8,128)(2,1)S(1)} %all_to_all.71.got, bf16[2304,1024]{1,0:T(8,128)(2,1)S(1)} %copy-done.1), custom_call_target="tpu_custom_call" | custom-call | flops 301989888 | bytes 4718592 | tf_op jit(solution)/shard_map/pallas_call | solution.py:450
  151.1 15.7 %all_to_all.72.got = bf16[16,112,128]{2,1,0:T(8,128)(2,1)S(1)} all-to-all(bf16[16,112,128]{2,1,0:T(8,128)(2,1)S(1)} %shard_map.65), channel_id=1, replica_groups=mesh['chips'=32,'samples'=16] {'samples'}, dimensions={0} | all-to-all | bytes 917504 | tf_op jit(solution)/shard_map/all_to_all | solution.py:462
  166.7 1.5 shard_map.66
  168.3 14.4 %all_to_all.73.got = f32[16,1,128]{2,1,0:T(1,128)S(1)} all-to-all(f32[16,1,128]{2,1,0:T(1,128)S(1)} %get-tuple-element.51), channel_id=1, replica_groups=mesh['chips'=32,'samples'=16] {'samples'}, dimensions={0} | all-to-all | bytes 16384 | tf_op jit(solution)/shard_map/all_to_all | solution.py:462
  182.7 0.6 shard_map.67
  183.3 8.9 %all-to-all-start.12 = ((f32[32,1,128]{2,1,0:T(1,128)}), f32[32,1,128]{2,1,0:T(1,128)S(1)}, u32[]{:S(2)}, u32[]{:S(2)}) async-start(f32[32,1,128]{2,1,0:T(1,128)} %shard_map.67), calls=%async_computation.12 | async-start | bytes 32768 | tf_op jit(solution)/shard_map/all_to_all | solution.py:462
  192.2 0.7 copy.9
  192.9 7.2 %all-to-all-done.12.got = f32[32,1,128]{2,1,0:T(1,128)S(1)} async-done(((f32[32,1,128]{2,1,0:T(1,128)}), f32[32,1,128]{2,1,0:T(1,128)S(1)}, u32[]{:S(2)}, u32[]{:S(2)}) %all-to-all-start.12) | async-done | bytes 16416 | tf_op jit(solution)/shard_map/all_to_all | solution.py:462
  200.1 0.7 shard_map.68
  (1 shorter events, 0.0 us)
Async XLA Ops:
  0.6 26.3 %copy-start.1 = (bf16[2304,1024]{1,0:T(8,128)(2,1)S(1)}, bf16[2304,1024]{1,0:T(8,128)(2,1)}, u32[]{:S(2)}) copy-start(bf16[2304,1024]{1,0:T(8,128)(2,1)} %tile.7) | copy-start | bytes 14155780
  0.7 53.0 %copy-start = (f32[64,32]{0,1:T(8,128)S(1)}, f32[64,32]{0,1:T(8,128)}, u32[]{:S(2)}) copy-start(f32[64,32]{0,1:T(8,128)} %param.7) | copy-start | bytes 24580
  183.3 16.8 %all-to-all-start.12 = ((f32[32,1,128]{2,1,0:T(1,128)}), f32[32,1,128]{2,1,0:T(1,128)S(1)}, u32[]{:S(2)}, u32[]{:S(2)}) async-start(f32[32,1,128]{2,1,0:T(1,128)} %shard_map.67), calls=%async_computation.12 | async-start | bytes 32768 | tf_op jit(solution)/shard_map/all_to_all | solution.py:462
